TPU v7x, 32 devices: a whole 2x2x4 slice. The times are simulated.
32 devices in a mesh: fsdp: 4 (over y, core), ctx: 8 (over z, x).
Axes of the slice: x: 2, y: 2, z: 4, core: 2. Of those that a mesh axis runs over, the one named last changes fastest.
Arguments:
- tokens: bfloat16 [8, 1024, 2048], P('fsdp', 'ctx'), may hold values from -6 to 6
- lengths: int32 [8], P('fsdp'), may hold values from 1024 to 1024, as said below
- cotangent: bfloat16 [8, 1024, 2048], P('fsdp', 'ctx'), may hold values from -6 to 6
- norm_gain: bfloat16 [2048], P('fsdp'), may hold values from 0.5 to 1.5
- norm_shift: bfloat16 [2048], P('fsdp'), may hold values from -1.75 to 1.75
- query_weight: bfloat16 [2048, 2048], P('fsdp'), may hold values from -0.125 to 0.125
- query_bias: bfloat16 [2048], P('fsdp'), may hold values from -3 to 3
- keyval_weight: bfloat16 [2048, 256], P('fsdp'), may hold values from -0.125 to 0.125
- value_bias: bfloat16 [128], P('fsdp'), may hold values from -0.3125 to 0.3125
- mixer_weight: bfloat16 [2048, 2048], P('fsdp'), may hold values from -0.5 to 0.5
- mixer_bias: bfloat16 [2048], P('fsdp'), may hold values from -1.75 to 1.75
- ffnorm_gain: bfloat16 [2048], P('fsdp'), may hold values from 0.5 to 1.5
- ffnorm_shift: bfloat16 [2048], P('fsdp'), may hold values from -1.75 to 1.75
- up_weight: bfloat16 [2048, 8192], P('fsdp'), may hold values from -0.125 to 0.125
- up_bias: bfloat16 [8192], P('fsdp'), may hold values from -3 to 3
- down_weight: bfloat16 [8192, 2048], P('fsdp'), may hold values from -0.0625 to 0.0625
- down_bias: bfloat16 [2048], P('fsdp'), may hold values from -1.75 to 1.75
Outputs:
- layer_out: bfloat16 [8, 1024, 2048], P('fsdp', 'ctx')
- tokens_grad: bfloat16 [8, 1024, 2048], P('fsdp', 'ctx')
- gain_grad: float32 [2048], P(('fsdp', 'ctx'))
- shift_grad: float32 [2048], P(('fsdp', 'ctx'))
- query_grad: float32 [2048, 2048], P(('fsdp', 'ctx'))
- qbias_grad: float32 [2048], P(('fsdp', 'ctx'))
- keyval_grad: float32 [2048, 256], P(('fsdp', 'ctx'))
- vbias_grad: float32 [128], P(('fsdp', 'ctx'))
- mixer_grad: float32 [2048, 2048], P(('fsdp', 'ctx'))
- mbias_grad: float32 [2048], P(('fsdp', 'ctx'))
- ffgain_grad: float32 [2048], P(('fsdp', 'ctx'))
- ffshift_grad: float32 [2048], P(('fsdp', 'ctx'))
- up_grad: float32 [2048, 8192], P(('fsdp', 'ctx'))
- ubias_grad: float32 [8192], P(('fsdp', 'ctx'))
- down_grad: float32 [8192, 2048], P(('fsdp', 'ctx'))
- dbias_grad: float32 [2048], P(('fsdp', 'ctx'))
Inputs may be any that keep to these rules, and one draw needn't show every extreme that they name: Slot s holds one sequence in its first lengths[s] positions and padding after it; of the 2 slots of each index of fsdp, one is full.
All inputs are finite; a program needn't handle non-finite values.
Results may differ from a plain program's by a relative error of at most 0.015.
Values may be sent and summed in bfloat16 or wider, within the bound.
A program may use at most 384 MiB of HBM per device.

v0:
```python
import jax
import jax.numpy as jnp
from jax import lax
from jax.sharding import PartitionSpec as P

EPSILON = 1e-05
NEG_LARGE = -1e30


def normalize(values, gain, shift):
    center = values - jnp.mean(values, axis=-1, keepdims=True)
    spread = jnp.mean(center * center, axis=-1, keepdims=True)
    return center * lax.rsqrt(spread + EPSILON) * gain + shift


def contract_last(left_side, right_side):
    return lax.dot_general(
        left_side, right_side, (((1,), (1,)), ((), ())), preferred_element_type=jnp.float32
    )


def contract_first(left_side, right_side):
    return lax.dot_general(
        left_side, right_side, (((0,), (0,)), ((), ())), preferred_element_type=jnp.float32
    )


def key_mask(query_pos, key_start, block_len, length):
    key_pos = key_start + jnp.arange(block_len, dtype=jnp.int32)
    return (key_pos[None, :] <= query_pos[:, None]) & (key_pos[None, :] < length)


def block_scores(query_rows, query_pos, kv_block, key_start, length):
    head_dim = query_rows.shape[1]
    allowed = key_mask(query_pos, key_start, kv_block.shape[0], length)
    raw_scores = contract_last(query_rows, kv_block[:, :head_dim]) * head_dim ** (-0.5)
    return (allowed, jnp.where(allowed, raw_scores, NEG_LARGE))


def block_probs(query_rows, query_pos, kv_block, key_start, length, logsum):
    allowed, scores = block_scores(query_rows, query_pos, kv_block, key_start, length)
    return jnp.where(allowed, jnp.exp(scores - logsum[:, None]), 0.0)


def split_blocks(kv_slot, block_len):
    block_count = kv_slot.shape[0] // block_len
    kv_blocks = kv_slot.reshape(block_count, block_len, kv_slot.shape[1])
    key_starts = jnp.arange(block_count, dtype=jnp.int32) * block_len
    return (kv_blocks, key_starts)


def attend_forward(query_rows, query_pos, kv_slot, length, block_len):
    head_dim = query_rows.shape[1]
    row_count = query_rows.shape[0]
    kv_blocks, key_starts = split_blocks(kv_slot, block_len)
    last_pos = jnp.max(query_pos)

    def stats_step(carry_in, scan_item):
        kv_block, key_start = scan_item

        def stats_compute(state):
            row_top, row_total = state
            allowed, scores = block_scores(query_rows, query_pos, kv_block, key_start, length)
            new_top = jnp.maximum(row_top, jnp.max(scores, axis=1))
            exp_terms = jnp.where(allowed, jnp.exp(scores - new_top[:, None]), 0.0)
            return (new_top, row_total * jnp.exp(row_top - new_top) + jnp.sum(exp_terms, axis=1))

        is_live = (key_start <= last_pos) & (key_start < length)
        return (lax.cond(is_live, stats_compute, lambda state: state, carry_in), None)

    start_state = (
        jnp.full((row_count,), NEG_LARGE, jnp.float32),
        jnp.zeros((row_count,), jnp.float32),
    )
    (row_top, row_total), unused_out = lax.scan(stats_step, start_state, (kv_blocks, key_starts))
    logsum = row_top + jnp.log(row_total)

    def mix_step(accum_out, scan_item):
        kv_block, key_start = scan_item

        def mix_compute(accum_in):
            attn_probs = block_probs(query_rows, query_pos, kv_block, key_start, length, logsum)
            return accum_in + jnp.dot(
                attn_probs.astype(jnp.bfloat16),
                kv_block[:, head_dim:],
                preferred_element_type=jnp.float32,
            )

        is_live = (key_start <= last_pos) & (key_start < length)
        return (lax.cond(is_live, mix_compute, lambda accum_in: accum_in, accum_out), None)

    mixed_out, unused_out = lax.scan(
        mix_step, jnp.zeros((row_count, head_dim), jnp.float32), (kv_blocks, key_starts)
    )
    return (mixed_out, logsum)


def attend_backward(query_rows, query_pos, kv_slot, length, logsum, mixed_out, d_mixed, block_len):
    head_dim = query_rows.shape[1]
    row_count = query_rows.shape[0]
    kv_blocks, key_starts = split_blocks(kv_slot, block_len)
    last_pos = jnp.max(query_pos)
    row_delta = jnp.sum(d_mixed.astype(jnp.float32) * mixed_out, axis=1)

    def back_step(accum_out, scan_item):
        kv_block, key_start = scan_item

        def back_compute(accum_in):
            attn_probs = block_probs(query_rows, query_pos, kv_block, key_start, length, logsum)
            d_probs = contract_last(d_mixed, kv_block[:, head_dim:])
            d_scores = (attn_probs * (d_probs - row_delta[:, None])).astype(jnp.bfloat16)
            new_accum = accum_in + jnp.dot(
                d_scores, kv_block[:, :head_dim], preferred_element_type=jnp.float32
            )
            d_keys = contract_first(d_scores, query_rows) * head_dim ** (-0.5)
            d_values = contract_first(attn_probs.astype(jnp.bfloat16), d_mixed)
            return (new_accum, jnp.concatenate([d_keys, d_values], axis=1))

        def skipped(accum_in):
            return (accum_in, jnp.zeros((block_len, 2 * head_dim), jnp.float32))

        is_live = (key_start <= last_pos) & (key_start < length)
        return lax.cond(is_live, back_compute, skipped, accum_out)

    d_rows, d_blocks = lax.scan(
        back_step, jnp.zeros((row_count, head_dim), jnp.float32), (kv_blocks, key_starts)
    )
    return (d_rows * head_dim ** (-0.5), d_blocks.reshape(kv_slot.shape[0], 2 * head_dim))


def forward(tokens, lengths, weights):
    (
        norm_gain,
        norm_shift,
        query_weight,
        query_bias,
        keyval_weight,
        value_bias,
        mixer_weight,
        mixer_bias,
        ffnorm_gain,
        ffnorm_shift,
        up_weight,
        up_bias,
        down_weight,
        down_bias,
    ) = weights
    slot_count, seg_len, model_width = tokens.shape
    head_dim = value_bias.shape[0]
    head_count = model_width // head_dim
    ctx_size = lax.axis_size("ctx")
    ctx_place = lax.axis_index("ctx")
    block_len = min(512, seg_len * ctx_size)
    row_count = slot_count * seg_len
    inputs = tokens.reshape(row_count, model_width).astype(jnp.float32)
    first = normalize(inputs, norm_gain.astype(jnp.float32), norm_shift.astype(jnp.float32)).astype(
        jnp.bfloat16
    )
    queries = (
        jnp.dot(first, query_weight, preferred_element_type=jnp.float32)
        + query_bias.astype(jnp.float32)
    ).astype(jnp.bfloat16)
    pair_bias = jnp.concatenate(
        [jnp.zeros((head_dim,), jnp.float32), value_bias.astype(jnp.float32)]
    )
    keyvals = (
        jnp.dot(first, keyval_weight, preferred_element_type=jnp.float32) + pair_bias
    ).astype(jnp.bfloat16)
    gathered = lax.all_gather(
        keyvals.reshape(slot_count, seg_len, 2 * head_dim), "ctx", axis=1, tiled=True
    )
    query_pos = ctx_place * seg_len + jnp.repeat(jnp.arange(seg_len, dtype=jnp.int32), head_count)
    query_slots = queries.reshape(slot_count, seg_len * head_count, head_dim)
    mixed_list = []
    logsum_list = []
    for slot_idx in range(slot_count):
        mixed_out, logsum = attend_forward(
            query_slots[slot_idx], query_pos, gathered[slot_idx], lengths[slot_idx], block_len
        )
        mixed_list.append(mixed_out)
        logsum_list.append(logsum)
    mixed_full = jnp.stack(mixed_list)
    logsums = jnp.stack(logsum_list)
    attn_rows = mixed_full.reshape(row_count, model_width).astype(jnp.bfloat16)
    residual = (
        inputs
        + jnp.dot(attn_rows, mixer_weight, preferred_element_type=jnp.float32)
        + mixer_bias.astype(jnp.float32)
    )
    second = normalize(
        residual, ffnorm_gain.astype(jnp.float32), ffnorm_shift.astype(jnp.float32)
    ).astype(jnp.bfloat16)
    upper = jnp.dot(second, up_weight, preferred_element_type=jnp.float32) + up_bias.astype(
        jnp.float32
    )
    active = jax.nn.gelu(upper, approximate=True).astype(jnp.bfloat16)
    output = (
        residual
        + jnp.dot(active, down_weight, preferred_element_type=jnp.float32)
        + down_bias.astype(jnp.float32)
    )
    stored = (
        inputs,
        first,
        query_slots,
        gathered,
        mixed_full,
        logsums,
        attn_rows,
        residual,
        second,
        upper,
        active,
        query_pos,
    )
    return (output, stored)


def outer_term(left_side, right_side):
    return contract_first(left_side, right_side)


def body(
    tokens,
    lengths,
    cotangent,
    norm_gain,
    norm_shift,
    query_weight,
    query_bias,
    keyval_weight,
    value_bias,
    mixer_weight,
    mixer_bias,
    ffnorm_gain,
    ffnorm_shift,
    up_weight,
    up_bias,
    down_weight,
    down_bias,
):
    shards = (
        norm_gain,
        norm_shift,
        query_weight,
        query_bias,
        keyval_weight,
        value_bias,
        mixer_weight,
        mixer_bias,
        ffnorm_gain,
        ffnorm_shift,
        up_weight,
        up_bias,
        down_weight,
        down_bias,
    )
    weights = (
        lax.all_gather(shards[0], "fsdp", axis=0, tiled=True),
        lax.all_gather(shards[1], "fsdp", axis=0, tiled=True),
        lax.all_gather(shards[2], "fsdp", axis=0, tiled=True),
        lax.all_gather(shards[3], "fsdp", axis=0, tiled=True),
        lax.all_gather(shards[4], "fsdp", axis=0, tiled=True),
        lax.all_gather(shards[5], "fsdp", axis=0, tiled=True),
        lax.all_gather(shards[6], "fsdp", axis=0, tiled=True),
        lax.all_gather(shards[7], "fsdp", axis=0, tiled=True),
        lax.all_gather(shards[8], "fsdp", axis=0, tiled=True),
        lax.all_gather(shards[9], "fsdp", axis=0, tiled=True),
        lax.all_gather(shards[10], "fsdp", axis=0, tiled=True),
        lax.all_gather(shards[11], "fsdp", axis=0, tiled=True),
        lax.all_gather(shards[12], "fsdp", axis=0, tiled=True),
        lax.all_gather(shards[13], "fsdp", axis=0, tiled=True),
    )
    output, stored = forward(tokens, lengths, weights)
    weights = (
        lax.all_gather(shards[0], "fsdp", axis=0, tiled=True),
        lax.all_gather(shards[1], "fsdp", axis=0, tiled=True),
        lax.all_gather(shards[2], "fsdp", axis=0, tiled=True),
        lax.all_gather(shards[3], "fsdp", axis=0, tiled=True),
        lax.all_gather(shards[4], "fsdp", axis=0, tiled=True),
        lax.all_gather(shards[5], "fsdp", axis=0, tiled=True),
        lax.all_gather(shards[6], "fsdp", axis=0, tiled=True),
        lax.all_gather(shards[7], "fsdp", axis=0, tiled=True),
        lax.all_gather(shards[8], "fsdp", axis=0, tiled=True),
        lax.all_gather(shards[9], "fsdp", axis=0, tiled=True),
        lax.all_gather(shards[10], "fsdp", axis=0, tiled=True),
        lax.all_gather(shards[11], "fsdp", axis=0, tiled=True),
        lax.all_gather(shards[12], "fsdp", axis=0, tiled=True),
        lax.all_gather(shards[13], "fsdp", axis=0, tiled=True),
    )
    stored = forward(tokens, lengths, weights)[1]
    (
        inputs,
        first,
        query_slots,
        gathered,
        mixed_full,
        logsums,
        attn_rows,
        residual,
        second,
        upper,
        active,
        query_pos,
    ) = stored
    (
        full_gain,
        full_shift,
        full_query,
        full_qbias,
        full_keyval,
        full_vbias,
        full_mixer,
        full_mbias,
        full_ffgain,
        full_ffshift,
        full_up,
        full_ubias,
        full_down,
        full_dbias,
    ) = weights
    slot_count, seg_len, model_width = tokens.shape
    head_dim = full_vbias.shape[0]
    head_count = model_width // head_dim
    ctx_size = lax.axis_size("ctx")
    ctx_place = lax.axis_index("ctx")
    block_len = min(512, seg_len * ctx_size)
    row_count = slot_count * seg_len
    token_pos = ctx_place * seg_len + jnp.arange(seg_len, dtype=jnp.int32)
    valid_rows = (token_pos[None, :] < lengths[:, None]).astype(jnp.float32).reshape(row_count, 1)
    d_out = cotangent.reshape(row_count, model_width).astype(jnp.float32) * valid_rows
    d_down = d_out.astype(jnp.bfloat16)
    d_active = contract_last(d_down, full_down)
    unused_val, gelu_back = jax.vjp(lambda values: jax.nn.gelu(values, approximate=True), upper)
    d_upper = gelu_back(d_active)[0].astype(jnp.bfloat16)
    d_second = contract_last(d_upper, full_up)
    unused_val, norm_back = jax.vjp(
        normalize, residual, full_ffgain.astype(jnp.float32), full_ffshift.astype(jnp.float32)
    )
    d_resid_part, d_ffgain, d_ffshift = norm_back(d_second)
    d_residual = d_resid_part + d_out
    d_mix = d_residual.astype(jnp.bfloat16)
    d_mixed = contract_last(d_mix, full_mixer).astype(jnp.bfloat16)
    d_mixed_slots = d_mixed.reshape(slot_count, seg_len * head_count, head_dim)
    d_query_list = []
    kv_term_list = []
    for slot_idx in range(slot_count):
        d_rows, kv_term = attend_backward(
            query_slots[slot_idx],
            query_pos,
            gathered[slot_idx],
            lengths[slot_idx],
            logsums[slot_idx],
            mixed_full[slot_idx],
            d_mixed_slots[slot_idx],
            block_len,
        )
        d_query_list.append(d_rows)
        kv_term_list.append(kv_term)
    d_queries = jnp.stack(d_query_list).reshape(row_count, model_width).astype(jnp.bfloat16)
    kv_terms = jnp.stack(kv_term_list)
    d_keyvals = lax.psum_scatter(
        kv_terms.astype(jnp.bfloat16), "ctx", scatter_dimension=1, tiled=True
    ).astype(jnp.float32)
    d_keyvals = d_keyvals.reshape(row_count, 2 * head_dim).astype(jnp.bfloat16)
    d_first = contract_last(d_queries, full_query) + contract_last(d_keyvals, full_keyval)
    unused_val, first_back = jax.vjp(
        normalize, inputs, full_gain.astype(jnp.float32), full_shift.astype(jnp.float32)
    )
    d_input_part, d_gain, d_shift = first_back(d_first)
    tokens_grad = (d_input_part + d_residual).astype(jnp.bfloat16).reshape(tokens.shape)
    layer_out = output.astype(jnp.bfloat16).reshape(tokens.shape)
    query_grad = lax.psum_scatter(
        outer_term(first, d_queries), ("fsdp", "ctx"), scatter_dimension=0, tiled=True
    )
    keyval_grad = lax.psum_scatter(
        outer_term(first, d_keyvals), ("fsdp", "ctx"), scatter_dimension=0, tiled=True
    )
    mixer_grad = lax.psum_scatter(
        outer_term(attn_rows, d_mix), ("fsdp", "ctx"), scatter_dimension=0, tiled=True
    )
    up_grad = lax.psum_scatter(
        outer_term(second, d_upper), ("fsdp", "ctx"), scatter_dimension=0, tiled=True
    )
    down_grad = lax.psum_scatter(
        outer_term(active, d_down), ("fsdp", "ctx"), scatter_dimension=0, tiled=True
    )
    vector_sums = (
        d_gain,
        d_shift,
        jnp.sum(d_queries.astype(jnp.float32), axis=0),
        jnp.sum(d_keyvals[:, head_dim:].astype(jnp.float32), axis=0),
        jnp.sum(d_mix.astype(jnp.float32), axis=0),
        d_ffgain,
        d_ffshift,
        jnp.sum(d_upper.astype(jnp.float32), axis=0),
        jnp.sum(d_out, axis=0),
    )
    (
        gain_grad,
        shift_grad,
        qbias_grad,
        vbias_grad,
        mbias_grad,
        ffgain_grad,
        ffshift_grad,
        ubias_grad,
        dbias_grad,
    ) = (
        lax.psum_scatter(vector_sums[0], ("fsdp", "ctx"), scatter_dimension=0, tiled=True),
        lax.psum_scatter(vector_sums[1], ("fsdp", "ctx"), scatter_dimension=0, tiled=True),
        lax.psum_scatter(vector_sums[2], ("fsdp", "ctx"), scatter_dimension=0, tiled=True),
        lax.psum_scatter(vector_sums[3], ("fsdp", "ctx"), scatter_dimension=0, tiled=True),
        lax.psum_scatter(vector_sums[4], ("fsdp", "ctx"), scatter_dimension=0, tiled=True),
        lax.psum_scatter(vector_sums[5], ("fsdp", "ctx"), scatter_dimension=0, tiled=True),
        lax.psum_scatter(vector_sums[6], ("fsdp", "ctx"), scatter_dimension=0, tiled=True),
        lax.psum_scatter(vector_sums[7], ("fsdp", "ctx"), scatter_dimension=0, tiled=True),
        lax.psum_scatter(vector_sums[8], ("fsdp", "ctx"), scatter_dimension=0, tiled=True),
    )
    return (
        layer_out,
        tokens_grad,
        gain_grad,
        shift_grad,
        query_grad,
        qbias_grad,
        keyval_grad,
        vbias_grad,
        mixer_grad,
        mbias_grad,
        ffgain_grad,
        ffshift_grad,
        up_grad,
        ubias_grad,
        down_grad,
        dbias_grad,
    )


def solution(mesh):
    return jax.shard_map(
        body,
        mesh=mesh,
        in_specs=(
            P("fsdp", "ctx", None),
            P("fsdp"),
            P("fsdp", "ctx", None),
            P("fsdp"),
            P("fsdp"),
            P("fsdp", None),
            P("fsdp"),
            P("fsdp", None),
            P("fsdp"),
            P("fsdp", None),
            P("fsdp"),
            P("fsdp"),
            P("fsdp"),
            P("fsdp", None),
            P("fsdp"),
            P("fsdp", None),
            P("fsdp"),
        ),
        out_specs=(
            P("fsdp", "ctx", None),
            P("fsdp", "ctx", None),
            P(("fsdp", "ctx")),
            P(("fsdp", "ctx")),
            P(("fsdp", "ctx"), None),
            P(("fsdp", "ctx")),
            P(("fsdp", "ctx"), None),
            P(("fsdp", "ctx")),
            P(("fsdp", "ctx"), None),
            P(("fsdp", "ctx")),
            P(("fsdp", "ctx")),
            P(("fsdp", "ctx")),
            P(("fsdp", "ctx"), None),
            P(("fsdp", "ctx")),
            P(("fsdp", "ctx"), None),
            P(("fsdp", "ctx")),
        ),
        check_vma=False,
    )
```

profile of v0, /device:TPU:0, one launch (start us, length us, event | category | flops | bytes accessed | tf_op | source)
XLA Modules:
  0.0 4593.7 jit_solution(6073791191139701139)
XLA Ops:
  8.7 6.1 all-gather.1
  15.5 5.4 all-gather
  23.7 7.3 all-reduce.1
  32.4 1.6 multiply_reduce_fusion.6
  34.7 1.7 add_convert_fusion.3
  36.4 2.3 fusion.65
  41.4 5.2 all-gather.3
  46.6 5.2 all-gather.2
  51.8 5.2 all_gather.71
  57.0 5.2 all-gather.5
  62.2 5.2 all-gather.4
  70.8 1.4 add_convert_fusion
  72.2 7.2 all-gather.16.cloned.1.call-done
  80.7 57.4 %all-gather.18.cloned.1.call-done = bf16[2048,2048]{1,0:T(8,128)(2,1)} async-done(((bf16[512,2048]{1,0:T(8,128)(2,1)}), bf16[2048,2048]{1,0:T(8,128)(2,1)}) %all-gather.18.cloned.1.call-update) | async-done | bytes 8388624 | tf_op jit(solution)/shard_map/all_gather | solution.py:261
  138.0 5.7 fusion.61
  145.1 12.7 while.110
  148.9 5.7 conditional.20
  151.0 2.2 fusion.78
  158.9 13.3 while.111
  162.1 6.8 conditional.21
  164.2 4.7 convolution_add_fusion.1
  172.2 11.1 while.108
  175.4 4.6 conditional.18
  184.4 13.1 while.109
  187.6 6.7 conditional.19
  189.7 4.6 convolution_add_fusion
  197.5 1.9 convert_bitcast_fusion
  200.4 2.5 convert_element_type.214
  202.9 7.4 fusion.83
  212.1 188.7 %all-gather.24.cloned.1.call-done = bf16[8192,2048]{1,0:T(8,128)(2,1)} async-done(((bf16[2048,2048]{1,0:T(8,128)(2,1)}), bf16[8192,2048]{1,0:T(8,128)(2,1)}) %all-gather.24.cloned.1.call-update) | async-done | bytes 33554448 | tf_op jit(solution)/shard_map/all_gather | solution.py:271
  400.7 21.2 fusion.84
  421.9 181.8 %all-gather.22.cloned.1.call-done = bf16[2048,8192]{1,0:T(8,128)(2,1)} async-done(((bf16[512,8192]{1,0:T(8,128)(2,1)}), bf16[2048,8192]{1,0:T(8,128)(2,1)}) %all-gather.22.cloned.1.call-update) | async-done | bytes 33554448 | tf_op jit(solution)/shard_map/all_gather | solution.py:269
  603.7 25.1 convert_reduce_fusion
  628.8 18.4 multiply_reduce_fusion.1
  647.3 2.3 fusion.76
  652.0 6.2 convolution_convert_fusion
  660.6 17.7 while.113
  663.8 9.2 conditional.23
  665.9 2.7 fusion.46
  671.0 1.9 convolution_multiply_fusion.1
  679.6 1.6 multiply_reduce_fusion.8
  682.1 19.6 while.112
  685.3 8.1 conditional.22
  687.4 2.6 fusion.37
  701.7 2.3 pad_maximum_fusion.1
  705.6 7.2 fusion.85
  712.8 72.0 %reduce-scatter.7.cloned.1.call-done = bf16[2,128,256]{2,1,0:T(8,128)(2,1)} async-done(((bf16[2,1024,256]{2,1,0:T(8,128)(2,1)}), bf16[2,128,256]{2,1,0:T(8,128)(2,1)}) %reduce-scatter.7.cloned.1.call-update) | async-done | bytes 131088 | tf_op jit(solution)/shard_map/reduce_scatter | solution.py:362
  786.2 3.4 fusion.73
  791.1 1.5 multiply_reduce_fusion.2
  792.6 1.9 convolution_bitcast_fusion
  794.7 8.1 fusion.86
  804.4 8.1 fusion.87
  812.6 1.5 copy-done.5
  814.1 25.5 fusion.71
  839.7 27.6 fusion.72
  868.0 5.4 all-gather.6
  873.4 19.6 fusion.62
  893.0 4.5 add_convert_fusion.1
  897.6 19.6 all-reduce.14.cloned.1.call-done
  928.5 130.2 %reduce-scatter.11.cloned.1.call-done = f32[64,256]{1,0:T(8,128)} async-done(((f32[2048,256]{1,0:T(8,128)}), f32[64,256]{1,0:T(8,128)}) %reduce-scatter.11.cloned.1.call-update) | async-done | bytes 65552 | tf_op jit(solution)/shard_map/reduce_scatter | solution.py:376
  1058.7 357.6 %reduce-scatter.9.cloned.1.call-done = f32[64,2048]{1,0:T(8,128)} async-done(((f32[2048,2048]{1,0:T(8,128)}), f32[64,2048]{1,0:T(8,128)}) %reduce-scatter.9.cloned.1.call-update) | async-done | bytes 524304 | tf_op jit(solution)/shard_map/reduce_scatter | solution.py:373
  1416.3 360.4 %reduce-scatter.13.cloned.1.call-done = f32[64,2048]{1,0:T(8,128)} async-done(((f32[2048,2048]{1,0:T(8,128)}), f32[64,2048]{1,0:T(8,128)}) %reduce-scatter.13.cloned.1.call-update) | async-done | bytes 524304 | tf_op jit(solution)/shard_map/reduce_scatter | solution.py:379
  1776.7 1404.7 %reduce-scatter.15.cloned.1.call-done = f32[64,8192]{1,0:T(8,128)} async-done(((f32[2048,8192]{1,0:T(8,128)}), f32[64,8192]{1,0:T(8,128)}) %reduce-scatter.15.cloned.1.call-update) | async-done | bytes 2097168 | tf_op jit(solution)/shard_map/reduce_scatter | solution.py:382
  3181.4 1405.6 %reduce-scatter.17.cloned.1.call-done = f32[256,2048]{1,0:T(8,128)} async-done(((f32[8192,2048]{1,0:T(8,128)}), f32[256,2048]{1,0:T(8,128)}) %reduce-scatter.17.cloned.1.call-update) | async-done | bytes 2097168 | tf_op jit(solution)/shard_map/reduce_scatter | solution.py:385
  (265 shorter events, 81.1 us)
Async XLA Ops:
  7.2 29.2 all-gather.14.cloned.1.call-start
  7.9 71.5 %all-gather.16.cloned.1.call-start = ((), (), s32[]{:S(2)}) async-start(), calls=%async_computation.7 | async-start | bytes 1179648 | tf_op jit(solution)/shard_map/all_gather | solution.py:169
  20.9 49.9 %copy-start.18 = (f32[4,1,512]{2,1,0:T(1,128)}, f32[4,1,512]{2,1,0:T(1,128)S(1)}, u32[]{:S(2)}) copy-start(f32[4,1,512]{2,1,0:T(1,128)S(1)} %convert_element_type.248) | copy-start | bytes 24580
  32.4 1.7 copy-start.20
  34.1 35.5 copy-start.24
  34.1 0.6 copy-start.22
  38.7 99.3 %all-gather.18.cloned.1.call-start = ((), (), s32[]{:S(2)}) async-start(), calls=%async_computation.8 | async-start | bytes 10485760 | tf_op jit(solution)/shard_map/all_gather | solution.py:261
  39.5 163.4 %all-gather.20.cloned.1.call-start = ((), (), s32[]{:S(2)}) async-start(), calls=%async_computation.9 | async-start | bytes 10485760 | tf_op jit(solution)/shard_map/all_gather | solution.py:265
  40.1 360.7 %all-gather.24.cloned.1.call-start = ((), (), s32[]{:S(2)}) async-start(), calls=%async_computation.11 | async-start | bytes 41943040 | tf_op jit(solution)/shard_map/all_gather | solution.py:271
  40.6 0.7 copy-start.32
  40.7 5.9 copy-start.33
  40.7 11.1 copy-start.31
  40.7 16.3 copy-start.34
  40.7 21.5 copy-start.35
  40.7 27.3 copy-start.30
  40.7 27.9 copy-start.10
  40.7 30.0 copy-start
  40.7 563.0 %all-gather.22.cloned.1.call-start = ((), (), s32[]{:S(2)}) async-start(), calls=%async_computation.10 | async-start | bytes 41943040 | tf_op jit(solution)/shard_map/all_gather | solution.py:269
  41.3 743.5 %reduce-scatter.7.cloned.1.call-start = ((), (), s32[]{:S(2)}) async-start(), calls=%async_computation.12 | async-start | bytes 1179648 | tf_op jit(solution)/shard_map/reduce_scatter | solution.py:362
  68.6 580.9 %copy-start.26 = (f32[256]{0:T(256)}, f32[256]{0:T(256)S(1)}, u32[]{:S(2)}) copy-start(f32[256]{0:T(256)S(1)} %get-tuple-element.1079) | copy-start | bytes 3076
  197.5 12.9 copy-start.8
  210.4 1.3 copy-start.3
  212.1 391.7 %copy-start.4 = (f32[256,2048]{1,0:T(8,128)S(1)}, f32[256,2048]{1,0:T(8,128)}, u32[]{:S(2)}) copy-start(f32[256,2048]{1,0:T(8,128)} %copy-done.3) | copy-start | bytes 6291460
  647.2 3.7 copy-start.11
  649.6 1.4 copy-start.6
  649.6 8.6 copy-start.28
  652.0 6.2 copy-start.15
  652.0 7.3 copy-start.13
  690.8 1.8 copy-start.9
  693.4 0.7 copy-start.2
  699.2 0.7 copy-start.2
  704.0 213.2 %all-reduce.14.cloned.1.call-start = ((), (), s32[]{:S(2)}) async-start(), calls=%async_computation.18 | async-start | bytes 181248
  705.6 80.6 %copy-start.1 = (bf16[2,128,2048]{2,1,0:T(8,128)(2,1)S(1)}, bf16[2,128,2048]{2,1,0:T(8,128)(2,1)}, u32[]{:S(2)}) copy-start(bf16[2,128,2048]{2,1,0:T(8,128)(2,1)} %param.41) | copy-start | bytes 3145732
  705.6 80.6 %copy-start.19 = (f32[4,1,512]{2,1,0:T(1,128)S(1)}, f32[4,1,512]{2,1,0:T(1,128)}, u32[]{:S(2)}) copy-start(f32[4,1,512]{2,1,0:T(1,128)} %copy-done.18) | copy-start | bytes 24580
  705.6 80.6 %copy-start.21 = (f32[256]{0:T(256)S(1)}, f32[256]{0:T(256)}, u32[]{:S(2)}) copy-start(f32[256]{0:T(256)} %copy-done.20) | copy-start | bytes 3076
  712.8 76.9 %copy-start.25 = (f32[2,128]{1,0:T(2,128)S(1)}, f32[2,128]{1,0:T(2,128)}, u32[]{:S(2)}) copy-start(f32[2,128]{1,0:T(2,128)} %copy-done.24) | copy-start | bytes 3076
  712.8 78.3 %copy-start.23 = (f32[256]{0:T(256)S(1)}, f32[256]{0:T(256)}, u32[]{:S(2)}) copy-start(f32[256]{0:T(256)} %copy-done.22) | copy-start | bytes 3076
  786.2 6.4 copy-start.12
  786.2 6.4 copy-start.17
  789.7 1.4 copy-start.7
  792.6 266.1 %reduce-scatter.11.cloned.1.call-start = ((), (), s32[]{:S(2)}) async-start(), calls=%async_computation.14 | async-start | bytes 2162688 | tf_op jit(solution)/shard_map/reduce_scatter | solution.py:376
  794.5 621.8 %reduce-scatter.9.cloned.1.call-start = ((), (), s32[]{:S(2)}) async-start(), calls=%async_computation.13 | async-start | bytes 17301504 | tf_op jit(solution)/shard_map/reduce_scatter | solution.py:373
  802.8 1.2 copy-start.14
  802.8 1.5 copy-start.16
  802.9 973.8 %reduce-scatter.13.cloned.1.call-start = ((), (), s32[]{:S(2)}) async-start(), calls=%async_computation.15 | async-start | bytes 17301504 | tf_op jit(solution)/shard_map/reduce_scatter | solution.py:379
  812.5 1.6 copy-start.5
  812.5 2368.9 %reduce-scatter.15.cloned.1.call-start = ((), (), s32[]{:S(2)}) async-start(), calls=%async_computation.16 | async-start | bytes 69206016 | tf_op jit(solution)/shard_map/reduce_scatter | solution.py:382
  839.7 3747.3 %reduce-scatter.17.cloned.1.call-start = ((), (), s32[]{:S(2)}) async-start(), calls=%async_computation.17 | async-start | bytes 69206016 | tf_op jit(solution)/shard_map/reduce_scatter | solution.py:385
  867.3 0.7 copy-start.36
  873.4 19.6 copy-start.27
  873.4 19.6 copy-start.29
Sparse Core Ops, SparseCore 0:
  9.6 19.4 all-gather.13
  38.9 40.4 all-gather.15
  81.0 57.0 all-gather.17
  139.4 58.3 all-gather.19
  199.2 201.4 all-gather.23
  402.2 201.5 all-gather.21
  704.1 80.6 reduce-scatter.6
  793.0 124.1 all-reduce.13
  920.0 138.6 reduce-scatter.10
  1061.5 354.7 reduce-scatter.8
  1419.3 357.3 reduce-scatter.12
  1779.6 1401.7 reduce-scatter.14
  3184.4 1402.4 reduce-scatter.16
where the time goes:
time: 4600 us; the launch traced here: 4590 us
  waiting for transfers between devices  4190 us (91%)
  matrix products  213 us (5%)
  local copies, waits for them, and re-layouts  50.1 us (1%)
  blocking collectives  50 us (1%)
    reduce_scatter x1, waiting for transfers between devices, body(): lax.psum_scatter(outer_term(active, d_down), ('fsdp', 'ctx'), scatter_dim...  1410 us
    reduce_scatter x1, waiting for transfers between devices, body(): lax.psum_scatter(outer_term(second, d_upper), ('fsdp', 'ctx'), scatter_di...  1400 us
    reduce_scatter x1, waiting for transfers between devices, body(): lax.psum_scatter(outer_term(attn_rows, d_mix), ('fsdp', 'ctx'), scatter_d...  360 us
    reduce_scatter x1, waiting for transfers between devices, body(): lax.psum_scatter(outer_term(first, d_queries), ('fsdp', 'ctx'), scatter_d...  358 us
    all_gather x1, waiting for transfers between devices, body(): lax.all_gather(shards[12], 'fsdp', axis=0, tiled=True)  189 us
    all_gather x1, waiting for transfers between devices, body(): lax.all_gather(shards[10], 'fsdp', axis=0, tiled=True)  182 us
    reduce_scatter x1, waiting for transfers between devices, body(): lax.psum_scatter(outer_term(first, d_keyvals), ('fsdp', 'ctx'), scatter_d...  130 us
  transfers between devices with their start and end apart: 13, of which 11 were waited for; matrix products, arithmetic and copies ran while one was open for 4% of the time, Pallas kernels for 0%

commit v1 on v0

v1 whole, which is shorter than its diff:
```python
import functools

import jax
import jax.numpy as jnp
from jax import lax
from jax.experimental import pallas as pl
from jax.experimental.pallas import tpu as pltpu
from jax.sharding import Mesh, PartitionSpec as P

EPSILON = 1e-05
NEG_LARGE = -1e30
MIN_LEN = 1024
BF = jnp.bfloat16
F32 = jnp.float32
GELU_K = 0.7978845608028654
GELU_C = 0.044715


def dot(left_side, right_side, dims=((1,), (0,))):
    return lax.dot_general(left_side, right_side, (dims, ((), ())), preferred_element_type=F32)


def swap(values, axis):
    return lax.ppermute(values, axis, [(0, 1), (1, 0)])


def pick(values, index, axis):
    return lax.dynamic_index_in_dim(values, index, axis, keepdims=False)


def stack_heads(block, head_dim):
    heads = block.shape[0] // head_dim
    return jnp.concatenate([block[h * head_dim : (h + 1) * head_dim] for h in range(heads)], axis=1)


def unstack_heads(stacked, seg):
    heads = stacked.shape[1] // seg
    return jnp.concatenate([stacked[:, h * seg : (h + 1) * seg] for h in range(heads)], axis=0)


def masked_scores(scal_ref, queries, keys, step, seg, heads, with_length, first_block):
    scores = dot(keys, queries) * (keys.shape[1] ** (-0.5))
    pair = keys.shape[0]
    if not (with_length or first_block):
        return scores
    key_pos = lax.broadcasted_iota(jnp.int32, (pair, seg), 0)
    allowed = None
    if first_block:
        query_pos = lax.broadcasted_iota(jnp.int32, (pair, seg), 1) + scal_ref[1] * seg
        allowed = key_pos <= query_pos
    if with_length:
        length = scal_ref[2 + pl.program_id(0)]
        inside = key_pos + (scal_ref[0] - step) * pair < length
        allowed = inside if allowed is None else allowed & inside
    bias = jnp.where(allowed, 0.0, NEG_LARGE).astype(F32)
    return scores + jnp.concatenate([bias] * heads, axis=1)


def attn_fwd_kernel(scal_ref, q_ref, kv_ref, out_ref, lse_ref, *, with_length):
    head_dim = kv_ref.shape[-1] // 2
    seg = q_ref.shape[1]
    heads = q_ref.shape[0] // head_dim
    queries = stack_heads(q_ref[...], head_dim)

    def block(step, state, first_block):
        top, total, accum = state
        keys = kv_ref[0, step, :, :head_dim]
        values = kv_ref[0, step, :, head_dim:]
        scores = masked_scores(scal_ref, queries, keys, step, seg, heads, with_length, first_block)
        new_top = jnp.maximum(top, jnp.max(scores, axis=0, keepdims=True))
        terms = jnp.exp(scores - new_top)
        fade = jnp.exp(top - new_top)
        total = total * fade + jnp.sum(terms, axis=0, keepdims=True)
        accum = accum * fade + dot(values, terms.astype(BF), ((0,), (0,)))
        return new_top, total, accum

    lanes = heads * seg
    state = (
        jnp.full((1, lanes), NEG_LARGE, F32),
        jnp.zeros((1, lanes), F32),
        jnp.zeros((head_dim, lanes), F32),
    )
    state = block(0, state, True)
    top, total, accum = lax.fori_loop(1, scal_ref[0] + 1, lambda t, s: block(t, s, False), state)
    out_ref[...] = unstack_heads(accum / total, seg).astype(BF)
    lse_ref[0, 0] = top + jnp.log(total)


def attn_bwd_kernel(scal_ref, q_ref, kv_ref, out_ref, dout_ref, lse_ref, dq_ref, dkv_ref, *, with_length):
    head_dim = kv_ref.shape[-1] // 2
    seg = q_ref.shape[1]
    heads = q_ref.shape[0] // head_dim
    scale = head_dim ** (-0.5)
    queries = stack_heads(q_ref[...], head_dim)
    d_mixed = stack_heads(dout_ref[...], head_dim)
    mixed = stack_heads(out_ref[...], head_dim)
    delta = jnp.sum(mixed.astype(F32) * d_mixed.astype(F32), axis=0, keepdims=True)
    lse = lse_ref[0, 0]

    @pl.when(pl.program_id(1) == 0)
    def clear():
        dkv_ref[...] = jnp.zeros_like(dkv_ref)

    def block(step, accum, first_block):
        keys = kv_ref[0, step, :, :head_dim]
        values = kv_ref[0, step, :, head_dim:]
        scores = masked_scores(scal_ref, queries, keys, step, seg, heads, with_length, first_block)
        probs = jnp.exp(scores - lse)
        d_probs = dot(values, d_mixed)
        d_scores = (probs * (d_probs - delta)).astype(BF)
        dkv_ref[0, step, :, :head_dim] += dot(d_scores, queries, ((1,), (1,))) * scale
        dkv_ref[0, step, :, head_dim:] += dot(probs.astype(BF), d_mixed, ((1,), (1,)))
        return accum + dot(keys, d_scores, ((0,), (0,)))

    accum = block(0, jnp.zeros((head_dim, heads * seg), F32), True)
    accum = lax.fori_loop(1, scal_ref[0] + 1, lambda t, s: block(t, s, False), accum)
    dq_ref[...] = (unstack_heads(accum, seg) * scale).astype(BF)


def attn_specs(slots, steps, pair, seg, rows, groups, head_dim):
    lanes = rows // groups // head_dim * seg
    scal = pl.BlockSpec(memory_space=pltpu.SMEM)
    feat = pl.BlockSpec((rows // groups, seg), lambda s, g: (g, s))
    kv = pl.BlockSpec((1, steps, pair, 2 * head_dim), lambda s, g: (s, 0, 0, 0))
    lse = pl.BlockSpec((1, 1, 1, lanes), lambda s, g: (s, g, 0, 0))
    return scal, feat, kv, lse, lanes


def attn_forward(scal, q_t, kv, groups, with_length):
    slots, steps, pair, width = kv.shape
    rows, cols = q_t.shape
    seg = cols // slots
    scal_s, feat, kv_s, lse_s, lanes = attn_specs(slots, steps, pair, seg, rows, groups, width // 2)
    return pl.pallas_call(
        functools.partial(attn_fwd_kernel, with_length=with_length),
        grid=(slots, groups),
        in_specs=[scal_s, feat, kv_s],
        out_specs=[feat, lse_s],
        out_shape=[
            jax.ShapeDtypeStruct((rows, cols), BF),
            jax.ShapeDtypeStruct((slots, groups, 1, lanes), F32),
        ],
        compiler_params=pltpu.CompilerParams(vmem_limit_bytes=40 << 20),
        cost_estimate=pl.CostEstimate(
            flops=4 * rows * cols * steps * pair, bytes_accessed=6 << 20, transcendentals=0
        ),
    )(scal, q_t, kv)


def attn_backward(scal, q_t, kv, out_t, dout_t, lse, groups, with_length):
    slots, steps, pair, width = kv.shape
    rows, cols = q_t.shape
    seg = cols // slots
    scal_s, feat, kv_s, lse_s, lanes = attn_specs(slots, steps, pair, seg, rows, groups, width // 2)
    return pl.pallas_call(
        functools.partial(attn_bwd_kernel, with_length=with_length),
        grid=(slots, groups),
        in_specs=[scal_s, feat, kv_s, feat, feat, lse_s],
        out_specs=[feat, kv_s],
        out_shape=[
            jax.ShapeDtypeStruct((rows, cols), BF),
            jax.ShapeDtypeStruct(kv.shape, F32),
        ],
        compiler_params=pltpu.CompilerParams(vmem_limit_bytes=48 << 20),
        cost_estimate=pl.CostEstimate(
            flops=10 * rows * cols * steps * pair, bytes_accessed=9 << 20, transcendentals=0
        ),
    )(scal, q_t, kv, out_t, dout_t, lse)


def norm_stats(values):
    center = values - jnp.mean(values, axis=-1, keepdims=True)
    spread = jnp.mean(center * center, axis=-1, keepdims=True)
    rstd = lax.rsqrt(spread + EPSILON)
    return center * rstd, rstd


def norm_backward(d_values, unit, rstd, gain):
    scaled = d_values * gain
    return rstd * (
        scaled
        - jnp.mean(scaled, axis=-1, keepdims=True)
        - unit * jnp.mean(scaled * unit, axis=-1, keepdims=True)
    )


def gather_rows(shard, x, place):
    rows = shard.shape[0]
    half = rows // 2
    mine = lax.dynamic_slice_in_dim(shard, x * half, half, 0)
    direct = swap(mine, "y")
    other = swap(direct, "x")
    sib = swap(shard, "c")
    sib_direct = swap(direct, "c")
    sib_other = swap(other, "c")
    full = jnp.zeros((4 * rows,) + shard.shape[1:], shard.dtype)
    far = place ^ 2
    pieces = (
        (shard, place * rows),
        (sib, (place ^ 1) * rows),
        (direct, far * rows + x * half),
        (other, far * rows + (1 - x) * half),
        (sib_direct, (far ^ 1) * rows + x * half),
        (sib_other, (far ^ 1) * rows + (1 - x) * half),
    )
    for piece, start in pieces:
        full = lax.dynamic_update_slice_in_dim(full, piece, start, 0)
    return full


def gather_plane(block):
    half = block.shape[0] // 2
    from_x = swap(block, "x")
    from_y = swap(block, "y")
    diag = jnp.concatenate([swap(from_y[:half], "x"), swap(from_x[half:], "y")], axis=0)
    return [
        jnp.concatenate([part, swap(part, "c")], axis=0) for part in (block, from_x, from_y, diag)
    ]


def scatter_plane(parts):
    rows = parts[0].shape[0] // 2
    half = rows // 2
    own, to_x, to_y, diag = [
        part[:rows].astype(F32) + swap(part[rows:].astype(BF), "c").astype(F32) for part in parts
    ]
    via_x = swap(diag[:half].astype(BF), "x").astype(F32)
    via_y = swap(diag[half:].astype(BF), "y").astype(F32)
    to_y = jnp.concatenate([to_y[:half] + via_x, to_y[half:]], axis=0)
    to_x = jnp.concatenate([to_x[:half], to_x[half:] + via_y], axis=0)
    return own + swap(to_x.astype(BF), "x").astype(F32) + swap(to_y.astype(BF), "y").astype(F32)


def scatter_line(parts, z, length):
    def block(index):
        return pick(parts, jnp.clip(index, 0, length - 1), 0).astype(F32)

    from_left = from_right = None
    for step in range(1, length):
        up = block(length - step + z)
        down = block(z - length + step)
        if from_left is not None:
            up, down = up + from_left, down + from_right
        from_left = lax.ppermute(up.astype(BF), "z", [(i, i + 1) for i in range(step)]).astype(F32)
        from_right = lax.ppermute(
            down.astype(BF), "z", [(i, i - 1) for i in range(length - step, length)]
        ).astype(F32)
    return block(z) + from_left + from_right


def scatter_all(left_side, right_side, vectors, place_yczx, sizes):
    y, c, z, x = place_yczx
    length, width = sizes
    tokens = left_side.shape[0]
    block = width // (8 * length)
    left_parts = left_side.reshape(tokens, 2, 2, width // 4)
    left_mine = pick(left_parts, c, 2).reshape(tokens, width // 2)
    left_sib = swap(pick(left_parts, 1 - c, 2), "c").reshape(tokens, width // 2)
    right_sib = swap(right_side, "c")
    partial = dot(
        jnp.concatenate([left_mine, left_sib], axis=0),
        jnp.concatenate([right_side, right_sib], axis=0),
        ((0,), (0,)),
    )
    extra = jnp.pad(jnp.stack(vectors, axis=1), ((0, 0), (0, 128 - len(vectors))))
    extra = extra.reshape(2, 2, width // 4, 128)
    extra = pick(extra, c, 1) + swap(pick(extra, 1 - c, 1).astype(BF), "c").astype(F32)
    partial = jnp.concatenate([partial, extra.reshape(width // 2, 128)], axis=1)
    cols = partial.shape[1]
    partial = partial.reshape(2, length, 2, block, cols)
    cut = (cols // 256) * 128
    side_a, side_b = partial[..., :cut], partial[..., cut:]
    side_a = pick(side_a, y, 0) + swap(pick(side_a, 1 - y, 0).astype(BF), "y").astype(F32)
    side_b = pick(side_b, x, 2) + swap(pick(side_b, 1 - x, 2).astype(BF), "x").astype(F32)
    side_a = pick(side_a, x, 1) + swap(pick(side_a, 1 - x, 1).astype(BF), "x").astype(F32)
    side_b = pick(side_b, y, 0) + swap(pick(side_b, 1 - y, 0).astype(BF), "y").astype(F32)
    return scatter_line(jnp.concatenate([side_a, side_b], axis=-1), z, length)


def body(
    tokens,
    lengths,
    cotangent,
    norm_gain,
    norm_shift,
    query_weight,
    query_bias,
    keyval_weight,
    value_bias,
    mixer_weight,
    mixer_bias,
    ffnorm_gain,
    ffnorm_shift,
    up_weight,
    up_bias,
    down_weight,
    down_bias,
):
    y, c, z, x = [lax.axis_index(name) for name in ("y", "c", "z", "x")]
    length = lax.axis_size("z")
    place = y * 2 + c
    slots, seg, width = tokens.shape
    rows = slots * seg
    head_dim = value_bias.shape[0] * 4
    hidden = up_weight.shape[1]
    hidden_block = hidden // (8 * length)
    hidden_mine = hidden // 8
    with_length = 2 * length * seg > MIN_LEN
    scal = jnp.concatenate([jnp.stack([z, x]).astype(jnp.int32), lengths])

    quarter = width // 4
    small = jnp.stack(
        [
            norm_gain,
            norm_shift,
            query_bias,
            mixer_bias,
            ffnorm_gain,
            ffnorm_shift,
            down_bias,
            jnp.pad(value_bias, (0, quarter - value_bias.shape[0])),
        ]
    )
    pair = jnp.stack([small, swap(small, "c")])
    pair = jnp.where(c == 0, pair, pair[::-1])
    quad = jnp.stack([pair, swap(pair, "y")])
    quad = jnp.where(y == 0, quad, quad[::-1]).reshape(4, 8, quarter)
    smalls = quad.transpose(1, 0, 2).reshape(8, width).astype(F32)
    gain, shift, q_bias, m_bias, ffgain, ffshift, d_bias = [smalls[i][None, :] for i in range(7)]
    v_bias = quad[:, 7, : value_bias.shape[0]].reshape(1, head_dim).astype(F32)

    full_keyval = gather_rows(keyval_weight, x, place)
    full_query = gather_rows(query_weight, x, place)
    full_mixer = gather_rows(mixer_weight, x, place)

    down_mine = pick(down_weight.reshape(length, 2, hidden_block, width), x, 1).reshape(
        hidden_mine, width
    )
    up_bias_mine = pick(up_bias.reshape(length, 2, hidden_block), x, 1).reshape(1, hidden_mine)
    up_parts = pick(up_weight.reshape(quarter, 4, length, 2, hidden_block), x, 3).reshape(
        quarter, 4, hidden_mine
    )
    up_mine = jnp.zeros((width, hidden_mine), BF)
    for flip in range(4):
        piece = pick(up_parts, place ^ flip, 1)
        if flip:
            piece = lax.ppermute(piece, ("y", "c"), [(i, i ^ flip) for i in range(4)])
        up_mine = lax.dynamic_update_slice_in_dim(up_mine, piece, (place ^ flip) * quarter, 0)

    inputs = tokens.reshape(rows, width).astype(F32)
    unit1, rstd1 = norm_stats(inputs)
    first = (unit1 * gain + shift).astype(BF)
    kv_bias = jnp.concatenate([jnp.zeros_like(v_bias), v_bias], axis=1)
    keyvals = (dot(first, full_keyval) + kv_bias).astype(BF).reshape(slots, seg, 2 * head_dim)
    blocks = []
    current = keyvals
    for step in range(length):
        if step:
            current = lax.ppermute(current, "z", [(i, i + 1) for i in range(length - 1)])
        both = jnp.stack([current, swap(current, "x")], axis=1)
        both = jnp.where(x == 0, both, both[:, ::-1])
        blocks.append(both.reshape(slots, 2 * seg, 2 * head_dim))
    kv_all = jnp.stack(blocks, axis=1)
    q_t = (dot(full_query, first, ((0,), (1,))) + q_bias.reshape(width, 1)).astype(BF)
    mixed_t, lse = attn_forward(scal, q_t, kv_all, 4, with_length)
    residual = inputs + dot(mixed_t, full_mixer, ((0,), (0,))) + m_bias
    unit2, rstd2 = norm_stats(residual)
    second = (unit2 * ffgain + ffshift).astype(BF)

    token_pos = (z * 2 + x) * seg + jnp.arange(seg, dtype=jnp.int32)
    valid = (token_pos[None, :] < lengths[:, None]).astype(F32).reshape(rows, 1)
    d_out = cotangent.reshape(rows, width).astype(F32) * valid
    d_down = d_out.astype(BF)

    down_all = gather_plane(d_down)
    second_all = gather_plane(second)
    out_parts, dsecond_parts, actives, d_uppers = [], [], [], []
    for chip in range(4):
        d_active = dot(down_all[chip], down_mine, ((1,), (1,)))
        upper = dot(second_all[chip], up_mine) + up_bias_mine.astype(F32)
        inner = jnp.tanh(GELU_K * (upper + GELU_C * upper * upper * upper))
        active = (0.5 * upper * (1.0 + inner)).astype(BF)
        slope = 0.5 * (1.0 + inner) + 0.5 * upper * (1.0 - inner * inner) * GELU_K * (
            1.0 + 3.0 * GELU_C * upper * upper
        )
        d_upper = (d_active * slope).astype(BF)
        actives.append(active)
        d_uppers.append(d_upper)
        dsecond_parts.append(dot(d_upper, up_mine, ((1,), (1,))))
        out_parts.append(dot(active, down_mine))
    d_second = scatter_plane(dsecond_parts)
    output = residual + scatter_plane(out_parts) + d_bias
    layer_out = output.astype(BF).reshape(tokens.shape)
    active_cat = jnp.concatenate(actives, axis=0)
    d_upper_cat = jnp.concatenate(d_uppers, axis=0)
    down_cat = jnp.concatenate(down_all, axis=0)
    second_cat = jnp.concatenate(second_all, axis=0)
    down_part = dot(active_cat, down_cat, ((0,), (0,)))
    down_grad = scatter_line(down_part.reshape(length, hidden_block, width), z, length)
    ubias_part = jnp.sum(d_upper_cat.astype(F32), axis=0).reshape(length, hidden_block)
    ubias_grad = scatter_line(ubias_part, z, length)
    up_part = dot(second_cat, d_upper_cat, ((0,), (0,)))
    out_rows = width // (8 * length)
    up_part = up_part.reshape(4, length, 2, out_rows, hidden_mine).transpose(1, 0, 2, 3, 4)
    up_sum = scatter_line(up_part, z, length).astype(BF)
    up_sum = up_sum.reshape(2, 2, 2, out_rows, hidden_mine)
    up_rows = lax.all_to_all(
        up_sum.reshape(8, out_rows, hidden_mine), ("y", "c", "x"), 0, 0, tiled=True
    )
    up_grad = (
        up_rows.reshape(4, 2, out_rows, length, hidden_block)
        .transpose(2, 0, 3, 1, 4)
        .reshape(out_rows, hidden)
        .astype(F32)
    )

    d_residual = d_out + norm_backward(d_second, unit2, rstd2, ffgain)
    d_mix = d_residual.astype(BF)
    d_mixed_t = dot(full_mixer, d_mix, ((1,), (1,))).astype(BF)
    where = (y, c, z, x)
    sizes = (length, width)
    mixer_all = scatter_all(
        mixed_t.T,
        d_mix,
        (
            jnp.sum(d_mix.astype(F32), axis=0),
            jnp.sum(d_second * unit2, axis=0),
            jnp.sum(d_second, axis=0),
            jnp.sum(d_out, axis=0),
        ),
        where,
        sizes,
    )

    dq_t, dkv = attn_backward(scal, q_t, kv_all, mixed_t, d_mixed_t, lse, 4, with_length)
    dkv = dkv.reshape(slots, length, 2, seg, 2 * head_dim)
    running = None
    for step in range(length - 1, -1, -1):
        term = dkv[:, step]
        term = pick(term, x, 1) + swap(pick(term, 1 - x, 1).astype(BF), "x").astype(F32)
        if running is not None:
            term = term + lax.ppermute(
                running.astype(BF), "z", [(i, i - 1) for i in range(1, length)]
            ).astype(F32)
        running = term
    d_keyvals = running.reshape(rows, 2 * head_dim).astype(BF)
    d_first = dot(dq_t, full_query, ((0,), (1,))) + dot(d_keyvals, full_keyval, ((1,), (1,)))
    tokens_grad = (d_residual + norm_backward(d_first, unit1, rstd1, gain)).astype(BF)
    d_queries = dq_t.T
    devices = 8 * length
    vbias = jnp.sum(d_keyvals[:, head_dim:].astype(F32), axis=0)
    vbias = jnp.pad(
        vbias.reshape(devices, head_dim // devices),
        ((0, 0), (0, out_rows - head_dim // devices)),
    ).reshape(width)
    query_all = scatter_all(
        first,
        jnp.concatenate([d_queries, d_keyvals], axis=1),
        (
            jnp.sum(d_first * unit1, axis=0),
            jnp.sum(d_first, axis=0),
            jnp.sum(d_queries.astype(F32), axis=0),
            vbias,
        ),
        where,
        sizes,
    )
    kv_end = width + 2 * head_dim
    return (
        layer_out,
        tokens_grad.reshape(tokens.shape),
        query_all[:, kv_end],
        query_all[:, kv_end + 1],
        query_all[:, :width],
        query_all[:, kv_end + 2],
        query_all[:, width:kv_end],
        query_all[: head_dim // devices, kv_end + 3],
        mixer_all[:, :width],
        mixer_all[:, width],
        mixer_all[:, width + 1],
        mixer_all[:, width + 2],
        up_grad,
        ubias_grad,
        down_grad,
        mixer_all[:, width + 3],
    )


def solution(mesh):
    ctx = mesh.shape["ctx"]
    fine = Mesh(mesh.devices.reshape(2, 2, ctx // 2, 2), ("y", "c", "z", "x"))
    fsdp, both, every = ("y", "c"), ("z", "x"), ("y", "c", "z", "x")
    return jax.shard_map(
        body,
        mesh=fine,
        in_specs=(
            P(fsdp, both, None),
            P(fsdp),
            P(fsdp, both, None),
            P(fsdp),
            P(fsdp),
            P(fsdp, None),
            P(fsdp),
            P(fsdp, None),
            P(fsdp),
            P(fsdp, None),
            P(fsdp),
            P(fsdp),
            P(fsdp),
            P(fsdp, None),
            P(fsdp),
            P(fsdp, None),
            P(fsdp),
        ),
        out_specs=(
            P(fsdp, both, None),
            P(fsdp, both, None),
            P(every),
            P(every),
            P(every, None),
            P(every),
            P(every, None),
            P(every),
            P(every, None),
            P(every),
            P(every),
            P(every),
            P(every, None),
            P(every),
            P(every, None),
            P(every),
        ),
        check_vma=False,
    )
```

time: 4600 us -> 850 us (0.18)
  waiting for transfers between devices: 4190 us -> 320 us
  starting transfers between devices: 0.69 us -> 154 us
  local copies, waits for them, and re-layouts: 50.1 us -> 156 us
  matrix products: 213 us -> 121 us
  blocking collectives: 50 us -> 0 us
    reduce_scatter x6 -> x0, waiting for transfers between devices: 3730 us -> none  [the longest x1 1410 us: body(): lax.psum_scatter(outer_term(active, d_down), ('fsdp', 'ctx'), scatter_dim...]
    all_gather x6 -> x0, waiting for transfers between devices: 435 us -> none  [the longest x1 189 us: body(): lax.all_gather(shards[12], 'fsdp', axis=0, tiled=True)]
    ppermute x0 -> x110, waiting for transfers between devices: none -> 319 us  [the longest x71 217 us: swap(): return lax.ppermute(values, axis, [(0, 1), (1, 0)])]
    ppermute x0 -> x110, starting transfers between devices: none -> 149 us  [the longest x15 69.1 us: scatter_line(): lax.ppermute(up.astype(BF), 'z', [(i, i + 1) for i in range(step)])]
    dot_general x29 -> x26, matrix products: 213 us -> 121 us  [dot(): lax.dot_general(left_side, right_side, (dims, ((), ())), preferred_elemen...]
  transfers between devices with their start and end apart: 13 -> 111, of which waited for: 11 -> 39; matrix products, arithmetic and copies ran while one was open for 4% -> 39% of each run, Pallas kernels for 0% -> 2%
where the time goes in v1:
time: 850 us; the launch traced here: 840 us
  waiting for transfers between devices  320 us (38%)
  local copies, waits for them, and re-layouts  156 us (18%)
  starting transfers between devices  154 us (18%)
  matrix products  121 us (14%)
  other arithmetic  73.1 us (9%)
  Pallas kernels  13.3 us (2%)
    ppermute x71, waiting for transfers between devices, swap(): return lax.ppermute(values, axis, [(0, 1), (1, 0)])  217 us
    dot_general x26, matrix products, dot(): lax.dot_general(left_side, right_side, (dims, ((), ())), preferred_elemen...  121 us
    ppermute x15, starting transfers between devices, scatter_line(): lax.ppermute(up.astype(BF), 'z', [(i, i + 1) for i in range(step)])  69.1 us
    ppermute x15, waiting for transfers between devices, scatter_line(): lax.ppermute(up.astype(BF), 'z', [(i, i + 1) for i in range(step)])  55.8 us
    ppermute x71, starting transfers between devices, swap(): return lax.ppermute(values, axis, [(0, 1), (1, 0)])  46.9 us
    unnamed x249, local copies, waits for them, and re-layouts  37.1 us
    dynamic_slice x15, local copies, waits for them, and re-layouts, pick(): return lax.dynamic_index_in_dim(values, index, axis, keepdims=False)  25.9 us
    ppermute x3, waiting for transfers between devices, body(): lax.ppermute(running.astype(BF), 'z', [(i, i - 1) for i in range(1, lengt...  25 us
  transfers between devices with their start and end apart: 111, of which 39 were waited for; matrix products, arithmetic and copies ran while one was open for 39% of the time, Pallas kernels for 2%

profile of v1, /device:TPU:0, one launch (start us, length us, event | category | flops | bytes accessed | tf_op | source)
XLA Modules:
  0.0 840.2 jit_solution(13476344462789078126)
XLA Ops:
  14.9 11.9 %copy.111 = bf16[512,8192]{0,1:T(8,128)(2,1)} copy(bf16[512,8192]{1,0:T(8,128)(2,1)} %param.30) | data formatting | bytes 16777216 | tf_op args[13]
  26.8 5.1 constant_dynamic-slice_fusion.16
  67.1 3.8 collective-permute-done.9
  77.8 3.9 collective-permute-start.13
  85.7 4.2 collective-permute-start.15
  91.5 4.4 broadcast.127.clone
  103.1 4.1 collective-permute-start.17
  128.6 21.3 %collective-permute-done.48 = bf16[256,2048]{1,0:T(8,128)(2,1)} collective-permute-done((bf16[256,2048]{1,0:T(8,128)(2,1)}, bf16[256,2048]{1,0:T(8,128)(2,1)}, u32[]{:S(2)}, u32[]{:S(2)}) %collective-permute-start.48) | collective-permute-done | bytes 1048608 | tf_op jit(solution)/shard_map/ppermute | solution.py:24
  156.9 14.4 %collective-permute-done.27 = bf16[512,1024]{1,0:T(8,128)(2,1)S(1)} collective-permute-done((bf16[512,1024]{1,0:T(8,128)(2,1)}, bf16[512,1024]{1,0:T(8,128)(2,1)S(1)}, u32[]{:S(2)}, u32[]{:S(2)}) %collective-permute-start.27) | collective-permute-done | bytes 1048608 | tf_op jit(solution)/shard_map/ppermute | solution.py:347
  175.6 10.3 %collective-permute-done.49 = bf16[128,2048]{1,0:T(8,128)(2,1)S(1)} collective-permute-done((bf16[128,2048]{1,0:T(8,128)(2,1)S(1)}, bf16[128,2048]{1,0:T(8,128)(2,1)S(1)}, u32[]{:S(2)}, u32[]{:S(2)}) %collective-permute-start.49) | collective-permute-done | bytes 524320 | tf_op jit(solution)/shard_map/ppermute | solution.py:24
  185.9 19.6 %collective-permute-done.50 = bf16[128,2048]{1,0:T(8,128)(2,1)S(1)} collective-permute-done((bf16[128,2048]{1,0:T(8,128)(2,1)S(1)}, bf16[128,2048]{1,0:T(8,128)(2,1)S(1)}, u32[]{:S(2)}, u32[]{:S(2)}) %collective-permute-start.50) | collective-permute-done | bytes 524320 | tf_op jit(solution)/shard_map/ppermute | solution.py:24
  213.2 39.7 %collective-permute-done.2 = bf16[256,2048]{1,0:T(8,128)(2,1)S(1)} collective-permute-done((bf16[256,2048]{1,0:T(8,128)(2,1)S(1)}, bf16[256,2048]{1,0:T(8,128)(2,1)S(1)}, u32[]{:S(2)}, u32[]{:S(2)}) %collective-permute-start.2) | collective-permute-done | bytes 1048608 | tf_op jit(solution)/shard_map/ppermute | solution.py:24
  262.4 5.9 fusion.15.q_ref
  268.3 5.6 shard_map.288
  285.9 18.0 %collective-permute-done.32 = bf16[256,2048]{1,0:T(8,128)(2,1)S(1)} collective-permute-done((bf16[256,2048]{1,0:T(8,128)(2,1)S(1)}, bf16[256,2048]{1,0:T(8,128)(2,1)S(1)}, u32[]{:S(2)}, u32[]{:S(2)}) %collective-permute-start.32) | collective-permute-done | bytes 1048608 | tf_op jit(solution)/shard_map/ppermute | solution.py:24
  318.4 3.8 fusion.80
  322.2 5.3 fusion.56
  337.0 8.2 multiply_convert_fusion.2
  345.3 5.7 fusion.46
  350.9 4.4 fusion.245
  359.8 4.3 fusion.246
  368.4 4.3 fusion.242
  372.8 4.3 fusion.243
  377.1 4.3 fusion.240
  381.5 11.4 %fusion = f32[1024,2048]{1,0:T(8,128)} fusion(bf16[2048,2048]{1,0:T(8,128)(2,1)S(1)} %bitcast.453, bf16[512,1024]{1,0:T(8,128)(2,1)S(1)} %copy-done.100, bf16[512,1024]{1,0:T(8,128)(2,1)S(1)} %copy-done.101, bf16[512,1024]{1,0:T(8,128)(2,1)S(1)} %get-tuple-element.98, bf16[512,1024]{1,0:T(8,128)(2,1)S(1)} %copy-done.102), kind=kOutput, calls=%fused_computation.34 | convolution fusion | flops 8606711808 | bytes 20971520 | tf_op jit(solution)/shard_map/dot_general | solution.py:20
  394.0 13.4 %fusion.147 = f32[2048,1024]{1,0:T(8,128)} fusion(bf16[2048,2048]{1,0:T(8,128)(2,1)} %constant_dynamic-update-slice_fusion, bf16[512,1024]{1,0:T(8,128)(2,1)S(1)} %fusion.51, bf16[512,1024]{1,0:T(8,128)(2,1)S(1)} %fusion.56, bf16[512,1024]{1,0:T(8,128)(2,1)S(1)} %fusion.46, bf16[512,1024]{1,0:T(8,128)(2,1)S(1)} %fusion.41), kind=kOutput, calls=%fused_computation.277 | convolution fusion | flops 8606711808 | bytes 20971520 | tf_op jit(solution)/shard_map/dot_general | solution.py:20
  407.4 7.6 collective-permute-start.98
  421.8 6.8 collective-permute-start.100
  443.0 6.4 collective-permute-start.92
  457.6 36.1 %collective-permute-done.104 = bf16[256,2048]{1,0:T(8,128)(2,1)S(1)} collective-permute-done((bf16[256,2048]{1,0:T(8,128)(2,1)S(1)}, bf16[256,2048]{1,0:T(8,128)(2,1)S(1)}, u32[]{:S(2)}, u32[]{:S(2)}) %collective-permute-start.104) | collective-permute-done | bytes 1048608 | tf_op jit(solution)/shard_map/ppermute | solution.py:244
  501.4 9.6 %collective-permute-done.37 = bf16[128,2048]{1,0:T(8,128)(2,1)S(1)} collective-permute-done((bf16[128,2048]{1,0:T(8,128)(2,1)S(1)}, bf16[128,2048]{1,0:T(8,128)(2,1)S(1)}, u32[]{:S(2)}, u32[]{:S(2)}) %collective-permute-start.37) | collective-permute-done | bytes 524320 | tf_op jit(solution)/shard_map/ppermute | solution.py:24
  512.0 4.4 collective-permute-start.105
  516.6 8.0 collective-permute-done.53
  526.7 10.5 %collective-permute-done.57 = bf16[128,2048]{1,0:T(8,128)(2,1)S(1)} collective-permute-done((bf16[128,2048]{1,0:T(8,128)(2,1)S(1)}, bf16[128,2048]{1,0:T(8,128)(2,1)S(1)}, u32[]{:S(2)}, u32[]{:S(2)}) %collective-permute-start.57) | collective-permute-done | bytes 524320 | tf_op jit(solution)/shard_map/ppermute | solution.py:24
  537.2 4.4 collective-permute-start.93
  549.0 13.0 %collective-permute-done.93 = bf16[4,2,64,1024]{3,2,1,0:T(8,128)(2,1)S(1)} collective-permute-done((bf16[4,2,64,1024]{3,2,1,0:T(8,128)(2,1)S(1)}, bf16[4,2,64,1024]{3,2,1,0:T(8,128)(2,1)S(1)}, u32[]{:S(2)}, u32[]{:S(2)}) %collective-permute-start.93) | collective-permute-done | bytes 1048608 | tf_op jit(solution)/shard_map/ppermute | solution.py:244
  565.0 4.2 collective-permute-done.58
  573.2 15.6 %collective-permute-done.38 = bf16[256,2048]{1,0:T(8,128)(2,1)S(1)} collective-permute-done((bf16[256,2048]{1,0:T(8,128)(2,1)S(1)}, bf16[256,2048]{1,0:T(8,128)(2,1)S(1)}, u32[]{:S(2)}, u32[]{:S(2)}) %collective-permute-start.38) | collective-permute-done | bytes 1048608 | tf_op jit(solution)/shard_map/ppermute | solution.py:24
  594.4 7.8 shard_map.289
  618.0 3.9 collective-permute-done.63
  627.1 5.9 collective-permute-start.94
  645.0 21.1 %collective-permute-done.65 = bf16[2,128,256]{2,1,0:T(8,128)(2,1)S(1)} collective-permute-done((bf16[2,128,256]{2,1,0:T(8,128)(2,1)S(1)}, bf16[2,128,256]{2,1,0:T(8,128)(2,1)S(1)}, u32[]{:S(2)}, u32[]{:S(2)}) %collective-permute-start.65) | collective-permute-done | bytes 131104 | tf_op jit(solution)/shard_map/ppermute | solution.py:442
  669.6 8.2 multiply_reduce_fusion.2
  685.7 4.9 collective-permute-start.106
  690.7 3.7 fusion.102
  701.5 3.8 fusion.117
  705.3 4.6 all-to-all-start
  709.9 4.2 fusion.22
  717.8 5.2 collective-permute-done.81
  726.5 3.7 collective-permute-done.84
  732.5 4.2 fusion.111
  744.7 4.0 reshape.360
  748.7 4.1 collective-permute-done.82
  754.0 17.2 %collective-permute-done.85 = bf16[4,64,1152]{2,1,0:T(8,128)(2,1)} collective-permute-done((bf16[4,64,1152]{2,1,0:T(8,128)(2,1)S(1)}, bf16[4,64,1152]{2,1,0:T(8,128)(2,1)}, u32[]{:S(2)}, u32[]{:S(2)}) %collective-permute-start.85) | collective-permute-done | bytes 589856 | tf_op jit(solution)/shard_map/ppermute | solution.py:24
  775.6 5.3 collective-permute-done.71
  783.2 4.6 collective-permute-start.86
  788.4 4.1 collective-permute-done.69
  792.6 5.0 collective-permute-done.72
  797.9 3.9 collective-permute-start.73
  804.6 4.9 collective-permute-done.73
  809.7 4.4 collective-permute-start.74
  815.7 4.4 collective-permute-start.88
  821.9 6.3 collective-permute-start.75
  832.8 4.1 collective-permute-done.78
  (657 shorter events, 315.3 us)
Async XLA Ops:
  6.2 44.7 %collective-permute-start.5 = (bf16[8,512]{1,0:T(8,128)(2,1)S(1)}, bf16[8,512]{1,0:T(8,128)(2,1)}, u32[]{:S(2)}, u32[]{:S(2)}) collective-permute-start(bf16[8,512]{1,0:T(8,128)(2,1)S(1)} %stack.124), channel_id=1, source_target_pairs={{0,8},{8,0},{1,9},{9,1},{2,10},{10,2},{3,11},{11,3},{4,12},{12,4},... | collective-permute-start | bytes 24584 | tf_op jit(solution)/shard_map/ppermute | solution.py:24
  6.7 64.1 %collective-permute-start.7 = (bf16[512,256]{1,0:T(8,128)(2,1)}, bf16[512,256]{1,0:T(8,128)(2,1)}, u32[]{:S(2)}, u32[]{:S(2)}) collective-permute-start(bf16[512,256]{1,0:T(8,128)(2,1)} %param.24), channel_id=1, source_target_pairs={{0,8},{8,0},{1,9},{9,1},{2,10},{10,2},{3,11},{11,3},{4,12},{12,4},... | collective-permute-start | bytes 786440 | tf_op jit(solution)/shard_map/ppermute | solution.py:24
  8.4 56.3 %collective-permute-start.8 = (bf16[256,256]{1,0:T(8,128)(2,1)}, bf16[256,256]{1,0:T(8,128)(2,1)S(1)}, u32[]{:S(2)}, u32[]{:S(2)}) collective-permute-start(bf16[256,256]{1,0:T(8,128)(2,1)} %constant_dynamic-slice_fusion.24), channel_id=1, source_target_pairs={{0,16},{16,0},{1,17},{17,1},{2,18},{18,2},{3,19},{19,3},{4,20},{20... | collective-permute-start | bytes 393224 | tf_op jit(solution)/shard_map/ppermute | solution.py:24
  13.6 110.9 %collective-permute-start.20 = (bf16[256,2048]{1,0:T(8,128)(2,1)}, bf16[256,2048]{1,0:T(8,128)(2,1)}, u32[]{:S(2)}, u32[]{:S(2)}) collective-permute-start(bf16[256,2048]{1,0:T(8,128)(2,1)} %constant_dynamic-slice_fusion.23), channel_id=1, source_target_pairs={{0,16},{16,0},{1,17},{17,1},{2,18},{18,2},{3,19},{19,3},{4,20},{20... | collective-permute-start | bytes 3145736 | tf_op jit(solution)/shard_map/ppermute | solution.py:24
  63.3 37.8 %collective-permute-start.66 = (bf16[256,2,512]{2,0,1:T(8,128)(2,1)}, bf16[256,2,512]{2,0,1:T(8,128)(2,1)}, u32[]{:S(2)}, u32[]{:S(2)}) collective-permute-start(bf16[256,2,512]{2,0,1:T(8,128)(2,1)} %bitcast.382), channel_id=1, source_target_pairs={{0,8},{8,0},{1,9},{9,1},{2,10},{10,2},{3,11},{11,3},{4,12},{12,4},... | collective-permute-start | bytes 1572872 | tf_op jit(solution)/shard_map/ppermute | solution.py:24
  84.2 16.7 %collective-permute-start.12 = (bf16[2,128,256]{2,1,0:T(8,128)(2,1)}, bf16[2,128,256]{2,1,0:T(8,128)(2,1)}, u32[]{:S(2)}, u32[]{:S(2)}) collective-permute-start(bf16[2,128,256]{2,1,0:T(8,128)(2,1)} %bitcast.16), channel_id=1, source_target_pairs={{0,1},{1,0},{2,3},{3,2},{4,5},{5,4},{6,7},{7,6},{8,9},{9,8},{10,11... | collective-permute-start | bytes 393224 | tf_op jit(solution)/shard_map/ppermute | solution.py:24
  85.7 16.8 %collective-permute-start.15 = (bf16[2,128,256]{2,1,0:T(8,128)(2,1)S(1)}, bf16[2,128,256]{2,1,0:T(8,128)(2,1)S(1)}, u32[]{:S(2)}, u32[]{:S(2)}) collective-permute-start(bf16[2,128,256]{2,1,0:T(8,128)(2,1)S(1)} %collective-permute-done.13), channel_id=1, source_target_pairs={{0,2},{2,4},{4,6},{1,3},{3,5},{5,7},{8,10},{10,12},{12,14},{9,11},... | collective-permute-start | bytes 393224 | tf_op jit(solution)/shard_map/ppermute | solution.py:359
  101.0 24.6 %collective-permute-start.25 = (bf16[512,1024]{1,0:T(8,128)(2,1)}, bf16[512,1024]{1,0:T(8,128)(2,1)}, u32[]{:S(2)}, u32[]{:S(2)}) collective-permute-start(bf16[512,1024]{1,0:T(8,128)(2,1)} %bitcast.437), channel_id=1, source_target_pairs={{0,8},{8,0},{16,24},{24,16},{1,9},{9,1},{17,25},{25,17},{2,10},{10... | collective-permute-start | bytes 3145736 | tf_op jit(solution)/shard_map/ppermute | solution.py:347
  101.0 26.3 %collective-permute-start.26 = (bf16[512,1024]{1,0:T(8,128)(2,1)}, bf16[512,1024]{1,0:T(8,128)(2,1)}, u32[]{:S(2)}, u32[]{:S(2)}) collective-permute-start(bf16[512,1024]{1,0:T(8,128)(2,1)} %bitcast.436), channel_id=1, source_target_pairs={{0,16},{8,24},{16,0},{24,8},{1,17},{9,25},{17,1},{25,9},{2,18},{10... | collective-permute-start | bytes 3145736 | tf_op jit(solution)/shard_map/ppermute | solution.py:347
  102.6 47.3 %collective-permute-start.48 = (bf16[256,2048]{1,0:T(8,128)(2,1)}, bf16[256,2048]{1,0:T(8,128)(2,1)}, u32[]{:S(2)}, u32[]{:S(2)}) collective-permute-start(bf16[256,2048]{1,0:T(8,128)(2,1)} %get-tuple-element.111), channel_id=1, source_target_pairs={{0,16},{16,0},{1,17},{17,1},{2,18},{18,2},{3,19},{19,3},{4,20},{20... | collective-permute-start | bytes 3145736 | tf_op jit(solution)/shard_map/ppermute | solution.py:24
  120.9 30.5 %collective-permute-start.45 = (bf16[256,2048]{1,0:T(8,128)(2,1)}, bf16[256,2048]{1,0:T(8,128)(2,1)S(1)}, u32[]{:S(2)}, u32[]{:S(2)}) collective-permute-start(bf16[256,2048]{1,0:T(8,128)(2,1)} %get-tuple-element.111), channel_id=1, source_target_pairs={{0,1},{1,0},{2,3},{3,2},{4,5},{5,4},{6,7},{7,6},{8,9},{9,8},{10,11... | collective-permute-start | bytes 3145736 | tf_op jit(solution)/shard_map/ppermute | solution.py:24
  124.5 82.6 %collective-permute-start = (bf16[512,2048]{1,0:T(8,128)(2,1)}, bf16[512,2048]{1,0:T(8,128)(2,1)S(1)}, u32[]{:S(2)}, u32[]{:S(2)}) collective-permute-start(bf16[512,2048]{1,0:T(8,128)(2,1)} %param.22), channel_id=1, source_target_pairs={{0,8},{8,0},{1,9},{9,1},{2,10},{10,2},{3,11},{11,3},{4,12},{12,4},... | collective-permute-start | bytes 6291464 | tf_op jit(solution)/shard_map/ppermute | solution.py:24
  125.5 46.4 %collective-permute-start.43 = (bf16[256,2048]{1,0:T(8,128)(2,1)}, bf16[256,2048]{1,0:T(8,128)(2,1)S(1)}, u32[]{:S(2)}, u32[]{:S(2)}) collective-permute-start(bf16[256,2048]{1,0:T(8,128)(2,1)} %get-tuple-element.111), channel_id=1, source_target_pairs={{0,8},{8,0},{1,9},{9,1},{2,10},{10,2},{3,11},{11,3},{4,12},{12,4},... | collective-permute-start | bytes 3145736 | tf_op jit(solution)/shard_map/ppermute | solution.py:24
  127.4 43.9 %collective-permute-start.27 = (bf16[512,1024]{1,0:T(8,128)(2,1)}, bf16[512,1024]{1,0:T(8,128)(2,1)S(1)}, u32[]{:S(2)}, u32[]{:S(2)}) collective-permute-start(bf16[512,1024]{1,0:T(8,128)(2,1)} %bitcast.438), channel_id=1, source_target_pairs={{0,24},{8,16},{16,8},{24,0},{1,25},{9,17},{17,9},{25,1},{2,26},{10... | collective-permute-start | bytes 3145736 | tf_op jit(solution)/shard_map/ppermute | solution.py:347
  149.9 60.4 %collective-permute-start.19 = (bf16[512,2048]{1,0:T(8,128)(2,1)}, bf16[512,2048]{1,0:T(8,128)(2,1)S(1)}, u32[]{:S(2)}, u32[]{:S(2)}) collective-permute-start(bf16[512,2048]{1,0:T(8,128)(2,1)} %param.26), channel_id=1, source_target_pairs={{0,8},{8,0},{1,9},{9,1},{2,10},{10,2},{3,11},{11,3},{4,12},{12,4},... | collective-permute-start | bytes 6291464 | tf_op jit(solution)/shard_map/ppermute | solution.py:24
  151.4 55.7 %collective-permute-start.1 = (bf16[256,2048]{1,0:T(8,128)(2,1)S(1)}, bf16[256,2048]{1,0:T(8,128)(2,1)S(1)}, u32[]{:S(2)}, u32[]{:S(2)}) collective-permute-start(bf16[256,2048]{1,0:T(8,128)(2,1)S(1)} %copy-done.58), channel_id=1, source_target_pairs={{0,16},{16,0},{1,17},{17,1},{2,18},{18,2},{3,19},{19,3},{4,20},{20... | collective-permute-start | bytes 3145736 | tf_op jit(solution)/shard_map/ppermute | solution.py:24
  171.9 33.6 %collective-permute-start.50 = (bf16[128,2048]{1,0:T(8,128)(2,1)S(1)}, bf16[128,2048]{1,0:T(8,128)(2,1)S(1)}, u32[]{:S(2)}, u32[]{:S(2)}) collective-permute-start(bf16[128,2048]{1,0:T(8,128)(2,1)S(1)} %slice.296), channel_id=1, source_target_pairs={{0,16},{16,0},{1,17},{17,1},{2,18},{18,2},{3,19},{19,3},{4,20},{20... | collective-permute-start | bytes 1572872 | tf_op jit(solution)/shard_map/ppermute | solution.py:24
  185.9 75.1 %collective-permute-start.22 = (bf16[256,2048]{1,0:T(8,128)(2,1)}, bf16[256,2048]{1,0:T(8,128)(2,1)S(1)}, u32[]{:S(2)}, u32[]{:S(2)}) collective-permute-start(bf16[256,2048]{1,0:T(8,128)(2,1)} %collective-permute-done.20), channel_id=1, source_target_pairs={{0,8},{8,0},{1,9},{9,1},{2,10},{10,2},{3,11},{11,3},{4,12},{12,4},... | collective-permute-start | bytes 3145736 | tf_op jit(solution)/shard_map/ppermute | solution.py:24
  205.5 52.5 %collective-permute-start.21 = (bf16[256,2048]{1,0:T(8,128)(2,1)}, bf16[256,2048]{1,0:T(8,128)(2,1)}, u32[]{:S(2)}, u32[]{:S(2)}) collective-permute-start(bf16[256,2048]{1,0:T(8,128)(2,1)} %collective-permute-done.20), channel_id=1, source_target_pairs={{0,1},{1,0},{2,3},{3,2},{4,5},{5,4},{6,7},{7,6},{8,9},{9,8},{10,11... | collective-permute-start | bytes 3145736 | tf_op jit(solution)/shard_map/ppermute | solution.py:24
  207.1 46.9 %collective-permute-start.46 = (bf16[256,2048]{1,0:T(8,128)(2,1)S(1)}, bf16[256,2048]{1,0:T(8,128)(2,1)S(1)}, u32[]{:S(2)}, u32[]{:S(2)}) collective-permute-start(bf16[256,2048]{1,0:T(8,128)(2,1)S(1)} %collective-permute-done.45), channel_id=1, source_target_pairs={{0,8},{8,0},{1,9},{9,1},{2,10},{10,2},{3,11},{11,3},{4,12},{12,4},... | collective-permute-start | bytes 3145736 | tf_op jit(solution)/shard_map/ppermute | solution.py:24
  207.1 45.8 %collective-permute-start.2 = (bf16[256,2048]{1,0:T(8,128)(2,1)S(1)}, bf16[256,2048]{1,0:T(8,128)(2,1)S(1)}, u32[]{:S(2)}, u32[]{:S(2)}) collective-permute-start(bf16[256,2048]{1,0:T(8,128)(2,1)S(1)} %collective-permute-done.1), channel_id=1, source_target_pairs={{0,1},{1,0},{2,3},{3,2},{4,5},{5,4},{6,7},{7,6},{8,9},{9,8},{10,11... | collective-permute-start | bytes 3145736 | tf_op jit(solution)/shard_map/ppermute | solution.py:24
  210.3 49.1 %collective-permute-start.3 = (bf16[256,2048]{1,0:T(8,128)(2,1)S(1)}, bf16[256,2048]{1,0:T(8,128)(2,1)S(1)}, u32[]{:S(2)}, u32[]{:S(2)}) collective-permute-start(bf16[256,2048]{1,0:T(8,128)(2,1)S(1)} %collective-permute-done.1), channel_id=1, source_target_pairs={{0,8},{8,0},{1,9},{9,1},{2,10},{10,2},{3,11},{11,3},{4,12},{12,4},... | collective-permute-start | bytes 3145736 | tf_op jit(solution)/shard_map/ppermute | solution.py:24
  252.9 27.9 %collective-permute-start.55 = (bf16[256,2048]{1,0:T(8,128)(2,1)}, bf16[256,2048]{1,0:T(8,128)(2,1)S(1)}, u32[]{:S(2)}, u32[]{:S(2)}) collective-permute-start(bf16[256,2048]{1,0:T(8,128)(2,1)} %collective-permute-done.48), channel_id=1, source_target_pairs={{0,8},{8,0},{1,9},{9,1},{2,10},{10,2},{3,11},{11,3},{4,12},{12,4},... | collective-permute-start | bytes 3145736 | tf_op jit(solution)/shard_map/ppermute | solution.py:24
  257.9 25.7 %collective-permute-start.51 = (bf16[256,2048]{1,0:T(8,128)(2,1)}, bf16[256,2048]{1,0:T(8,128)(2,1)S(1)}, u32[]{:S(2)}, u32[]{:S(2)}) collective-permute-start(bf16[256,2048]{1,0:T(8,128)(2,1)} %pad_maximum_fusion.6), channel_id=1, source_target_pairs={{0,8},{8,0},{1,9},{9,1},{2,10},{10,2},{3,11},{11,3},{4,12},{12,4},... | collective-permute-start | bytes 3145736 | tf_op jit(solution)/shard_map/ppermute | solution.py:24
  278.8 25.2 %collective-permute-start.32 = (bf16[256,2048]{1,0:T(8,128)(2,1)S(1)}, bf16[256,2048]{1,0:T(8,128)(2,1)S(1)}, u32[]{:S(2)}, u32[]{:S(2)}) collective-permute-start(bf16[256,2048]{1,0:T(8,128)(2,1)S(1)} %get-tuple-element.44), channel_id=1, source_target_pairs={{0,16},{16,0},{1,17},{17,1},{2,18},{18,2},{3,19},{19,3},{4,20},{20... | collective-permute-start | bytes 3145736 | tf_op jit(solution)/shard_map/ppermute | solution.py:24
  280.3 24.9 %collective-permute-start.29 = (bf16[256,2048]{1,0:T(8,128)(2,1)S(1)}, bf16[256,2048]{1,0:T(8,128)(2,1)S(1)}, u32[]{:S(2)}, u32[]{:S(2)}) collective-permute-start(bf16[256,2048]{1,0:T(8,128)(2,1)S(1)} %get-tuple-element.44), channel_id=1, source_target_pairs={{0,1},{1,0},{2,3},{3,2},{4,5},{5,4},{6,7},{7,6},{8,9},{9,8},{10,11... | collective-permute-start | bytes 3145736 | tf_op jit(solution)/shard_map/ppermute | solution.py:24
  280.8 25.4 %collective-permute-start.24 = (bf16[256,2048]{1,0:T(8,128)(2,1)S(1)}, bf16[256,2048]{1,0:T(8,128)(2,1)S(1)}, u32[]{:S(2)}, u32[]{:S(2)}) collective-permute-start(bf16[256,2048]{1,0:T(8,128)(2,1)S(1)} %get-tuple-element.44), channel_id=1, source_target_pairs={{0,8},{8,0},{1,9},{9,1},{2,10},{10,2},{3,11},{11,3},{4,12},{12,4},... | collective-permute-start | bytes 3145736 | tf_op jit(solution)/shard_map/ppermute | solution.py:24
  315.7 232.8 %collective-permute-start.44 = (bf16[256,2048]{1,0:T(8,128)(2,1)}, bf16[256,2048]{1,0:T(8,128)(2,1)S(1)}, u32[]{:S(2)}, u32[]{:S(2)}) collective-permute-start(bf16[256,2048]{1,0:T(8,128)(2,1)} %slice.388), channel_id=1, source_target_pairs={{0,8},{8,0},{1,9},{9,1},{2,10},{10,2},{3,11},{11,3},{4,12},{12,4},... | collective-permute-start | bytes 3145736 | tf_op jit(solution)/shard_map/ppermute | solution.py:24
  316.2 17.3 %collective-permute-start.30 = (bf16[256,2048]{1,0:T(8,128)(2,1)S(1)}, bf16[256,2048]{1,0:T(8,128)(2,1)S(1)}, u32[]{:S(2)}, u32[]{:S(2)}) collective-permute-start(bf16[256,2048]{1,0:T(8,128)(2,1)S(1)} %collective-permute-done.29), channel_id=1, source_target_pairs={{0,8},{8,0},{1,9},{9,1},{2,10},{10,2},{3,11},{11,3},{4,12},{12,4},... | collective-permute-start | bytes 3145736 | tf_op jit(solution)/shard_map/ppermute | solution.py:24
  318.3 15.5 %collective-permute-start.35 = (bf16[256,2048]{1,0:T(8,128)(2,1)S(1)}, bf16[256,2048]{1,0:T(8,128)(2,1)S(1)}, u32[]{:S(2)}, u32[]{:S(2)}) collective-permute-start(bf16[256,2048]{1,0:T(8,128)(2,1)S(1)} %pad_maximum_fusion.3), channel_id=1, source_target_pairs={{0,8},{8,0},{1,9},{9,1},{2,10},{10,2},{3,11},{11,3},{4,12},{12,4},... | collective-permute-start | bytes 3145736 | tf_op jit(solution)/shard_map/ppermute | solution.py:24
  332.9 110.0 %collective-permute-start.56 = (bf16[256,2048]{1,0:T(8,128)(2,1)}, bf16[256,2048]{1,0:T(8,128)(2,1)S(1)}, u32[]{:S(2)}, u32[]{:S(2)}) collective-permute-start(bf16[256,2048]{1,0:T(8,128)(2,1)} %slice.385), channel_id=1, source_target_pairs={{0,8},{8,0},{1,9},{9,1},{2,10},{10,2},{3,11},{11,3},{4,12},{12,4},... | collective-permute-start | bytes 3145736 | tf_op jit(solution)/shard_map/ppermute | solution.py:24
  367.6 82.3 %collective-permute-start.31 = (bf16[256,2048]{1,0:T(8,128)(2,1)}, bf16[256,2048]{1,0:T(8,128)(2,1)}, u32[]{:S(2)}, u32[]{:S(2)}) collective-permute-start(bf16[256,2048]{1,0:T(8,128)(2,1)} %slice.391), channel_id=1, source_target_pairs={{0,8},{8,0},{1,9},{9,1},{2,10},{10,2},{3,11},{11,3},{4,12},{12,4},... | collective-permute-start | bytes 3145736 | tf_op jit(solution)/shard_map/ppermute | solution.py:24
  421.8 20.1 %collective-permute-start.100 = (bf16[256]{0:T(256)(128)(2,1)S(1)}, bf16[256]{0:T(256)(128)(2,1)S(1)}, u32[]{:S(2)}, u32[]{:S(2)}) collective-permute-start(bf16[256]{0:T(256)(128)(2,1)S(1)} %add_convert_fusion.6), channel_id=1, source_target_pairs={{0,2},{2,4},{4,6},{1,3},{3,5},{5,7},{8,10},{10,12},{12,14},{9,11},... | collective-permute-start | bytes 1544 | tf_op jit(solution)/shard_map/ppermute | solution.py:244
  441.9 52.2 %collective-permute-start.36 = (bf16[256,2048]{1,0:T(8,128)(2,1)}, bf16[256,2048]{1,0:T(8,128)(2,1)}, u32[]{:S(2)}, u32[]{:S(2)}) collective-permute-start(bf16[256,2048]{1,0:T(8,128)(2,1)} %slice.390), channel_id=1, source_target_pairs={{0,8},{8,0},{1,9},{9,1},{2,10},{10,2},{3,11},{11,3},{4,12},{12,4},... | collective-permute-start | bytes 3145736 | tf_op jit(solution)/shard_map/ppermute | solution.py:24
  443.0 54.9 %collective-permute-start.92 = (bf16[4,2,64,1024]{3,2,1,0:T(8,128)(2,1)}, bf16[4,2,64,1024]{3,2,1,0:T(8,128)(2,1)}, u32[]{:S(2)}, u32[]{:S(2)}) collective-permute-start(bf16[4,2,64,1024]{3,2,1,0:T(8,128)(2,1)} %get-tuple-element.55), channel_id=1, source_target_pairs={{0,2},{1,3},{8,10},{9,11},{16,18},{17,19},{24,26},{25,27}} | collective-permute-start | bytes 3145736 | tf_op jit(solution)/shard_map/ppermute | solution.py:244
  452.7 41.0 %collective-permute-start.104 = (bf16[256,2048]{1,0:T(8,128)(2,1)S(1)}, bf16[256,2048]{1,0:T(8,128)(2,1)S(1)}, u32[]{:S(2)}, u32[]{:S(2)}) collective-permute-start(bf16[256,2048]{1,0:T(8,128)(2,1)S(1)} %get-tuple-element.51), channel_id=1, source_target_pairs={{0,2},{1,3},{8,10},{9,11},{16,18},{17,19},{24,26},{25,27}} | collective-permute-start | bytes 3145736 | tf_op jit(solution)/shard_map/ppermute | solution.py:244
  456.1 92.4 %collective-permute-start.95 = (bf16[4,2,64,1024]{3,2,1,0:T(8,128)(2,1)S(1)}, bf16[4,2,64,1024]{3,2,1,0:T(8,128)(2,1)S(1)}, u32[]{:S(2)}, u32[]{:S(2)}) collective-permute-start(bf16[4,2,64,1024]{3,2,1,0:T(8,128)(2,1)S(1)} %get-tuple-element.56), channel_id=1, source_target_pairs={{6,4},{7,5},{14,12},{15,13},{22,20},{23,21},{30,28},{31,29}} | collective-permute-start | bytes 3145736 | tf_op jit(solution)/shard_map/ppermute | solution.py:245
  494.0 48.8 %collective-permute-start.107 = (bf16[256,2048]{1,0:T(8,128)(2,1)S(1)}, bf16[256,2048]{1,0:T(8,128)(2,1)S(1)}, u32[]{:S(2)}, u32[]{:S(2)}) collective-permute-start(bf16[256,2048]{1,0:T(8,128)(2,1)S(1)} %get-tuple-element.52), channel_id=1, source_target_pairs={{6,4},{7,5},{14,12},{15,13},{22,20},{23,21},{30,28},{31,29}} | collective-permute-start | bytes 3145736 | tf_op jit(solution)/shard_map/ppermute | solution.py:245
  512.0 31.7 %collective-permute-start.105 = (bf16[256,2048]{1,0:T(8,128)(2,1)S(1)}, bf16[256,2048]{1,0:T(8,128)(2,1)S(1)}, u32[]{:S(2)}, u32[]{:S(2)}) collective-permute-start(bf16[256,2048]{1,0:T(8,128)(2,1)S(1)} %fusion.109), channel_id=1, source_target_pairs={{0,2},{2,4},{1,3},{3,5},{8,10},{10,12},{9,11},{11,13},{16,18},{18,... | collective-permute-start | bytes 3145736 | tf_op jit(solution)/shard_map/ppermute | solution.py:244
  537.2 24.8 %collective-permute-start.93 = (bf16[4,2,64,1024]{3,2,1,0:T(8,128)(2,1)S(1)}, bf16[4,2,64,1024]{3,2,1,0:T(8,128)(2,1)S(1)}, u32[]{:S(2)}, u32[]{:S(2)}) collective-permute-start(bf16[4,2,64,1024]{3,2,1,0:T(8,128)(2,1)S(1)} %fusion.114), channel_id=1, source_target_pairs={{0,2},{2,4},{1,3},{3,5},{8,10},{10,12},{9,11},{11,13},{16,18},{18,... | collective-permute-start | bytes 3145736 | tf_op jit(solution)/shard_map/ppermute | solution.py:244
  542.8 26.3 %collective-permute-start.58 = (bf16[256,2048]{1,0:T(8,128)(2,1)}, bf16[256,2048]{1,0:T(8,128)(2,1)S(1)}, u32[]{:S(2)}, u32[]{:S(2)}) collective-permute-start(bf16[256,2048]{1,0:T(8,128)(2,1)} %pad_maximum_fusion.8), channel_id=1, source_target_pairs={{0,16},{16,0},{1,17},{17,1},{2,18},{18,2},{3,19},{19,3},{4,20},{20... | collective-permute-start | bytes 3145736 | tf_op jit(solution)/shard_map/ppermute | solution.py:24
  543.7 26.3 %collective-permute-start.54 = (bf16[256,2048]{1,0:T(8,128)(2,1)}, bf16[256,2048]{1,0:T(8,128)(2,1)S(1)}, u32[]{:S(2)}, u32[]{:S(2)}) collective-permute-start(bf16[256,2048]{1,0:T(8,128)(2,1)} %pad_maximum_fusion.7), channel_id=1, source_target_pairs={{0,1},{1,0},{2,3},{3,2},{4,5},{5,4},{6,7},{7,6},{8,9},{9,8},{10,11... | collective-permute-start | bytes 3145736 | tf_op jit(solution)/shard_map/ppermute | solution.py:24
  548.4 24.7 %collective-permute-start.28 = (bf16[256,2048]{1,0:T(8,128)(2,1)S(1)}, bf16[256,2048]{1,0:T(8,128)(2,1)S(1)}, u32[]{:S(2)}, u32[]{:S(2)}) collective-permute-start(bf16[256,2048]{1,0:T(8,128)(2,1)S(1)} %copy-done.62), channel_id=1, source_target_pairs={{0,8},{8,0},{1,9},{9,1},{2,10},{10,2},{3,11},{11,3},{4,12},{12,4},... | collective-permute-start | bytes 3145736 | tf_op jit(solution)/shard_map/ppermute | solution.py:24
  548.5 40.2 %collective-permute-start.38 = (bf16[256,2048]{1,0:T(8,128)(2,1)S(1)}, bf16[256,2048]{1,0:T(8,128)(2,1)S(1)}, u32[]{:S(2)}, u32[]{:S(2)}) collective-permute-start(bf16[256,2048]{1,0:T(8,128)(2,1)S(1)} %pad_maximum_fusion.4), channel_id=1, source_target_pairs={{0,1},{1,0},{2,3},{3,2},{4,5},{5,4},{6,7},{7,6},{8,9},{9,8},{10,11... | collective-permute-start | bytes 3145736 | tf_op jit(solution)/shard_map/ppermute | solution.py:24
  562.0 26.7 %collective-permute-start.42 = (bf16[256,2048]{1,0:T(8,128)(2,1)}, bf16[256,2048]{1,0:T(8,128)(2,1)S(1)}, u32[]{:S(2)}, u32[]{:S(2)}) collective-permute-start(bf16[256,2048]{1,0:T(8,128)(2,1)} %pad_maximum_fusion.5), channel_id=1, source_target_pairs={{0,16},{16,0},{1,17},{17,1},{2,18},{18,2},{3,19},{19,3},{4,20},{20... | collective-permute-start | bytes 3145736 | tf_op jit(solution)/shard_map/ppermute | solution.py:24
  569.1 116.6 %collective-permute-start.79 = (bf16[256,2,512]{0,2,1:T(8,128)(2,1)}, bf16[256,2,512]{0,2,1:T(8,128)(2,1)}, u32[]{:S(2)}, u32[]{:S(2)}) collective-permute-start(bf16[256,2,512]{0,2,1:T(8,128)(2,1)} %get-tuple-element.79), channel_id=1, source_target_pairs={{0,8},{8,0},{1,9},{9,1},{2,10},{10,2},{3,11},{11,3},{4,12},{12,4},... | collective-permute-start | bytes 1572872 | tf_op jit(solution)/shard_map/ppermute | solution.py:24
  570.0 64.0 %collective-permute-start.108 = (bf16[256,2048]{1,0:T(8,128)(2,1)}, bf16[256,2048]{1,0:T(8,128)(2,1)}, u32[]{:S(2)}, u32[]{:S(2)}) collective-permute-start(bf16[256,2048]{1,0:T(8,128)(2,1)} %get-tuple-element.50), channel_id=1, source_target_pairs={{4,2},{6,4},{5,3},{7,5},{12,10},{14,12},{13,11},{15,13},{20,18},{2... | collective-permute-start | bytes 3145736 | tf_op jit(solution)/shard_map/ppermute | solution.py:245
  617.3 21.7 %collective-permute-start.96 = (bf16[4,2,64,1024]{3,2,1,0:T(8,128)(2,1)}, bf16[4,2,64,1024]{3,2,1,0:T(8,128)(2,1)S(1)}, u32[]{:S(2)}, u32[]{:S(2)}) collective-permute-start(bf16[4,2,64,1024]{3,2,1,0:T(8,128)(2,1)} %get-tuple-element.54), channel_id=1, source_target_pairs={{4,2},{6,4},{5,3},{7,5},{12,10},{14,12},{13,11},{15,13},{20,18},{2... | collective-permute-start | bytes 3145736 | tf_op jit(solution)/shard_map/ppermute | solution.py:245
  627.1 72.6 %collective-permute-start.94 = (bf16[4,2,64,1024]{3,2,1,0:T(8,128)(2,1)}, bf16[4,2,64,1024]{3,2,1,0:T(8,128)(2,1)}, u32[]{:S(2)}, u32[]{:S(2)}) collective-permute-start(bf16[4,2,64,1024]{3,2,1,0:T(8,128)(2,1)} %get-tuple-element.53), channel_id=1, source_target_pairs={{0,2},{2,4},{4,6},{1,3},{3,5},{5,7},{8,10},{10,12},{12,14},{9,11},... | collective-permute-start | bytes 3145736 | tf_op jit(solution)/shard_map/ppermute | solution.py:244
  633.0 57.6 %collective-permute-start.80 = (bf16[256,2048]{1,0:T(8,128)(2,1)}, bf16[256,2048]{1,0:T(8,128)(2,1)}, u32[]{:S(2)}, u32[]{:S(2)}) collective-permute-start(bf16[256,2048]{1,0:T(8,128)(2,1)} %copy-done.54), channel_id=1, source_target_pairs={{0,8},{8,0},{1,9},{9,1},{2,10},{10,2},{3,11},{11,3},{4,12},{12,4},... | collective-permute-start | bytes 3145736 | tf_op jit(solution)/shard_map/ppermute | solution.py:24
  638.9 27.1 %collective-permute-start.65 = (bf16[2,128,256]{2,1,0:T(8,128)(2,1)S(1)}, bf16[2,128,256]{2,1,0:T(8,128)(2,1)S(1)}, u32[]{:S(2)}, u32[]{:S(2)}) collective-permute-start(bf16[2,128,256]{2,1,0:T(8,128)(2,1)S(1)} %fusion.208), channel_id=1, source_target_pairs={{2,0},{4,2},{6,4},{3,1},{5,3},{7,5},{10,8},{12,10},{14,12},{11,9},... | collective-permute-start | bytes 393224 | tf_op jit(solution)/shard_map/ppermute | solution.py:442
  643.3 57.7 %collective-permute-start.97 = (bf16[4,2,64,1024]{3,2,1,0:T(8,128)(2,1)}, bf16[4,2,64,1024]{3,2,1,0:T(8,128)(2,1)}, u32[]{:S(2)}, u32[]{:S(2)}) collective-permute-start(bf16[4,2,64,1024]{3,2,1,0:T(8,128)(2,1)} %fusion.113), channel_id=1, source_target_pairs={{2,0},{4,2},{6,4},{3,1},{5,3},{7,5},{10,8},{12,10},{14,12},{11,9},... | collective-permute-start | bytes 3145736 | tf_op jit(solution)/shard_map/ppermute | solution.py:245
  685.5 24.4 %collective-permute-start.67 = (bf16[256,2304]{0,1:T(8,128)(2,1)}, bf16[256,2304]{0,1:T(8,128)(2,1)}, u32[]{:S(2)}, u32[]{:S(2)}) collective-permute-start(bf16[256,2304]{0,1:T(8,128)(2,1)} %pad_maximum_fusion.1), channel_id=1, source_target_pairs={{0,8},{8,0},{1,9},{9,1},{2,10},{10,2},{3,11},{11,3},{4,12},{12,4},... | collective-permute-start | bytes 3538952 | tf_op jit(solution)/shard_map/ppermute | solution.py:24
  685.7 46.7 %collective-permute-start.106 = (bf16[256,2048]{1,0:T(8,128)(2,1)}, bf16[256,2048]{1,0:T(8,128)(2,1)}, u32[]{:S(2)}, u32[]{:S(2)}) collective-permute-start(bf16[256,2048]{1,0:T(8,128)(2,1)} %get-tuple-element.49), channel_id=1, source_target_pairs={{0,2},{2,4},{4,6},{1,3},{3,5},{5,7},{8,10},{10,12},{12,14},{9,11},... | collective-permute-start | bytes 3145736 | tf_op jit(solution)/shard_map/ppermute | solution.py:244
  696.6 26.3 %collective-permute-start.81 = (bf16[4,2,64,1024]{3,2,0,1:T(8,128)(2,1)}, bf16[4,2,64,1024]{3,2,0,1:T(8,128)(2,1)}, u32[]{:S(2)}, u32[]{:S(2)}) collective-permute-start(bf16[4,2,64,1024]{3,2,0,1:T(8,128)(2,1)} %fusion.135), channel_id=1, source_target_pairs={{0,16},{16,0},{1,17},{17,1},{2,18},{18,2},{3,19},{19,3},{4,20},{20... | collective-permute-start | bytes 3145736 | tf_op jit(solution)/shard_map/ppermute | solution.py:24
  699.8 32.7 %collective-permute-start.109 = (bf16[256,2048]{1,0:T(8,128)(2,1)}, bf16[256,2048]{1,0:T(8,128)(2,1)}, u32[]{:S(2)}, u32[]{:S(2)}) collective-permute-start(bf16[256,2048]{1,0:T(8,128)(2,1)} %fusion.108), channel_id=1, source_target_pairs={{2,0},{4,2},{6,4},{3,1},{5,3},{7,5},{10,8},{12,10},{14,12},{11,9},... | collective-permute-start | bytes 3145736 | tf_op jit(solution)/shard_map/ppermute | solution.py:245
  701.1 29.2 %collective-permute-start.84 = (bf16[2,4,64,1152]{3,2,1,0:T(8,128)(2,1)}, bf16[2,4,64,1152]{3,2,1,0:T(8,128)(2,1)}, u32[]{:S(2)}, u32[]{:S(2)}) collective-permute-start(bf16[2,4,64,1152]{3,2,1,0:T(8,128)(2,1)} %fusion.130), channel_id=1, source_target_pairs={{0,1},{1,0},{2,3},{3,2},{4,5},{5,4},{6,7},{7,6},{8,9},{9,8},{10,11... | collective-permute-start | bytes 3538952 | tf_op jit(solution)/shard_map/ppermute | solution.py:24
  705.3 34.3 %all-to-all-start = ((bf16[8,64,1024]{2,1,0:T(8,128)(2,1)}), bf16[8,64,1024]{2,1,0:T(8,128)(2,1)}, u32[]{:S(2)}, u32[]{:S(2)}) async-start(bf16[8,64,1024]{2,1,0:T(8,128)(2,1)} %bitcast.428), calls=%async_computation | async-start | bytes 2097152 | tf_op jit(solution)/shard_map/all_to_all | solution.py:407
  715.8 56.7 %collective-permute-start.68 = (bf16[4,2,64,1152]{3,2,0,1:T(8,128)(2,1)}, bf16[4,2,64,1152]{3,2,0,1:T(8,128)(2,1)}, u32[]{:S(2)}, u32[]{:S(2)}) collective-permute-start(bf16[4,2,64,1152]{3,2,0,1:T(8,128)(2,1)} %fusion.129), channel_id=1, source_target_pairs={{0,16},{16,0},{1,17},{17,1},{2,18},{18,2},{3,19},{19,3},{4,20},{20... | collective-permute-start | bytes 3538952 | tf_op jit(solution)/shard_map/ppermute | solution.py:24
  725.5 27.3 %collective-permute-start.82 = (bf16[4,64,1024]{2,1,0:T(8,128)(2,1)}, bf16[4,64,1024]{2,1,0:T(8,128)(2,1)}, u32[]{:S(2)}, u32[]{:S(2)}) collective-permute-start(bf16[4,64,1024]{2,1,0:T(8,128)(2,1)} %fusion.199), channel_id=1, source_target_pairs={{0,1},{1,0},{2,3},{3,2},{4,5},{5,4},{6,7},{7,6},{8,9},{9,8},{10,11... | collective-permute-start | bytes 1572872 | tf_op jit(solution)/shard_map/ppermute | solution.py:24
  732.0 39.2 %collective-permute-start.85 = (bf16[4,64,1152]{2,1,0:T(8,128)(2,1)S(1)}, bf16[4,64,1152]{2,1,0:T(8,128)(2,1)}, u32[]{:S(2)}, u32[]{:S(2)}) collective-permute-start(bf16[4,64,1152]{2,1,0:T(8,128)(2,1)S(1)} %fusion.174), channel_id=1, source_target_pairs={{0,16},{16,0},{1,17},{17,1},{2,18},{18,2},{3,19},{19,3},{4,20},{20... | collective-permute-start | bytes 1769480 | tf_op jit(solution)/shard_map/ppermute | solution.py:24
  738.0 42.9 %collective-permute-start.71 = (bf16[2,4,64,1280]{3,2,1,0:T(8,128)(2,1)}, bf16[2,4,64,1280]{3,2,1,0:T(8,128)(2,1)}, u32[]{:S(2)}, u32[]{:S(2)}) collective-permute-start(bf16[2,4,64,1280]{3,2,1,0:T(8,128)(2,1)} %fusion.128), channel_id=1, source_target_pairs={{0,1},{1,0},{2,3},{3,2},{4,5},{5,4},{6,7},{7,6},{8,9},{9,8},{10,11... | collective-permute-start | bytes 3932168 | tf_op jit(solution)/shard_map/ppermute | solution.py:24
  775.1 17.4 %collective-permute-start.69 = (bf16[4,64,1152]{2,1,0:T(8,128)(2,1)S(1)}, bf16[4,64,1152]{2,1,0:T(8,128)(2,1)S(1)}, u32[]{:S(2)}, u32[]{:S(2)}) collective-permute-start(bf16[4,64,1152]{2,1,0:T(8,128)(2,1)S(1)} %fusion.173), channel_id=1, source_target_pairs={{0,1},{1,0},{2,3},{3,2},{4,5},{5,4},{6,7},{7,6},{8,9},{9,8},{10,11... | collective-permute-start | bytes 1769480 | tf_op jit(solution)/shard_map/ppermute | solution.py:24
  783.2 19.3 %collective-permute-start.86 = (bf16[64,2176]{1,0:T(8,128)(2,1)S(1)}, bf16[64,2176]{1,0:T(8,128)(2,1)S(1)}, u32[]{:S(2)}, u32[]{:S(2)}) collective-permute-start(bf16[64,2176]{1,0:T(8,128)(2,1)S(1)} %get-tuple-element.71), channel_id=1, source_target_pairs={{0,2},{1,3},{8,10},{9,11},{16,18},{17,19},{24,26},{25,27}} | collective-permute-start | bytes 835592 | tf_op jit(solution)/shard_map/ppermute | solution.py:244
  (163 other events, 2109.3 us)

commit v2 on v1

--- a/solution.py
+++ b/solution.py
@@ -275,6 +275,297 @@
     side_a = pick(side_a, x, 1) + swap(pick(side_a, 1 - x, 1).astype(BF), "x").astype(F32)
     side_b = pick(side_b, y, 0) + swap(pick(side_b, 1 - y, 0).astype(BF), "y").astype(F32)
     return scatter_line(jnp.concatenate([side_a, side_b], axis=-1), z, length)
+
+
+MESH = pl.DeviceIdType.MESH
+
+
+def remote(src, dst, send_sems, recv_sems, index, device):
+    return pltpu.make_async_remote_copy(
+        src_ref=src,
+        dst_ref=dst,
+        send_sem=send_sems.at[index],
+        recv_sem=recv_sems.at[index],
+        device_id=device,
+        device_id_type=MESH,
+    )
+
+
+def greet(devices):
+    barrier = pltpu.get_barrier_semaphore()
+    for device in devices:
+        pl.semaphore_signal(barrier, inc=1, device_id=device, device_id_type=MESH)
+    pl.semaphore_wait(barrier, len(devices))
+
+
+def tiles(count, size):
+    def over(fn):
+        @pl.loop(0, count)
+        def step(index):
+            fn(pl.ds(pl.multiple_of(index * size, size), size), index)
+
+    return over
+
+
+def gelu_pair(upper):
+    inner = jnp.tanh(upper * (GELU_K + (GELU_K * GELU_C) * (upper * upper)))
+    half = 0.5 + 0.5 * inner
+    slope = half + (0.5 * upper) * (1.0 - inner * inner) * (
+        GELU_K + (3.0 * GELU_K * GELU_C) * (upper * upper)
+    )
+    return upper * half, slope
+
+
+def ffn_kernel(
+    second_ref,
+    down_all_ref,
+    up_ref,
+    ubias_ref,
+    down_ref,
+    dsecond_ref,
+    out_parts_ref,
+    down_part_ref,
+    up_part_ref,
+    ubias_part_ref,
+    tokens_v,
+    cots_v,
+    up_v,
+    down_v,
+    active_v,
+    dupper_v,
+    sib_out,
+    sib_in,
+    chip_out,
+    chip_in,
+    acc_v,
+    stage_v,
+    load_sem,
+    stage_sem,
+    gs_send,
+    gs_recv,
+    rs_send,
+    rs_recv,
+    *,
+    length,
+):
+    rows, width = second_ref.shape
+    hidden = up_ref.shape[1]
+    half = rows // 2
+    chunk = 2 * rows
+    y, c, x = [lax.axis_index(name) for name in ("y", "c", "x")]
+    sib, to_x, to_y = {"c": 1 - c}, {"x": 1 - x}, {"y": 1 - y}
+    diag = {"x": 1 - x, "y": 1 - y}
+    chips = (None, to_x, to_y, diag)
+
+    loads = [
+        pltpu.make_async_copy(second_ref, tokens_v.at[0, pl.ds(0, rows)], load_sem.at[0]),
+        pltpu.make_async_copy(down_ref, down_v, load_sem.at[1]),
+        pltpu.make_async_copy(down_all_ref, cots_v, load_sem.at[2]),
+        pltpu.make_async_copy(up_ref, up_v, load_sem.at[3]),
+    ]
+    for load in loads:
+        load.start()
+    greet((sib, to_x, to_y, diag))
+    loads[0].wait()
+
+    same, other = pl.ds(0, rows), pl.ds(rows, rows)
+    top, bottom = pl.ds(0, half), pl.ds(half, half)
+
+    def gather(index, chip, span_src, chip_dst, span_dst, device):
+        return remote(
+            tokens_v.at[chip, span_src], tokens_v.at[chip_dst, span_dst], gs_send, gs_recv, index, device
+        )
+
+    send_x = gather(0, 0, same, 1, same, to_x)
+    send_y = gather(1, 0, same, 2, same, to_y)
+    share = [gather(2 + k, k, same, k, other, sib) for k in range(4)]
+    diag_x = gather(6, 2, top, 3, top, to_x)
+    diag_y = gather(7, 1, bottom, 3, bottom, to_y)
+    send_x.start()
+    send_y.start()
+    share[0].start()
+
+    loads[1].wait()
+    loads[2].wait()
+
+    @tiles(4 * chunk // 512, 512)
+    def grad_active(span, index):
+        @tiles(hidden // 512, 512)
+        def columns(cols, _):
+            dupper_v[span, cols] = dot(cots_v[span, :], down_v[cols, :], ((1,), (1,))).astype(BF)
+
+    loads[3].wait()
+
+    def chip_work(k):
+        @tiles(hidden // 256, 256)
+        def columns(cols, _):
+            block = pl.ds(k * chunk, chunk)
+            upper = dot(tokens_v[k], up_v[:, cols]) + ubias_ref[:, cols]
+            active, slope = gelu_pair(upper)
+            active_v[block, cols] = active.astype(BF)
+            d_upper = (dupper_v[block, cols].astype(F32) * slope).astype(BF)
+            dupper_v[block, cols] = d_upper
+            part = jnp.sum(d_upper.astype(F32), axis=0, keepdims=True)
+            if k == 0:
+                ubias_part_ref[:, cols] = part
+            else:
+                ubias_part_ref[:, cols] += part
+
+        @tiles(width // 512, 512)
+        def to_sibling(cols, _):
+            sib_out[k, :, cols] = dot(
+                dupper_v[pl.ds(k * chunk + rows, rows), :], up_v[cols, :], ((1,), (1,))
+            ).astype(BF)
+
+        pair = remote(sib_out.at[k], sib_in.at[k], rs_send, rs_recv, k, sib)
+        pair.start()
+
+        @tiles(width // 512, 512)
+        def keep(cols, _):
+            acc_v[:, cols] = dot(dupper_v[pl.ds(k * chunk, rows), :], up_v[cols, :], ((1,), (1,)))
+
+        pair.wait_recv()
+        if k == 0:
+            dsecond_ref[...] = acc_v[...] + sib_in[0].astype(F32)
+            return [pair]
+        chip_out[k - 1] = (acc_v[...] + sib_in[k].astype(F32)).astype(BF)
+        far = remote(chip_out.at[k - 1], chip_in.at[k - 1], rs_send, rs_recv, 3 + k, chips[k])
+        far.start()
+        return [pair, far]
+
+    share[0].wait_recv()
+    sent = chip_work(0)
+    send_x.wait_recv()
+    share[1].start()
+    diag_y.start()
+    send_y.wait_recv()
+    share[2].start()
+    diag_x.start()
+    share[1].wait_recv()
+    sent += chip_work(1)
+    share[2].wait_recv()
+    sent += chip_work(2)
+    diag_x.wait_recv()
+    diag_y.wait_recv()
+    share[3].start()
+    share[3].wait_recv()
+    sent += chip_work(3)
+
+    def staged(slot, value, target):
+        stage_v[slot] = value.astype(BF)
+        copy = pltpu.make_async_copy(stage_v.at[slot], target, stage_sem.at[slot])
+        copy.start()
+        return copy
+
+    @pl.loop(0, 4)
+    def outputs(k):
+        block = pl.ds(pl.multiple_of(k * chunk, chunk), chunk)
+        copies = []
+        for j in range(width // 512):
+            cols = pl.ds(j * 512, 512)
+            copies.append(
+                staged(j, dot(active_v[block, :], down_v[:, cols]), out_parts_ref.at[k, :, cols])
+            )
+        for copy in copies:
+            copy.wait()
+
+    @pl.loop(0, hidden // 512)
+    def downs(r):
+        block = pl.ds(pl.multiple_of(r * 512, 512), 512)
+        copies = []
+        for j in range(width // 512):
+            cols = pl.ds(j * 512, 512)
+            copies.append(
+                staged(
+                    j,
+                    dot(active_v[:, block], cots_v[:, cols], ((0,), (0,))),
+                    down_part_ref.at[block, cols],
+                )
+            )
+        for copy in copies:
+            copy.wait()
+
+    quarter = width // 4
+    piece = quarter // length
+
+    @pl.loop(0, hidden // 512)
+    def ups(r):
+        cols = pl.ds(pl.multiple_of(r * 512, 512), 512)
+        copies = []
+        for f in range(4):
+            value = None
+            for k in range(4):
+                term = dot(
+                    tokens_v[k, :, f * quarter : (f + 1) * quarter],
+                    dupper_v[k * chunk : (k + 1) * chunk, cols],
+                    ((0,), (0,)),
+                )
+                value = term if value is None else value + term
+            stage_v[f] = value.astype(BF)
+            for level in range(length):
+                copy = pltpu.make_async_copy(
+                    stage_v.at[f, pl.ds(level * piece, piece)],
+                    up_part_ref.at[level, f, :, cols],
+                    stage_sem.at[4 + f * length + level],
+                )
+                copy.start()
+                copies.append(copy)
+        for copy in copies:
+            copy.wait()
+
+    for k in range(3):
+        remote(chip_out.at[k], chip_in.at[k], rs_send, rs_recv, 4 + k, chips[k + 1]).wait_recv()
+    dsecond_ref[...] += (
+        chip_in[0].astype(F32) + chip_in[1].astype(F32) + chip_in[2].astype(F32)
+    )
+    for copy in [send_x, send_y, diag_x, diag_y] + share + sent:
+        copy.wait_send()
+
+
+def ffn(second, down_all, up_mine, ubias, down_mine, length):
+    rows, width = second.shape
+    hidden = up_mine.shape[1]
+    hbm = pl.BlockSpec(memory_space=pltpu.HBM)
+    vmem = pl.BlockSpec(memory_space=pltpu.VMEM)
+    sems = pltpu.SemaphoreType.DMA
+    return pl.pallas_call(
+        functools.partial(ffn_kernel, length=length),
+        in_specs=[hbm, hbm, hbm, vmem, hbm],
+        out_specs=[vmem, hbm, hbm, hbm, vmem],
+        out_shape=[
+            jax.ShapeDtypeStruct((rows, width), F32),
+            jax.ShapeDtypeStruct((4, 2 * rows, width), BF),
+            jax.ShapeDtypeStruct((hidden, width), BF),
+            jax.ShapeDtypeStruct((length, 4, width // 4 // length, hidden), BF),
+            jax.ShapeDtypeStruct((1, hidden), F32),
+        ],
+        scratch_shapes=[
+            pltpu.VMEM((4, 2 * rows, width), BF),
+            pltpu.VMEM((8 * rows, width), BF),
+            pltpu.VMEM((width, hidden), BF),
+            pltpu.VMEM((hidden, width), BF),
+            pltpu.VMEM((8 * rows, hidden), BF),
+            pltpu.VMEM((8 * rows, hidden), BF),
+            pltpu.VMEM((4, rows, width), BF),
+            pltpu.VMEM((4, rows, width), BF),
+            pltpu.VMEM((3, rows, width), BF),
+            pltpu.VMEM((3, rows, width), BF),
+            pltpu.VMEM((rows, width), F32),
+            pltpu.VMEM((4, 512, 512), BF),
+            sems((4,)),
+            sems((4 + 4 * length,)),
+            sems((8,)),
+            sems((8,)),
+            sems((7,)),
+            sems((7,)),
+        ],
+        compiler_params=pltpu.CompilerParams(
+            collective_id=1, has_side_effects=True, vmem_limit_bytes=60 << 20
+        ),
+        cost_estimate=pl.CostEstimate(
+            flops=12 * 8 * rows * width * hidden, bytes_accessed=40 << 20, transcendentals=0
+        ),
+    )(second, down_all, up_mine, ubias, down_mine)
 
 
 def body(
@@ -373,37 +664,20 @@
     d_down = d_out.astype(BF)
 
     down_all = gather_plane(d_down)
-    second_all = gather_plane(second)
-    out_parts, dsecond_parts, actives, d_uppers = [], [], [], []
-    for chip in range(4):
-        d_active = dot(down_all[chip], down_mine, ((1,), (1,)))
-        upper = dot(second_all[chip], up_mine) + up_bias_mine.astype(F32)
-        inner = jnp.tanh(GELU_K * (upper + GELU_C * upper * upper * upper))
-        active = (0.5 * upper * (1.0 + inner)).astype(BF)
-        slope = 0.5 * (1.0 + inner) + 0.5 * upper * (1.0 - inner * inner) * GELU_K * (
-            1.0 + 3.0 * GELU_C * upper * upper
-        )
-        d_upper = (d_active * slope).astype(BF)
-        actives.append(active)
-        d_uppers.append(d_upper)
-        dsecond_parts.append(dot(d_upper, up_mine, ((1,), (1,))))
-        out_parts.append(dot(active, down_mine))
-    d_second = scatter_plane(dsecond_parts)
-    output = residual + scatter_plane(out_parts) + d_bias
+    d_second, out_parts, down_part, up_part, ubias_part = ffn(
+        second,
+        jnp.concatenate(down_all, axis=0),
+        up_mine,
+        up_bias_mine.astype(F32),
+        down_mine,
+        length,
+    )
+    output = residual + scatter_plane([out_parts[i] for i in range(4)]) + d_bias
     layer_out = output.astype(BF).reshape(tokens.shape)
-    active_cat = jnp.concatenate(actives, axis=0)
-    d_upper_cat = jnp.concatenate(d_uppers, axis=0)
-    down_cat = jnp.concatenate(down_all, axis=0)
-    second_cat = jnp.concatenate(second_all, axis=0)
-    down_part = dot(active_cat, down_cat, ((0,), (0,)))
     down_grad = scatter_line(down_part.reshape(length, hidden_block, width), z, length)
-    ubias_part = jnp.sum(d_upper_cat.astype(F32), axis=0).reshape(length, hidden_block)
-    ubias_grad = scatter_line(ubias_part, z, length)
-    up_part = dot(second_cat, d_upper_cat, ((0,), (0,)))
+    ubias_grad = scatter_line(ubias_part.reshape(length, hidden_block), z, length)
     out_rows = width // (8 * length)
-    up_part = up_part.reshape(4, length, 2, out_rows, hidden_mine).transpose(1, 0, 2, 3, 4)
     up_sum = scatter_line(up_part, z, length).astype(BF)
-    up_sum = up_sum.reshape(2, 2, 2, out_rows, hidden_mine)
     up_rows = lax.all_to_all(
         up_sum.reshape(8, out_rows, hidden_mine), ("y", "c", "x"), 0, 0, tiled=True
     )

time: 850 us -> 802 us (0.944)
  waiting for transfers between devices: 320 us -> 217 us
  Pallas kernels: 13.3 us -> 108 us
  matrix products: 121 us -> 37.2 us
  local copies, waits for them, and re-layouts: 156 us -> 195 us
  starting transfers between devices: 154 us -> 164 us
    ppermute x71 -> x55, waiting for transfers between devices: 217 us -> 121 us  [swap(): return lax.ppermute(values, axis, [(0, 1), (1, 0)])]
    pallas_call x0 -> x1, Pallas kernels: none -> 95.5 us  [ffn(): pl.pallas_call(functools.partial(ffn_kernel, length=length), in_specs=[hb...]
    dot_general x26 -> x8, matrix products: 121 us -> 37.2 us  [dot(): lax.dot_general(left_side, right_side, (dims, ((), ())), preferred_elemen...]
    dynamic_slice x15 -> x12, local copies, waits for them, and re-layouts: 25.9 us -> 58.3 us  [pick(): return lax.dynamic_index_in_dim(values, index, axis, keepdims=False)]
    reshape x1 -> x3, local copies, waits for them, and re-layouts: 0.01 us -> 21.7 us  [the longest x1 14.5 us: body(): up_weight.reshape(quarter, 4, length, 2, hidden_block)]
    ppermute x15, starting transfers between devices: 69.1 us -> 85 us  [scatter_line(): lax.ppermute(up.astype(BF), 'z', [(i, i + 1) for i in range(step)])]
    unnamed x249 -> x150, local copies, waits for them, and re-layouts: 37.1 us -> 23.7 us
    ppermute x3, waiting for transfers between devices: 25 us -> 15.5 us  [body(): lax.ppermute(running.astype(BF), 'z', [(i, i - 1) for i in range(1, lengt...]
  transfers between devices with their start and end apart: 111 -> 95, of which waited for: 39 -> 34; matrix products, arithmetic and copies ran while one was open for 39% -> 34% of each run, Pallas kernels for 2% -> 2%
where the time goes in v2:
time: 802 us; the launch traced here: 791 us
  waiting for transfers between devices  217 us (27%)
  local copies, waits for them, and re-layouts  195 us (24%)
  starting transfers between devices  164 us (20%)
  Pallas kernels  108 us (13%)
  other arithmetic  65.6 us (8%)
  matrix products  37.2 us (5%)
    ppermute x55, waiting for transfers between devices, swap(): return lax.ppermute(values, axis, [(0, 1), (1, 0)])  121 us
    pallas_call x1, Pallas kernels, ffn(): pl.pallas_call(functools.partial(ffn_kernel, length=length), in_specs=[hb...  95.5 us
    ppermute x15, starting transfers between devices, scatter_line(): lax.ppermute(up.astype(BF), 'z', [(i, i + 1) for i in range(step)])  85 us
    dynamic_slice x12, local copies, waits for them, and re-layouts, pick(): return lax.dynamic_index_in_dim(values, index, axis, keepdims=False)  58.3 us
    ppermute x15, waiting for transfers between devices, scatter_line(): lax.ppermute(up.astype(BF), 'z', [(i, i + 1) for i in range(step)])  50.3 us
    ppermute x55, starting transfers between devices, swap(): return lax.ppermute(values, axis, [(0, 1), (1, 0)])  42 us
    dot_general x8, matrix products, dot(): lax.dot_general(left_side, right_side, (dims, ((), ())), preferred_elemen...  37.2 us
    dynamic_update_slice x18, local copies, waits for them, and re-layouts, gather_rows(): full = lax.dynamic_update_slice_in_dim(full, piece, start, 0)  24.7 us
  transfers between devices with their start and end apart: 95, of which 34 were waited for; matrix products, arithmetic and copies ran while one was open for 34% of the time, Pallas kernels for 2%

profile of v2, /device:TPU:0, one launch (start us, length us, event | category | flops | bytes accessed | tf_op | source)
XLA Modules:
  0.0 790.6 jit_solution(6329151877366112942)
XLA Ops:
  11.2 14.5 %reshape.358 = bf16[512,4,4,2,256]{4,3,2,1,0:T(2,128)(2,1)} reshape(bf16[512,8192]{1,0:T(8,128)(2,1)} %param.30) | data formatting | bytes 16777216 | tf_op jit(solution)/shard_map/reshape | solution.py:631
  25.7 29.7 %dynamic-slice_reduce_fusion = bf16[512,4,4,256]{3,2,1,0:T(4,128)(2,1)} fusion(bf16[512,4,4,2,256]{4,3,2,1,0:T(2,128)(2,1)} %reshape.358, s32[]{:T(128)S(6)} %select_n.209), kind=kLoop, calls=%fused_computation | loop fusion | bytes 8388612 | tf_op jit(solution)/shard_map/jit(dynamic_index_in_dim)/dynamic_slice | solution.py:28
  55.4 7.2 reshape.399
  62.6 4.7 constant_dynamic-slice_fusion.16
  67.3 4.4 broadcast.112.clone
  71.7 3.2 constant_dynamic-update-slice_fusion.20
  74.8 4.3 broadcast.112.clone.1
  79.1 3.1 constant_dynamic-update-slice_fusion.8
  82.3 15.3 %constant_dynamic-slice_fusion.18 = (bf16[512,1,1024]{2,1,0:T(2,128)(2,1)}, bf16[512,1,1024]{2,1,0:T(2,128)(2,1)S(1)}, bf16[512,1,1024]{2,1,0:T(2,128)(2,1)}, bf16[512,1,1024]{2,1,0:T(2,128)(2,1)}) fusion(bf16[512,4,1024]{2,1,0:T(4,128)(2,1)} %reshape.399, s32[]{:T(128)S(6)} %select_n.214, s32[]{:T(128)S(6)} %select_n.212, s32[]{:T(128)S(6)} %select_n.211, ...), kind=kLoop, calls=%fused_computation.294 | loop fusion | bytes 8388624 | tf_op jit(solution)/shard_map/jit(dynamic_index_in_dim)/dynamic_slice | solution.py:28
  106.5 3.4 add_convert_fusion
  116.1 5.5 collective-permute-done.9
  129.7 3.5 collective-permute-start.13
  140.0 3.5 collective-permute-start.15
  158.0 4.1 collective-permute-start.17
  184.3 17.5 %collective-permute-done.1 = bf16[256,2048]{1,0:T(8,128)(2,1)S(1)} collective-permute-done((bf16[256,2048]{1,0:T(8,128)(2,1)}, bf16[256,2048]{1,0:T(8,128)(2,1)S(1)}, u32[]{:S(2)}, u32[]{:S(2)}) %collective-permute-start.1) | collective-permute-done | bytes 1048608 | tf_op jit(solution)/shard_map/ppermute | solution.py:24
  202.6 20.0 %collective-permute-done.34 = bf16[512,1024]{1,0:T(8,128)(2,1)S(1)} collective-permute-done((bf16[512,1024]{1,0:T(8,128)(2,1)S(1)}, bf16[512,1024]{1,0:T(8,128)(2,1)S(1)}, u32[]{:S(2)}, u32[]{:S(2)}) %collective-permute-start.34) | collective-permute-done | bytes 1048608 | tf_op jit(solution)/shard_map/ppermute | solution.py:638
  229.4 7.5 collective-permute-done.29
  238.2 18.8 %collective-permute-done.30 = bf16[128,2048]{1,0:T(8,128)(2,1)S(1)} collective-permute-done((bf16[128,2048]{1,0:T(8,128)(2,1)S(1)}, bf16[128,2048]{1,0:T(8,128)(2,1)S(1)}, u32[]{:S(2)}, u32[]{:S(2)}) %collective-permute-start.30) | collective-permute-done | bytes 524320 | tf_op jit(solution)/shard_map/ppermute | solution.py:24
  269.3 15.7 %collective-permute-done.21 = bf16[256,2048]{1,0:T(8,128)(2,1)S(1)} collective-permute-done((bf16[256,2048]{1,0:T(8,128)(2,1)S(1)}, bf16[256,2048]{1,0:T(8,128)(2,1)S(1)}, u32[]{:S(2)}, u32[]{:S(2)}) %collective-permute-start.21) | collective-permute-done | bytes 1048608 | tf_op jit(solution)/shard_map/ppermute | solution.py:24
  293.7 6.0 fusion.7.q_ref
  299.7 5.1 shard_map.288
  306.8 5.8 fusion.137
  314.4 95.5 %shard_map.289 = (f32[256,2048]{1,0:T(8,128)}, bf16[4,512,2048]{2,1,0:T(8,128)(2,1)}, bf16[1024,2048]{1,0:T(8,128)(2,1)}, bf16[4,4,128,1024]{3,2,1,0:T(8,128)(2,1)}, f32[1,1024]{1,0:T(1,128)}) custom-call(bf16[256,2048]{1,0:T(8,128)(2,1)} %add_convert_fusion.2.second_ref, bf16[2048,2048]{1,0:T(8,128)(2,1)} %constant_dynamic-update-slice_fusion.21.down_all_ref, ...), custom_call_target="tpu_custom_call" | custom-call | flops 51539607552 | bytes 41943040 | tf_op jit(solution)/shard_map/pallas_call | solution.py:531
  413.0 7.5 collective-permute-start.88
  425.0 3.7 slice_bitcast_fusion.3
  431.3 11.3 %collective-permute-done.82 = bf16[256]{0:T(256)(128)(2,1)S(1)} collective-permute-done((bf16[256]{0:T(256)(128)(2,1)S(1)}, bf16[256]{0:T(256)(128)(2,1)S(1)}, u32[]{:S(2)}, u32[]{:S(2)}) %collective-permute-start.82) | collective-permute-done | bytes 544 | tf_op jit(solution)/shard_map/ppermute | solution.py:244
  443.2 4.4 collective-permute-start.83
  450.3 8.9 %collective-permute-start.76 = (bf16[4,128,1024]{2,1,0:T(8,128)(2,1)S(1)}, bf16[4,128,1024]{2,1,0:T(8,128)(2,1)S(1)}, u32[]{:S(2)}, u32[]{:S(2)}) collective-permute-start(bf16[4,128,1024]{2,1,0:T(8,128)(2,1)S(1)} %get-tuple-element.69), channel_id=1, source_target_pairs={{0,2},{1,3},{8,10},{9,11},{16,18},{17,19},{24,26},{25,27}} | collective-permute-start | bytes 3145736 | tf_op jit(solution)/shard_map/ppermute | solution.py:244
  469.1 9.6 %collective-permute-done.76 = bf16[4,128,1024]{2,1,0:T(8,128)(2,1)S(1)} collective-permute-done((bf16[4,128,1024]{2,1,0:T(8,128)(2,1)S(1)}, bf16[4,128,1024]{2,1,0:T(8,128)(2,1)S(1)}, u32[]{:S(2)}, u32[]{:S(2)}) %collective-permute-start.76) | collective-permute-done | bytes 1048608 | tf_op jit(solution)/shard_map/ppermute | solution.py:244
  480.3 4.5 collective-permute-start.77
  484.9 3.8 collective-permute-done.41
  488.6 4.4 collective-permute-start.89
  494.9 4.0 collective-permute-done.87
  499.9 8.3 %collective-permute-done.77 = bf16[4,128,1024]{2,1,0:T(8,128)(2,1)S(1)} collective-permute-done((bf16[4,128,1024]{2,1,0:T(8,128)(2,1)S(1)}, bf16[4,128,1024]{2,1,0:T(8,128)(2,1)S(1)}, u32[]{:S(2)}, u32[]{:S(2)}) %collective-permute-start.77) | collective-permute-done | bytes 1048608 | tf_op jit(solution)/shard_map/ppermute | solution.py:244
  512.2 13.2 %collective-permute-done.89 = bf16[256,2048]{1,0:T(8,128)(2,1)S(1)} collective-permute-done((bf16[256,2048]{1,0:T(8,128)(2,1)S(1)}, bf16[256,2048]{1,0:T(8,128)(2,1)S(1)}, u32[]{:S(2)}, u32[]{:S(2)}) %collective-permute-start.89) | collective-permute-done | bytes 1048608 | tf_op jit(solution)/shard_map/ppermute | solution.py:244
  529.4 3.3 convert_reduce_fusion
  534.7 6.1 convolution_convert_fusion.dout_ref
  540.8 7.8 shard_map.290
  562.9 7.2 collective-permute-done.47
  574.7 8.2 %collective-permute-done.48 = bf16[2,128,256]{2,1,0:T(8,128)(2,1)} collective-permute-done((bf16[2,128,256]{2,1,0:T(8,128)(2,1)}, bf16[2,128,256]{2,1,0:T(8,128)(2,1)}, u32[]{:S(2)}, u32[]{:S(2)}) %collective-permute-start.48) | collective-permute-done | bytes 131104 | tf_op jit(solution)/shard_map/ppermute | solution.py:716
  587.9 8.0 %collective-permute-start.78 = (bf16[4,128,1024]{2,1,0:T(8,128)(2,1)}, bf16[4,128,1024]{2,1,0:T(8,128)(2,1)}, u32[]{:S(2)}, u32[]{:S(2)}) collective-permute-start(bf16[4,128,1024]{2,1,0:T(8,128)(2,1)} %get-tuple-element.67), channel_id=1, source_target_pairs={{0,2},{2,4},{4,6},{1,3},{3,5},{5,7},{8,10},{10,12},{12,14},{9,11},... | collective-permute-start | bytes 3145736 | tf_op jit(solution)/shard_map/ppermute | solution.py:244
  602.3 7.7 multiply_reduce_fusion.2
  613.7 3.4 add_convert_fusion.1
  621.7 20.7 %collective-permute-start.90 = (bf16[256,2048]{1,0:T(8,128)(2,1)}, bf16[256,2048]{1,0:T(8,128)(2,1)}, u32[]{:S(2)}, u32[]{:S(2)}) collective-permute-start(bf16[256,2048]{1,0:T(8,128)(2,1)} %get-tuple-element.63), channel_id=1, source_target_pairs={{0,2},{2,4},{4,6},{1,3},{3,5},{5,7},{8,10},{10,12},{12,14},{9,11},... | collective-permute-start | bytes 3145736 | tf_op jit(solution)/shard_map/ppermute | solution.py:244
  642.3 3.7 fusion.21
  653.9 3.5 fusion.36
  657.4 4.6 all-to-all-start
  662.1 4.2 fusion.14
  669.9 4.7 collective-permute-done.65
  678.7 3.3 collective-permute-done.68
  685.6 3.7 fusion.30
  697.2 4.0 reshape.392
  701.2 3.2 collective-permute-done.66
  705.6 17.4 %collective-permute-done.69 = bf16[4,64,1152]{2,1,0:T(8,128)(2,1)} collective-permute-done((bf16[4,64,1152]{2,1,0:T(8,128)(2,1)}, bf16[4,64,1152]{2,1,0:T(8,128)(2,1)}, u32[]{:S(2)}, u32[]{:S(2)}) %collective-permute-start.69) | collective-permute-done | bytes 589856 | tf_op jit(solution)/shard_map/ppermute | solution.py:24
  728.5 4.0 collective-permute-done.55
  734.0 4.6 collective-permute-start.70
  739.3 5.1 collective-permute-done.53
  744.5 3.8 collective-permute-done.56
  748.5 3.9 collective-permute-start.57
  755.2 4.9 collective-permute-done.57
  760.3 4.4 collective-permute-start.58
  766.3 4.4 collective-permute-start.72
  772.9 5.4 collective-permute-start.59
  783.3 3.9 collective-permute-done.62
  (482 shorter events, 236.7 us)
Async XLA Ops:
  4.4 171.9 %collective-permute-start.25 = (bf16[256,2048]{1,0:T(8,128)(2,1)}, bf16[256,2048]{1,0:T(8,128)(2,1)}, u32[]{:S(2)}, u32[]{:S(2)}) collective-permute-start(bf16[256,2048]{1,0:T(8,128)(2,1)} %get-tuple-element.117), channel_id=1, source_target_pairs={{0,1},{1,0},{2,3},{3,2},{4,5},{5,4},{6,7},{7,6},{8,9},{9,8},{10,11... | collective-permute-start | bytes 3145736 | tf_op jit(solution)/shard_map/ppermute | solution.py:24
  7.4 169.6 %collective-permute-start.27 = (bf16[256,2048]{1,0:T(8,128)(2,1)}, bf16[256,2048]{1,0:T(8,128)(2,1)}, u32[]{:S(2)}, u32[]{:S(2)}) collective-permute-start(bf16[256,2048]{1,0:T(8,128)(2,1)} %get-tuple-element.117), channel_id=1, source_target_pairs={{0,16},{16,0},{1,17},{17,1},{2,18},{18,2},{3,19},{19,3},{4,20},{20... | collective-permute-start | bytes 3145736 | tf_op jit(solution)/shard_map/ppermute | solution.py:24
  8.9 107.0 %collective-permute-start.7 = (bf16[512,256]{1,0:T(8,128)(2,1)S(1)}, bf16[512,256]{1,0:T(8,128)(2,1)}, u32[]{:S(2)}, u32[]{:S(2)}) collective-permute-start(bf16[512,256]{1,0:T(8,128)(2,1)S(1)} %copy-done.42), channel_id=1, source_target_pairs={{0,8},{8,0},{1,9},{9,1},{2,10},{10,2},{3,11},{11,3},{4,12},{12,4},... | collective-permute-start | bytes 786440 | tf_op jit(solution)/shard_map/ppermute | solution.py:24
  9.6 105.8 %collective-permute-start.8 = (bf16[256,256]{1,0:T(8,128)(2,1)}, bf16[256,256]{1,0:T(8,128)(2,1)}, u32[]{:S(2)}, u32[]{:S(2)}) collective-permute-start(bf16[256,256]{1,0:T(8,128)(2,1)} %constant_dynamic-slice_fusion.23), channel_id=1, source_target_pairs={{0,16},{16,0},{1,17},{17,1},{2,18},{18,2},{3,19},{19,3},{4,20},{20... | collective-permute-start | bytes 393224 | tf_op jit(solution)/shard_map/ppermute | solution.py:24
  10.3 92.2 %collective-permute-start.5 = (bf16[8,512]{1,0:T(8,128)(2,1)S(1)}, bf16[8,512]{1,0:T(8,128)(2,1)S(1)}, u32[]{:S(2)}, u32[]{:S(2)}) collective-permute-start(bf16[8,512]{1,0:T(8,128)(2,1)S(1)} %stack.124), channel_id=1, source_target_pairs={{0,8},{8,0},{1,9},{9,1},{2,10},{10,2},{3,11},{11,3},{4,12},{12,4},... | collective-permute-start | bytes 24584 | tf_op jit(solution)/shard_map/ppermute | solution.py:24
  114.0 31.9 %collective-permute-start.50 = (bf16[256,2,512]{2,0,1:T(8,128)(2,1)}, bf16[256,2,512]{2,0,1:T(8,128)(2,1)}, u32[]{:S(2)}, u32[]{:S(2)}) collective-permute-start(bf16[256,2,512]{2,0,1:T(8,128)(2,1)} %bitcast.370), channel_id=1, source_target_pairs={{0,8},{8,0},{1,9},{9,1},{2,10},{10,2},{3,11},{11,3},{4,12},{12,4},... | collective-permute-start | bytes 1572872 | tf_op jit(solution)/shard_map/ppermute | solution.py:24
  145.8 29.2 %collective-permute-start.32 = (bf16[512,1024]{1,0:T(8,128)(2,1)}, bf16[512,1024]{1,0:T(8,128)(2,1)}, u32[]{:S(2)}, u32[]{:S(2)}) collective-permute-start(bf16[512,1024]{1,0:T(8,128)(2,1)} %bitcast.369), channel_id=1, source_target_pairs={{0,8},{8,0},{16,24},{24,16},{1,9},{9,1},{17,25},{25,17},{2,10},{10... | collective-permute-start | bytes 3145736 | tf_op jit(solution)/shard_map/ppermute | solution.py:638
  145.9 29.7 %collective-permute-start.33 = (bf16[512,1024]{1,0:T(8,128)(2,1)}, bf16[512,1024]{1,0:T(8,128)(2,1)}, u32[]{:S(2)}, u32[]{:S(2)}) collective-permute-start(bf16[512,1024]{1,0:T(8,128)(2,1)} %bitcast.368), channel_id=1, source_target_pairs={{0,16},{8,24},{16,0},{24,8},{1,17},{9,25},{17,1},{25,9},{2,18},{10... | collective-permute-start | bytes 3145736 | tf_op jit(solution)/shard_map/ppermute | solution.py:638
  174.9 82.2 %collective-permute-start = (bf16[512,2048]{1,0:T(8,128)(2,1)}, bf16[512,2048]{1,0:T(8,128)(2,1)S(1)}, u32[]{:S(2)}, u32[]{:S(2)}) collective-permute-start(bf16[512,2048]{1,0:T(8,128)(2,1)} %param.22), channel_id=1, source_target_pairs={{0,8},{8,0},{1,9},{9,1},{2,10},{10,2},{3,11},{11,3},{4,12},{12,4},... | collective-permute-start | bytes 6291464 | tf_op jit(solution)/shard_map/ppermute | solution.py:24
  174.9 49.0 %collective-permute-start.24 = (bf16[256,2048]{1,0:T(8,128)(2,1)}, bf16[256,2048]{1,0:T(8,128)(2,1)S(1)}, u32[]{:S(2)}, u32[]{:S(2)}) collective-permute-start(bf16[256,2048]{1,0:T(8,128)(2,1)} %get-tuple-element.117), channel_id=1, source_target_pairs={{0,8},{8,0},{1,9},{9,1},{2,10},{10,2},{3,11},{11,3},{4,12},{12,4},... | collective-permute-start | bytes 3145736 | tf_op jit(solution)/shard_map/ppermute | solution.py:24
  175.5 26.2 %collective-permute-start.1 = (bf16[256,2048]{1,0:T(8,128)(2,1)}, bf16[256,2048]{1,0:T(8,128)(2,1)S(1)}, u32[]{:S(2)}, u32[]{:S(2)}) collective-permute-start(bf16[256,2048]{1,0:T(8,128)(2,1)} %constant_dynamic-slice_fusion.24), channel_id=1, source_target_pairs={{0,16},{16,0},{1,17},{17,1},{2,18},{18,2},{3,19},{19,3},{4,20},{20... | collective-permute-start | bytes 3145736 | tf_op jit(solution)/shard_map/ppermute | solution.py:24
  176.3 46.2 %collective-permute-start.34 = (bf16[512,1024]{1,0:T(8,128)(2,1)S(1)}, bf16[512,1024]{1,0:T(8,128)(2,1)S(1)}, u32[]{:S(2)}, u32[]{:S(2)}) collective-permute-start(bf16[512,1024]{1,0:T(8,128)(2,1)S(1)} %bitcast.404), channel_id=1, source_target_pairs={{0,24},{8,16},{16,8},{24,0},{1,25},{9,17},{17,9},{25,1},{2,26},{10... | collective-permute-start | bytes 3145736 | tf_op jit(solution)/shard_map/ppermute | solution.py:638
  177.0 82.2 %collective-permute-start.19 = (bf16[512,2048]{1,0:T(8,128)(2,1)}, bf16[512,2048]{1,0:T(8,128)(2,1)S(1)}, u32[]{:S(2)}, u32[]{:S(2)}) collective-permute-start(bf16[512,2048]{1,0:T(8,128)(2,1)} %param.26), channel_id=1, source_target_pairs={{0,8},{8,0},{1,9},{9,1},{2,10},{10,2},{3,11},{11,3},{4,12},{12,4},... | collective-permute-start | bytes 6291464 | tf_op jit(solution)/shard_map/ppermute | solution.py:24
  201.7 57.4 %collective-permute-start.20 = (bf16[256,2048]{1,0:T(8,128)(2,1)S(1)}, bf16[256,2048]{1,0:T(8,128)(2,1)S(1)}, u32[]{:S(2)}, u32[]{:S(2)}) collective-permute-start(bf16[256,2048]{1,0:T(8,128)(2,1)S(1)} %copy-done.38), channel_id=1, source_target_pairs={{0,16},{16,0},{1,17},{17,1},{2,18},{18,2},{3,19},{19,3},{4,20},{20... | collective-permute-start | bytes 3145736 | tf_op jit(solution)/shard_map/ppermute | solution.py:24
  222.6 14.4 %collective-permute-start.29 = (bf16[128,2048]{1,0:T(8,128)(2,1)S(1)}, bf16[128,2048]{1,0:T(8,128)(2,1)S(1)}, u32[]{:S(2)}, u32[]{:S(2)}) collective-permute-start(bf16[128,2048]{1,0:T(8,128)(2,1)S(1)} %slice.228), channel_id=1, source_target_pairs={{0,1},{1,0},{2,3},{3,2},{4,5},{5,4},{6,7},{7,6},{8,9},{9,8},{10,11... | collective-permute-start | bytes 1572872 | tf_op jit(solution)/shard_map/ppermute | solution.py:24
  224.0 33.1 %collective-permute-start.30 = (bf16[128,2048]{1,0:T(8,128)(2,1)S(1)}, bf16[128,2048]{1,0:T(8,128)(2,1)S(1)}, u32[]{:S(2)}, u32[]{:S(2)}) collective-permute-start(bf16[128,2048]{1,0:T(8,128)(2,1)S(1)} %slice.229), channel_id=1, source_target_pairs={{0,16},{16,0},{1,17},{17,1},{2,18},{18,2},{3,19},{19,3},{4,20},{20... | collective-permute-start | bytes 1572872 | tf_op jit(solution)/shard_map/ppermute | solution.py:24
  236.9 31.0 %collective-permute-start.2 = (bf16[256,2048]{1,0:T(8,128)(2,1)S(1)}, bf16[256,2048]{1,0:T(8,128)(2,1)S(1)}, u32[]{:S(2)}, u32[]{:S(2)}) collective-permute-start(bf16[256,2048]{1,0:T(8,128)(2,1)S(1)} %collective-permute-done.1), channel_id=1, source_target_pairs={{0,1},{1,0},{2,3},{3,2},{4,5},{5,4},{6,7},{7,6},{8,9},{9,8},{10,11... | collective-permute-start | bytes 3145736 | tf_op jit(solution)/shard_map/ppermute | solution.py:24
  257.1 32.4 %collective-permute-start.3 = (bf16[256,2048]{1,0:T(8,128)(2,1)S(1)}, bf16[256,2048]{1,0:T(8,128)(2,1)S(1)}, u32[]{:S(2)}, u32[]{:S(2)}) collective-permute-start(bf16[256,2048]{1,0:T(8,128)(2,1)S(1)} %collective-permute-done.1), channel_id=1, source_target_pairs={{0,8},{8,0},{1,9},{9,1},{2,10},{10,2},{3,11},{11,3},{4,12},{12,4},... | collective-permute-start | bytes 3145736 | tf_op jit(solution)/shard_map/ppermute | solution.py:24
  259.2 25.8 %collective-permute-start.28 = (bf16[256,2048]{1,0:T(8,128)(2,1)}, bf16[256,2048]{1,0:T(8,128)(2,1)S(1)}, u32[]{:S(2)}, u32[]{:S(2)}) collective-permute-start(bf16[256,2048]{1,0:T(8,128)(2,1)} %collective-permute-done.27), channel_id=1, source_target_pairs={{0,8},{8,0},{1,9},{9,1},{2,10},{10,2},{3,11},{11,3},{4,12},{12,4},... | collective-permute-start | bytes 3145736 | tf_op jit(solution)/shard_map/ppermute | solution.py:24
  259.2 25.8 %collective-permute-start.21 = (bf16[256,2048]{1,0:T(8,128)(2,1)S(1)}, bf16[256,2048]{1,0:T(8,128)(2,1)S(1)}, u32[]{:S(2)}, u32[]{:S(2)}) collective-permute-start(bf16[256,2048]{1,0:T(8,128)(2,1)S(1)} %collective-permute-done.20), channel_id=1, source_target_pairs={{0,1},{1,0},{2,3},{3,2},{4,5},{5,4},{6,7},{7,6},{8,9},{9,8},{10,11... | collective-permute-start | bytes 3145736 | tf_op jit(solution)/shard_map/ppermute | solution.py:24
  264.3 26.2 %collective-permute-start.22 = (bf16[256,2048]{1,0:T(8,128)(2,1)S(1)}, bf16[256,2048]{1,0:T(8,128)(2,1)S(1)}, u32[]{:S(2)}, u32[]{:S(2)}) collective-permute-start(bf16[256,2048]{1,0:T(8,128)(2,1)S(1)} %collective-permute-done.20), channel_id=1, source_target_pairs={{0,8},{8,0},{1,9},{9,1},{2,10},{10,2},{3,11},{11,3},{4,12},{12,4},... | collective-permute-start | bytes 3145736 | tf_op jit(solution)/shard_map/ppermute | solution.py:24
  267.9 23.7 %collective-permute-start.31 = (bf16[256,2048]{1,0:T(8,128)(2,1)S(1)}, bf16[256,2048]{1,0:T(8,128)(2,1)S(1)}, u32[]{:S(2)}, u32[]{:S(2)}) collective-permute-start(bf16[256,2048]{1,0:T(8,128)(2,1)S(1)} %pad_maximum_fusion.2), channel_id=1, source_target_pairs={{0,8},{8,0},{1,9},{9,1},{2,10},{10,2},{3,11},{11,3},{4,12},{12,4},... | collective-permute-start | bytes 3145736 | tf_op jit(solution)/shard_map/ppermute | solution.py:24
  285.0 19.8 %collective-permute-start.23 = (bf16[256,2048]{1,0:T(8,128)(2,1)S(1)}, bf16[256,2048]{1,0:T(8,128)(2,1)S(1)}, u32[]{:S(2)}, u32[]{:S(2)}) collective-permute-start(bf16[256,2048]{1,0:T(8,128)(2,1)S(1)} %collective-permute-done.21), channel_id=1, source_target_pairs={{0,8},{8,0},{1,9},{9,1},{2,10},{10,2},{3,11},{11,3},{4,12},{12,4},... | collective-permute-start | bytes 3145736 | tf_op jit(solution)/shard_map/ppermute | solution.py:24
  413.0 53.3 %collective-permute-start.88 = (bf16[256,2048]{1,0:T(8,128)(2,1)}, bf16[256,2048]{1,0:T(8,128)(2,1)}, u32[]{:S(2)}, u32[]{:S(2)}) collective-permute-start(bf16[256,2048]{1,0:T(8,128)(2,1)} %get-tuple-element.65), channel_id=1, source_target_pairs={{0,2},{1,3},{8,10},{9,11},{16,18},{17,19},{24,26},{25,27}} | collective-permute-start | bytes 3145736 | tf_op jit(solution)/shard_map/ppermute | solution.py:244
  421.8 20.8 %collective-permute-start.82 = (bf16[256]{0:T(256)(128)(2,1)S(1)}, bf16[256]{0:T(256)(128)(2,1)S(1)}, u32[]{:S(2)}, u32[]{:S(2)}) collective-permute-start(bf16[256]{0:T(256)(128)(2,1)S(1)} %get-tuple-element.51), channel_id=1, source_target_pairs={{0,2},{1,3},{8,10},{9,11},{16,18},{17,19},{24,26},{25,27}} | collective-permute-start | bytes 1544 | tf_op jit(solution)/shard_map/ppermute | solution.py:244
  428.6 21.7 %collective-permute-start.36 = (bf16[256,2048]{1,0:T(8,128)(2,1)S(1)}, bf16[256,2048]{1,0:T(8,128)(2,1)S(1)}, u32[]{:S(2)}, u32[]{:S(2)}) collective-permute-start(bf16[256,2048]{1,0:T(8,128)(2,1)S(1)} %get-tuple-element.59), channel_id=1, source_target_pairs={{0,8},{8,0},{1,9},{9,1},{2,10},{10,2},{3,11},{11,3},{4,12},{12,4},... | collective-permute-start | bytes 3145736 | tf_op jit(solution)/shard_map/ppermute | solution.py:24
  428.6 30.6 %collective-permute-start.37 = (bf16[256,2048]{1,0:T(8,128)(2,1)S(1)}, bf16[256,2048]{1,0:T(8,128)(2,1)S(1)}, u32[]{:S(2)}, u32[]{:S(2)}) collective-permute-start(bf16[256,2048]{1,0:T(8,128)(2,1)S(1)} %get-tuple-element.58), channel_id=1, source_target_pairs={{0,8},{8,0},{1,9},{9,1},{2,10},{10,2},{3,11},{11,3},{4,12},{12,4},... | collective-permute-start | bytes 3145736 | tf_op jit(solution)/shard_map/ppermute | solution.py:24
  429.2 31.8 %collective-permute-start.40 = (bf16[256,2048]{1,0:T(8,128)(2,1)S(1)}, bf16[256,2048]{1,0:T(8,128)(2,1)S(1)}, u32[]{:S(2)}, u32[]{:S(2)}) collective-permute-start(bf16[256,2048]{1,0:T(8,128)(2,1)S(1)} %get-tuple-element.57), channel_id=1, source_target_pairs={{0,8},{8,0},{1,9},{9,1},{2,10},{10,2},{3,11},{11,3},{4,12},{12,4},... | collective-permute-start | bytes 3145736 | tf_op jit(solution)/shard_map/ppermute | solution.py:24
  449.6 62.6 %collective-permute-start.91 = (bf16[256,2048]{1,0:T(8,128)(2,1)S(1)}, bf16[256,2048]{1,0:T(8,128)(2,1)S(1)}, u32[]{:S(2)}, u32[]{:S(2)}) collective-permute-start(bf16[256,2048]{1,0:T(8,128)(2,1)S(1)} %copy-done.36), channel_id=1, source_target_pairs={{6,4},{7,5},{14,12},{15,13},{22,20},{23,21},{30,28},{31,29}} | collective-permute-start | bytes 3145736 | tf_op jit(solution)/shard_map/ppermute | solution.py:245
  450.3 28.4 %collective-permute-start.76 = (bf16[4,128,1024]{2,1,0:T(8,128)(2,1)S(1)}, bf16[4,128,1024]{2,1,0:T(8,128)(2,1)S(1)}, u32[]{:S(2)}, u32[]{:S(2)}) collective-permute-start(bf16[4,128,1024]{2,1,0:T(8,128)(2,1)S(1)} %get-tuple-element.69), channel_id=1, source_target_pairs={{0,2},{1,3},{8,10},{9,11},{16,18},{17,19},{24,26},{25,27}} | collective-permute-start | bytes 3145736 | tf_op jit(solution)/shard_map/ppermute | solution.py:244
  460.3 38.6 %collective-permute-start.79 = (bf16[4,128,1024]{2,1,0:T(8,128)(2,1)S(1)}, bf16[4,128,1024]{2,1,0:T(8,128)(2,1)S(1)}, u32[]{:S(2)}, u32[]{:S(2)}) collective-permute-start(bf16[4,128,1024]{2,1,0:T(8,128)(2,1)S(1)} %get-tuple-element.70), channel_id=1, source_target_pairs={{6,4},{7,5},{14,12},{15,13},{22,20},{23,21},{30,28},{31,29}} | collective-permute-start | bytes 3145736 | tf_op jit(solution)/shard_map/ppermute | solution.py:245
  462.0 31.4 %collective-permute-start.84 = (bf16[256]{0:T(256)(128)(2,1)S(1)}, bf16[256]{0:T(256)(128)(2,1)S(1)}, u32[]{:S(2)}, u32[]{:S(2)}) collective-permute-start(bf16[256]{0:T(256)(128)(2,1)S(1)} %add_convert_fusion.6), channel_id=1, source_target_pairs={{0,2},{2,4},{4,6},{1,3},{3,5},{5,7},{8,10},{10,12},{12,14},{9,11},... | collective-permute-start | bytes 1544 | tf_op jit(solution)/shard_map/ppermute | solution.py:244
  466.4 13.9 %collective-permute-start.38 = (bf16[128,2048]{1,0:T(8,128)(2,1)S(1)}, bf16[128,2048]{1,0:T(8,128)(2,1)S(1)}, u32[]{:S(2)}, u32[]{:S(2)}) collective-permute-start(bf16[128,2048]{1,0:T(8,128)(2,1)S(1)} %get-tuple-element.96), channel_id=1, source_target_pairs={{0,16},{16,0},{1,17},{17,1},{2,18},{18,2},{3,19},{19,3},{4,20},{20... | collective-permute-start | bytes 1572872 | tf_op jit(solution)/shard_map/ppermute | solution.py:24
  480.3 28.0 %collective-permute-start.77 = (bf16[4,128,1024]{2,1,0:T(8,128)(2,1)S(1)}, bf16[4,128,1024]{2,1,0:T(8,128)(2,1)S(1)}, u32[]{:S(2)}, u32[]{:S(2)}) collective-permute-start(bf16[4,128,1024]{2,1,0:T(8,128)(2,1)S(1)} %fusion.33), channel_id=1, source_target_pairs={{0,2},{2,4},{1,3},{3,5},{8,10},{10,12},{9,11},{11,13},{16,18},{18,... | collective-permute-start | bytes 3145736 | tf_op jit(solution)/shard_map/ppermute | solution.py:244
  488.6 36.8 %collective-permute-start.89 = (bf16[256,2048]{1,0:T(8,128)(2,1)S(1)}, bf16[256,2048]{1,0:T(8,128)(2,1)S(1)}, u32[]{:S(2)}, u32[]{:S(2)}) collective-permute-start(bf16[256,2048]{1,0:T(8,128)(2,1)S(1)} %fusion.28), channel_id=1, source_target_pairs={{0,2},{2,4},{1,3},{3,5},{8,10},{10,12},{9,11},{11,13},{16,18},{18,... | collective-permute-start | bytes 3145736 | tf_op jit(solution)/shard_map/ppermute | solution.py:244
  498.9 30.5 %collective-permute-start.35 = (bf16[256,2048]{1,0:T(8,128)(2,1)S(1)}, bf16[256,2048]{1,0:T(8,128)(2,1)S(1)}, u32[]{:S(2)}, u32[]{:S(2)}) collective-permute-start(bf16[256,2048]{1,0:T(8,128)(2,1)S(1)} %copy-done.39), channel_id=1, source_target_pairs={{0,8},{8,0},{1,9},{9,1},{2,10},{10,2},{3,11},{11,3},{4,12},{12,4},... | collective-permute-start | bytes 3145736 | tf_op jit(solution)/shard_map/ppermute | solution.py:24
  498.9 30.5 %collective-permute-start.39 = (bf16[256,2048]{1,0:T(8,128)(2,1)S(1)}, bf16[256,2048]{1,0:T(8,128)(2,1)S(1)}, u32[]{:S(2)}, u32[]{:S(2)}) collective-permute-start(bf16[256,2048]{1,0:T(8,128)(2,1)S(1)} %pad_maximum_fusion.3), channel_id=1, source_target_pairs={{0,1},{1,0},{2,3},{3,2},{4,5},{5,4},{6,7},{7,6},{8,9},{9,8},{10,11... | collective-permute-start | bytes 3145736 | tf_op jit(solution)/shard_map/ppermute | solution.py:24
  508.3 21.2 %collective-permute-start.42 = (bf16[256,2048]{1,0:T(8,128)(2,1)S(1)}, bf16[256,2048]{1,0:T(8,128)(2,1)S(1)}, u32[]{:S(2)}, u32[]{:S(2)}) collective-permute-start(bf16[256,2048]{1,0:T(8,128)(2,1)S(1)} %pad_maximum_fusion.4), channel_id=1, source_target_pairs={{0,16},{16,0},{1,17},{17,1},{2,18},{18,2},{3,19},{19,3},{4,20},{20... | collective-permute-start | bytes 3145736 | tf_op jit(solution)/shard_map/ppermute | solution.py:24
  512.2 109.4 %collective-permute-start.63 = (bf16[256,2,512]{0,2,1:T(8,128)(2,1)}, bf16[256,2,512]{0,2,1:T(8,128)(2,1)}, u32[]{:S(2)}, u32[]{:S(2)}) collective-permute-start(bf16[256,2,512]{0,2,1:T(8,128)(2,1)} %get-tuple-element.93), channel_id=1, source_target_pairs={{0,8},{8,0},{1,9},{9,1},{2,10},{10,2},{3,11},{11,3},{4,12},{12,4},... | collective-permute-start | bytes 1572872 | tf_op jit(solution)/shard_map/ppermute | solution.py:24
  525.5 72.3 %collective-permute-start.80 = (bf16[4,128,1024]{2,1,0:T(8,128)(2,1)}, bf16[4,128,1024]{2,1,0:T(8,128)(2,1)}, u32[]{:S(2)}, u32[]{:S(2)}) collective-permute-start(bf16[4,128,1024]{2,1,0:T(8,128)(2,1)} %get-tuple-element.68), channel_id=1, source_target_pairs={{4,2},{6,4},{5,3},{7,5},{12,10},{14,12},{13,11},{15,13},{20,18},{2... | collective-permute-start | bytes 3145736 | tf_op jit(solution)/shard_map/ppermute | solution.py:245
  554.8 30.3 %collective-permute-start.67 = (bf16[2,512,128]{2,1,0:T(8,128)(2,1)}, bf16[2,512,128]{2,1,0:T(8,128)(2,1)S(1)}, u32[]{:S(2)}, u32[]{:S(2)}) collective-permute-start(bf16[2,512,128]{2,1,0:T(8,128)(2,1)} %bitcast.413), channel_id=1, source_target_pairs={{0,8},{8,0},{1,9},{9,1},{2,10},{10,2},{3,11},{11,3},{4,12},{12,4},... | collective-permute-start | bytes 786440 | tf_op jit(solution)/shard_map/ppermute | solution.py:24
  570.8 12.1 %collective-permute-start.48 = (bf16[2,128,256]{2,1,0:T(8,128)(2,1)}, bf16[2,128,256]{2,1,0:T(8,128)(2,1)}, u32[]{:S(2)}, u32[]{:S(2)}) collective-permute-start(bf16[2,128,256]{2,1,0:T(8,128)(2,1)} %fusion.117), channel_id=1, source_target_pairs={{2,0},{4,2},{6,4},{3,1},{5,3},{7,5},{10,8},{12,10},{14,12},{11,9},... | collective-permute-start | bytes 393224 | tf_op jit(solution)/shard_map/ppermute | solution.py:716
  573.0 44.0 %collective-permute-start.92 = (bf16[256,2048]{1,0:T(8,128)(2,1)}, bf16[256,2048]{1,0:T(8,128)(2,1)}, u32[]{:S(2)}, u32[]{:S(2)}) collective-permute-start(bf16[256,2048]{1,0:T(8,128)(2,1)} %get-tuple-element.64), channel_id=1, source_target_pairs={{4,2},{6,4},{5,3},{7,5},{12,10},{14,12},{13,11},{15,13},{20,18},{2... | collective-permute-start | bytes 3145736 | tf_op jit(solution)/shard_map/ppermute | solution.py:245
  587.9 63.5 %collective-permute-start.78 = (bf16[4,128,1024]{2,1,0:T(8,128)(2,1)}, bf16[4,128,1024]{2,1,0:T(8,128)(2,1)}, u32[]{:S(2)}, u32[]{:S(2)}) collective-permute-start(bf16[4,128,1024]{2,1,0:T(8,128)(2,1)} %get-tuple-element.67), channel_id=1, source_target_pairs={{0,2},{2,4},{4,6},{1,3},{3,5},{5,7},{8,10},{10,12},{12,14},{9,11},... | collective-permute-start | bytes 3145736 | tf_op jit(solution)/shard_map/ppermute | solution.py:244
  595.9 46.4 %collective-permute-start.64 = (bf16[256,2048]{1,0:T(8,128)(2,1)}, bf16[256,2048]{1,0:T(8,128)(2,1)}, u32[]{:S(2)}, u32[]{:S(2)}) collective-permute-start(bf16[256,2048]{1,0:T(8,128)(2,1)} %get-tuple-element.54), channel_id=1, source_target_pairs={{0,8},{8,0},{1,9},{9,1},{2,10},{10,2},{3,11},{11,3},{4,12},{12,4},... | collective-permute-start | bytes 3145736 | tf_op jit(solution)/shard_map/ppermute | solution.py:24
  600.8 51.9 %collective-permute-start.81 = (bf16[4,128,1024]{2,1,0:T(8,128)(2,1)}, bf16[4,128,1024]{2,1,0:T(8,128)(2,1)}, u32[]{:S(2)}, u32[]{:S(2)}) collective-permute-start(bf16[4,128,1024]{2,1,0:T(8,128)(2,1)} %fusion.32), channel_id=1, source_target_pairs={{2,0},{4,2},{6,4},{3,1},{5,3},{7,5},{10,8},{12,10},{14,12},{11,9},... | collective-permute-start | bytes 3145736 | tf_op jit(solution)/shard_map/ppermute | solution.py:245
  621.6 40.5 %collective-permute-start.51 = (bf16[256,2304]{0,1:T(8,128)(2,1)}, bf16[256,2304]{0,1:T(8,128)(2,1)}, u32[]{:S(2)}, u32[]{:S(2)}) collective-permute-start(bf16[256,2304]{0,1:T(8,128)(2,1)} %pad_maximum_fusion), channel_id=1, source_target_pairs={{0,8},{8,0},{1,9},{9,1},{2,10},{10,2},{3,11},{11,3},{4,12},{12,4},... | collective-permute-start | bytes 3538952 | tf_op jit(solution)/shard_map/ppermute | solution.py:24
  621.7 64.0 %collective-permute-start.90 = (bf16[256,2048]{1,0:T(8,128)(2,1)}, bf16[256,2048]{1,0:T(8,128)(2,1)}, u32[]{:S(2)}, u32[]{:S(2)}) collective-permute-start(bf16[256,2048]{1,0:T(8,128)(2,1)} %get-tuple-element.63), channel_id=1, source_target_pairs={{0,2},{2,4},{4,6},{1,3},{3,5},{5,7},{8,10},{10,12},{12,14},{9,11},... | collective-permute-start | bytes 3145736 | tf_op jit(solution)/shard_map/ppermute | solution.py:244
  648.3 26.3 %collective-permute-start.65 = (bf16[4,2,64,1024]{3,2,0,1:T(8,128)(2,1)}, bf16[4,2,64,1024]{3,2,0,1:T(8,128)(2,1)}, u32[]{:S(2)}, u32[]{:S(2)}) collective-permute-start(bf16[4,2,64,1024]{3,2,0,1:T(8,128)(2,1)} %fusion.49), channel_id=1, source_target_pairs={{0,16},{16,0},{1,17},{17,1},{2,18},{18,2},{3,19},{19,3},{4,20},{20... | collective-permute-start | bytes 3145736 | tf_op jit(solution)/shard_map/ppermute | solution.py:24
  651.4 34.2 %collective-permute-start.93 = (bf16[256,2048]{1,0:T(8,128)(2,1)}, bf16[256,2048]{1,0:T(8,128)(2,1)}, u32[]{:S(2)}, u32[]{:S(2)}) collective-permute-start(bf16[256,2048]{1,0:T(8,128)(2,1)} %fusion.27), channel_id=1, source_target_pairs={{2,0},{4,2},{6,4},{3,1},{5,3},{7,5},{10,8},{12,10},{14,12},{11,9},... | collective-permute-start | bytes 3145736 | tf_op jit(solution)/shard_map/ppermute | solution.py:245
  652.7 29.2 %collective-permute-start.68 = (bf16[2,4,64,1152]{3,2,1,0:T(8,128)(2,1)}, bf16[2,4,64,1152]{3,2,1,0:T(8,128)(2,1)}, u32[]{:S(2)}, u32[]{:S(2)}) collective-permute-start(bf16[2,4,64,1152]{3,2,1,0:T(8,128)(2,1)} %fusion.47), channel_id=1, source_target_pairs={{0,1},{1,0},{2,3},{3,2},{4,5},{5,4},{6,7},{7,6},{8,9},{9,8},{10,11... | collective-permute-start | bytes 3538952 | tf_op jit(solution)/shard_map/ppermute | solution.py:24
  657.4 34.9 %all-to-all-start = ((bf16[8,64,1024]{2,1,0:T(8,128)(2,1)}), bf16[8,64,1024]{2,1,0:T(8,128)(2,1)}, u32[]{:S(2)}, u32[]{:S(2)}) async-start(bf16[8,64,1024]{2,1,0:T(8,128)(2,1)} %bitcast.395), calls=%async_computation | async-start | bytes 2097152 | tf_op jit(solution)/shard_map/all_to_all | solution.py:681
  668.0 56.4 %collective-permute-start.52 = (bf16[4,2,64,1152]{3,2,0,1:T(8,128)(2,1)}, bf16[4,2,64,1152]{3,2,0,1:T(8,128)(2,1)}, u32[]{:S(2)}, u32[]{:S(2)}) collective-permute-start(bf16[4,2,64,1152]{3,2,0,1:T(8,128)(2,1)} %fusion.46), channel_id=1, source_target_pairs={{0,16},{16,0},{1,17},{17,1},{2,18},{18,2},{3,19},{19,3},{4,20},{20... | collective-permute-start | bytes 3538952 | tf_op jit(solution)/shard_map/ppermute | solution.py:24
  677.2 27.2 %collective-permute-start.66 = (bf16[4,64,1024]{2,1,0:T(8,128)(2,1)}, bf16[4,64,1024]{2,1,0:T(8,128)(2,1)}, u32[]{:S(2)}, u32[]{:S(2)}) collective-permute-start(bf16[4,64,1024]{2,1,0:T(8,128)(2,1)} %fusion.110), channel_id=1, source_target_pairs={{0,1},{1,0},{2,3},{3,2},{4,5},{5,4},{6,7},{7,6},{8,9},{9,8},{10,11... | collective-permute-start | bytes 1572872 | tf_op jit(solution)/shard_map/ppermute | solution.py:24
  684.5 38.5 %collective-permute-start.69 = (bf16[4,64,1152]{2,1,0:T(8,128)(2,1)}, bf16[4,64,1152]{2,1,0:T(8,128)(2,1)}, u32[]{:S(2)}, u32[]{:S(2)}) collective-permute-start(bf16[4,64,1152]{2,1,0:T(8,128)(2,1)} %fusion.85), channel_id=1, source_target_pairs={{0,16},{16,0},{1,17},{17,1},{2,18},{18,2},{3,19},{19,3},{4,20},{20... | collective-permute-start | bytes 1769480 | tf_op jit(solution)/shard_map/ppermute | solution.py:24
  690.5 41.9 %collective-permute-start.55 = (bf16[2,4,64,1280]{3,2,1,0:T(8,128)(2,1)}, bf16[2,4,64,1280]{3,2,1,0:T(8,128)(2,1)S(1)}, u32[]{:S(2)}, u32[]{:S(2)}) collective-permute-start(bf16[2,4,64,1280]{3,2,1,0:T(8,128)(2,1)} %fusion.45), channel_id=1, source_target_pairs={{0,1},{1,0},{2,3},{3,2},{4,5},{5,4},{6,7},{7,6},{8,9},{9,8},{10,11... | collective-permute-start | bytes 3932168 | tf_op jit(solution)/shard_map/ppermute | solution.py:24
  727.3 17.1 %collective-permute-start.53 = (bf16[4,64,1152]{2,1,0:T(8,128)(2,1)S(1)}, bf16[4,64,1152]{2,1,0:T(8,128)(2,1)S(1)}, u32[]{:S(2)}, u32[]{:S(2)}) collective-permute-start(bf16[4,64,1152]{2,1,0:T(8,128)(2,1)S(1)} %fusion.84), channel_id=1, source_target_pairs={{0,1},{1,0},{2,3},{3,2},{4,5},{5,4},{6,7},{7,6},{8,9},{9,8},{10,11... | collective-permute-start | bytes 1769480 | tf_op jit(solution)/shard_map/ppermute | solution.py:24
  732.8 15.4 %collective-permute-start.56 = (bf16[4,64,1280]{2,1,0:T(8,128)(2,1)S(1)}, bf16[4,64,1280]{2,1,0:T(8,128)(2,1)S(1)}, u32[]{:S(2)}, u32[]{:S(2)}) collective-permute-start(bf16[4,64,1280]{2,1,0:T(8,128)(2,1)S(1)} %fusion.59), channel_id=1, source_target_pairs={{0,16},{16,0},{1,17},{17,1},{2,18},{18,2},{3,19},{19,3},{4,20},{20... | collective-permute-start | bytes 1966088 | tf_op jit(solution)/shard_map/ppermute | solution.py:24
  734.0 19.1 %collective-permute-start.70 = (bf16[64,2176]{1,0:T(8,128)(2,1)S(1)}, bf16[64,2176]{1,0:T(8,128)(2,1)S(1)}, u32[]{:S(2)}, u32[]{:S(2)}) collective-permute-start(bf16[64,2176]{1,0:T(8,128)(2,1)S(1)} %get-tuple-element.85), channel_id=1, source_target_pairs={{0,2},{1,3},{8,10},{9,11},{16,18},{17,19},{24,26},{25,27}} | collective-permute-start | bytes 835592 | tf_op jit(solution)/shard_map/ppermute | solution.py:244
  738.6 14.5 %collective-permute-start.73 = (bf16[64,2176]{1,0:T(8,128)(2,1)S(1)}, bf16[64,2176]{1,0:T(8,128)(2,1)S(1)}, u32[]{:S(2)}, u32[]{:S(2)}) collective-permute-start(bf16[64,2176]{1,0:T(8,128)(2,1)S(1)} %get-tuple-element.86), channel_id=1, source_target_pairs={{6,4},{7,5},{14,12},{15,13},{22,20},{23,21},{30,28},{31,29}} | collective-permute-start | bytes 835592 | tf_op jit(solution)/shard_map/ppermute | solution.py:245
  748.5 11.7 %collective-permute-start.57 = (bf16[64,2432]{1,0:T(8,128)(2,1)S(1)}, bf16[64,2432]{1,0:T(8,128)(2,1)S(1)}, u32[]{:S(2)}, u32[]{:S(2)}) collective-permute-start(bf16[64,2432]{1,0:T(8,128)(2,1)S(1)} %get-tuple-element.79), channel_id=1, source_target_pairs={{0,2},{1,3},{8,10},{9,11},{16,18},{17,19},{24,26},{25,27}} | collective-permute-start | bytes 933896 | tf_op jit(solution)/shard_map/ppermute | solution.py:244
  753.2 12.9 %collective-permute-start.71 = (bf16[64,2176]{1,0:T(8,128)(2,1)S(1)}, bf16[64,2176]{1,0:T(8,128)(2,1)S(1)}, u32[]{:S(2)}, u32[]{:S(2)}) collective-permute-start(bf16[64,2176]{1,0:T(8,128)(2,1)S(1)} %get-tuple-element.83), channel_id=1, source_target_pairs={{0,2},{2,4},{1,3},{3,5},{8,10},{10,12},{9,11},{11,13},{16,18},{18,... | collective-permute-start | bytes 835592 | tf_op jit(solution)/shard_map/ppermute | solution.py:244
  760.3 12.5 %collective-permute-start.58 = (bf16[64,2432]{1,0:T(8,128)(2,1)S(1)}, bf16[64,2432]{1,0:T(8,128)(2,1)S(1)}, u32[]{:S(2)}, u32[]{:S(2)}) collective-permute-start(bf16[64,2432]{1,0:T(8,128)(2,1)S(1)} %get-tuple-element.77), channel_id=1, source_target_pairs={{0,2},{2,4},{1,3},{3,5},{8,10},{10,12},{9,11},{11,13},{16,18},{18,... | collective-permute-start | bytes 933896 | tf_op jit(solution)/shard_map/ppermute | solution.py:244
  766.3 13.4 %collective-permute-start.72 = (bf16[64,2176]{1,0:T(8,128)(2,1)S(1)}, bf16[64,2176]{1,0:T(8,128)(2,1)S(1)}, u32[]{:S(2)}, u32[]{:S(2)}) collective-permute-start(bf16[64,2176]{1,0:T(8,128)(2,1)S(1)} %get-tuple-element.81), channel_id=1, source_target_pairs={{0,2},{2,4},{4,6},{1,3},{3,5},{5,7},{8,10},{10,12},{12,14},{9,11},... | collective-permute-start | bytes 835592 | tf_op jit(solution)/shard_map/ppermute | solution.py:244
  (100 other events, 964.2 us)

commit v3 on v2

--- a/solution.py
+++ b/solution.py
@@ -568,6 +568,496 @@
     )(second, down_all, up_mine, ubias, down_mine)
 
 
+ROW_TILE = 32
+
+
+def for_rows(total, fn):
+    @pl.loop(0, total // ROW_TILE)
+    def step(index):
+        fn(pl.ds(pl.multiple_of(index * ROW_TILE, ROW_TILE), ROW_TILE))
+
+
+def norm_rows(values):
+    center = values - jnp.mean(values, axis=-1, keepdims=True)
+    spread = jnp.mean(center * center, axis=-1, keepdims=True)
+    rstd = lax.rsqrt(spread + EPSILON)
+    return center * rstd, rstd
+
+
+class Gathered:
+    def __init__(self, shard_ref, full_ref, sems, base, where):
+        self.y, self.c, self.x = where
+        self.shard, self.full, self.sems, self.base = shard_ref, full_ref, sems, base
+        self.rows = shard_ref.shape[0]
+        self.half = self.rows // 2
+        self.step = self.half // 4
+        self.place = self.y * 2 + self.c
+
+    def copy(self, src, dst, index, device):
+        send_sems, recv_sems = self.sems
+        return remote(src, dst, send_sems, recv_sems, self.base + index, device)
+
+    def span(self, place, side, i):
+        start = place * self.rows + side * self.half + i * self.step
+        return self.full.at[pl.ds(pl.multiple_of(start, self.step), self.step)]
+
+    def over_y(self, i):
+        start = pl.multiple_of(self.x * self.half + i * self.step, self.step)
+        return self.copy(
+            self.shard.at[pl.ds(start, self.step)], self.span(self.place, self.x, i), i, {"y": 1 - self.y}
+        )
+
+    def over_x(self, i):
+        ref = self.span(self.place ^ 2, self.x, i)
+        return self.copy(ref, ref, 4 + i, {"x": 1 - self.x})
+
+    def over_c(self, i, side):
+        ref = self.span(self.place ^ 2, self.x if side == 0 else 1 - self.x, i)
+        return self.copy(ref, ref, 8 + 4 * side + i, {"c": 1 - self.c})
+
+    def own_c(self):
+        start = pl.multiple_of(self.place * self.rows, self.rows)
+        return self.copy(self.shard, self.full.at[pl.ds(start, self.rows)], 16, {"c": 1 - self.c})
+
+    def own(self, sem):
+        start = pl.multiple_of(self.place * self.rows, self.rows)
+        return pltpu.make_async_copy(self.shard, self.full.at[pl.ds(start, self.rows)], sem)
+
+
+class Stream:
+    def __init__(self, weights):
+        self.order = [(w, i) for w in weights for i in range(4)]
+        self.next = 0
+        self.sent = []
+
+    def begin(self, copy):
+        copy.start()
+        self.sent.append(copy)
+
+    def start(self):
+        for n in range(2):
+            w, i = self.order[n]
+            self.begin(w.over_y(i))
+
+    def event(self):
+        n = self.next
+        self.next += 1
+        if n < len(self.order):
+            w, i = self.order[n]
+            w.over_y(i).wait_recv()
+            if n + 2 < len(self.order):
+                w2, i2 = self.order[n + 2]
+                self.begin(w2.over_y(i2))
+            self.begin(w.over_x(i))
+            self.begin(w.over_c(i, 0))
+        if n >= 1:
+            w, i = self.order[n - 1]
+            w.over_x(i).wait_recv()
+            self.begin(w.over_c(i, 1))
+
+    def settle(self, weight):
+        weight.own_c().wait_recv()
+        for i in range(4):
+            weight.over_c(i, 0).wait_recv()
+            weight.over_c(i, 1).wait_recv()
+
+
+def front_kernel(
+    lengths_ref,
+    tokens_v,
+    smalls_ref,
+    kvw_ref,
+    qw_ref,
+    mw_ref,
+    up_ref,
+    cot_ref,
+    second_ref,
+    residual_ref,
+    first_v,
+    q_v,
+    kv_v,
+    mixed_v,
+    lse_ref,
+    vec_v,
+    wq_out,
+    wm_out,
+    wkv_v,
+    up_out,
+    cots_out,
+    wq_v,
+    wm_v,
+    smalls_v,
+    local_sem,
+    w_send,
+    w_recv,
+    s_send,
+    s_recv,
+    k_send,
+    k_recv,
+    u_send,
+    u_recv,
+    uz_send,
+    uz_recv,
+    c_send,
+    c_recv,
+    *,
+    length,
+    slots,
+    with_length,
+    aligned,
+):
+    rows, width = tokens_v.shape
+    seg = rows // slots
+    head_dim = kvw_ref.shape[1] // 2
+    heads = width // head_dim
+    group = 4
+    quarter = width // 4
+    y, c, z, x = [lax.axis_index(name) for name in ("y", "c", "z", "x")]
+    place = y * 2 + c
+    sib, to_x, to_y = {"c": 1 - c}, {"x": 1 - x}, {"y": 1 - y}
+    cross, diag = {"y": 1 - y, "c": 1 - c}, {"x": 1 - x, "y": 1 - y}
+
+    weights = [
+        Gathered(ref, full, (w_send, w_recv), 17 * n, (y, c, x))
+        for n, (ref, full) in enumerate(((qw_ref, wq_v), (mw_ref, wm_v)))
+    ]
+    query_w, mixer_w = weights
+    locals_ = [query_w.own(local_sem.at[0]), mixer_w.own(local_sem.at[1])]
+    kv_rows = pl.ds(pl.multiple_of(place * quarter, quarter), quarter)
+    locals_.append(pltpu.make_async_copy(kvw_ref, wkv_v.at[kv_rows], local_sem.at[2]))
+    locals_.append(pltpu.make_async_copy(smalls_ref, smalls_v.at[place], local_sem.at[3]))
+    for copy in locals_:
+        copy.start()
+
+    barrier = pltpu.get_barrier_semaphore()
+    for device in (sib, to_x, to_y, cross, diag):
+        pl.semaphore_signal(barrier, inc=1, device_id=device, device_id_type=MESH)
+    for other in range(length):
+        @pl.when(other != z)
+        def hello():
+            pl.semaphore_signal(barrier, inc=1, device_id={"z": other}, device_id_type=MESH)
+    pl.semaphore_wait(barrier, 5 + length - 1)
+
+    sent = []
+
+    def begin(copy):
+        copy.start()
+        sent.append(copy)
+        return copy
+
+    small_copies = [
+        begin(remote(smalls_ref, smalls_v.at[place], s_send, s_recv, n, device))
+        for n, device in enumerate((sib, to_y, cross))
+    ]
+    kv_near = begin(remote(kvw_ref, wkv_v.at[kv_rows], s_send, s_recv, 3, sib))
+    kv_far = begin(remote(kvw_ref, wkv_v.at[kv_rows], s_send, s_recv, 4, to_y))
+    stream = Stream(weights)
+    stream.start()
+    for weight in weights:
+        begin(weight.own_c())
+
+    for copy in small_copies:
+        copy.wait_recv()
+    locals_[3].wait()
+    vec_v[...] = jnp.concatenate([smalls_v[f].astype(F32) for f in range(4)], axis=1)
+
+    def first_norm(span):
+        unit, _ = norm_rows(tokens_v[span, :].astype(F32))
+        first_v[span, :] = (unit * vec_v[0:1, :] + vec_v[1:2, :]).astype(BF)
+
+    for_rows(rows, first_norm)
+
+    kv_far.wait_recv()
+    far_rows = wkv_v.at[pl.ds(pl.multiple_of((place ^ 2) * quarter, quarter), quarter)]
+    kv_pass = begin(remote(far_rows, far_rows, s_send, s_recv, 5, sib))
+    stream.event()
+    kv_near.wait_recv()
+    locals_[2].wait()
+    kv_pass.wait_recv()
+    v_bias = (
+        vec_v[7:8, 0:head_dim]
+        + vec_v[7:8, quarter : quarter + head_dim]
+        + vec_v[7:8, 2 * quarter : 2 * quarter + head_dim]
+        + vec_v[7:8, 3 * quarter : 3 * quarter + head_dim]
+    )
+    keyvals = dot(first_v[...], wkv_v[...]) + jnp.concatenate([jnp.zeros_like(v_bias), v_bias], axis=1)
+    mine = pl.ds(pl.multiple_of(x * seg, seg), seg)
+    for s in range(slots):
+        kv_v[s, 0, mine, :] = keyvals[s * seg : (s + 1) * seg].astype(BF)
+
+    def kv_up(t):
+        return remote(kv_v.at[:, t - 1, mine], kv_v.at[:, t, mine], k_send, k_recv, t, {"z": z + 1})
+
+    def kv_side(t):
+        ref = kv_v.at[:, t, mine]
+        return remote(ref, ref, k_send, k_recv, length + t, to_x)
+
+    def kv_step(t):
+        if t:
+            @pl.when(z >= t)
+            def arrive():
+                kv_up(t).wait_recv()
+
+        @pl.when(z >= t)
+        def side():
+            kv_side(t).start()
+
+        if t + 1 < length:
+            @pl.when((z >= t) & (z < length - 1))
+            def onward():
+                kv_up(t + 1).start()
+
+    part = quarter // length
+    hidden = up_out.shape[1]
+    block = hidden // length
+
+    def up_copies(index, flip, span, device):
+        target = place ^ flip
+        dst_rows = pl.ds(pl.multiple_of(place * quarter + span[0], span[1]), span[1])
+        copies = []
+        for b in range(length if aligned else 1):
+            if aligned:
+                start = target * (hidden * 2) + (2 * b + x) * block
+                src = up_ref.at[pl.ds(span[0], span[1]), pl.ds(pl.multiple_of(start, block), block)]
+                dst = up_out.at[dst_rows, pl.ds(b * block, block)]
+            else:
+                src = up_ref.at[target, pl.ds(span[0], span[1])]
+                dst = up_out.at[dst_rows]
+            n = index * length + b
+            if device is None:
+                copies.append(pltpu.make_async_copy(src, dst, u_send.at[n]))
+            else:
+                copies.append(remote(src, dst, u_send, u_recv, n, device))
+        return copies
+
+    up_local = up_copies(0, 0, (0, quarter), None)
+    up_near = up_copies(1, 1, (0, quarter), sib)
+    z_part = (pl.multiple_of(z * part, part), part)
+    up_far = up_copies(2, 2, z_part, to_y) + up_copies(3, 3, z_part, cross)
+
+    def up_share(k, source, target):
+        start = (place ^ (2 + k)) * quarter + source * part
+        ref = up_out.at[pl.ds(pl.multiple_of(start, part), part)]
+        return pltpu.make_async_remote_copy(
+            src_ref=ref,
+            dst_ref=ref,
+            send_sem=uz_send.at[k, target],
+            recv_sem=uz_recv.at[k, source],
+            device_id={"z": target},
+            device_id_type=MESH,
+        )
+
+    for copy in up_local:
+        copy.start()
+    for copy in up_near:
+        begin(copy)
+
+    for t in range(length):
+        kv_step(t)
+        if t < 3:
+            stream.event()
+
+    same, other_half = pl.ds(0, rows), pl.ds(rows, rows)
+    top, bottom = pl.ds(0, rows // 2), pl.ds(rows // 2, rows // 2)
+    cot_local = pltpu.make_async_copy(cot_ref, cots_out.at[0, same], local_sem.at[4])
+    cot_local.start()
+    cot_x = remote(cot_ref, cots_out.at[1, same], c_send, c_recv, 0, to_x)
+    cot_y = remote(cot_ref, cots_out.at[2, same], c_send, c_recv, 1, to_y)
+    cot_share = [
+        remote(cot_ref if k == 0 else cots_out.at[k, same], cots_out.at[k, other_half], c_send, c_recv, 2 + k, sib)
+        for k in range(4)
+    ]
+    cot_dx = remote(cots_out.at[2, top], cots_out.at[3, top], c_send, c_recv, 6, to_x)
+    cot_dy = remote(cots_out.at[1, bottom], cots_out.at[3, bottom], c_send, c_recv, 7, to_y)
+
+    stream.event()
+    locals_[0].wait()
+    stream.settle(query_w)
+
+    @tiles(width // 512, 512)
+    def project(cols, _):
+        q_v[:, cols] = (dot(first_v[...], wq_v[:, cols]) + vec_v[2:3, cols]).astype(BF)
+
+    wq_copy = pltpu.make_async_copy(wq_v, wq_out, local_sem.at[5])
+    wq_copy.start()
+    for t in range(length):
+        @pl.when(z >= t)
+        def arrived():
+            kv_side(t).wait_recv()
+            kv_side(t).wait_send()
+
+        if t:
+            @pl.when((z >= t - 1) & (z < length - 1))
+            def gone():
+                kv_up(t).wait_send()
+
+    scale = head_dim ** (-0.5)
+
+    def attend(s, g):
+        lanes = pl.ds(pl.multiple_of(g * group * head_dim, group * head_dim), group * head_dim)
+        wide = q_v[pl.ds(s * seg, seg), lanes]
+        queries = jnp.concatenate(
+            [wide[:, h * head_dim : (h + 1) * head_dim] for h in range(group)], axis=0
+        )
+
+        def step(t, state, diagonal):
+            top_, total, accum = state
+            keys = kv_v[s, t, :, :head_dim]
+            values = kv_v[s, t, :, head_dim:]
+            scores = dot(keys, queries, ((1,), (1,))) * scale
+            if diagonal or with_length:
+                key_pos = lax.broadcasted_iota(jnp.int32, (2 * seg, seg), 0)
+                allowed = None
+                if diagonal:
+                    query_pos = lax.broadcasted_iota(jnp.int32, (2 * seg, seg), 1) + x * seg
+                    allowed = key_pos <= query_pos
+                if with_length:
+                    inside = key_pos + (z - t) * (2 * seg) < lengths_ref[s]
+                    allowed = inside if allowed is None else allowed & inside
+                bias = jnp.where(allowed, 0.0, NEG_LARGE).astype(F32)
+                scores = scores + jnp.concatenate([bias] * group, axis=1)
+            new_top = jnp.maximum(top_, jnp.max(scores, axis=0, keepdims=True))
+            terms = jnp.exp(scores - new_top)
+            fade = jnp.exp(top_ - new_top)
+            total = total * fade + jnp.sum(terms, axis=0, keepdims=True)
+            accum = accum * fade + dot(values, terms.astype(BF), ((0,), (0,)))
+            return new_top, total, accum
+
+        span = group * seg
+        state = (
+            jnp.full((1, span), NEG_LARGE, F32),
+            jnp.zeros((1, span), F32),
+            jnp.zeros((head_dim, span), F32),
+        )
+        state = step(0, state, True)
+        top_, total, accum = lax.fori_loop(1, z + 1, lambda t, st: step(t, st, False), state)
+        out = accum / total
+        mixed_v[pl.ds(s * seg, seg), lanes] = jnp.concatenate(
+            [out[:, h * seg : (h + 1) * seg].T for h in range(group)], axis=1
+        ).astype(BF)
+        lse_ref[s, g] = top_ + jnp.log(total)
+
+    for s in range(slots):
+        @pl.loop(0, heads // group)
+        def over_groups(g):
+            attend(s, g)
+
+        stream.event()
+        stream.event()
+
+    locals_[1].wait()
+    while stream.next <= len(stream.order):
+        stream.event()
+    for copy in up_far:
+        begin(copy)
+    begin(cot_x)
+    begin(cot_y)
+    begin(cot_share[0])
+    stream.settle(mixer_w)
+    wm_copy = pltpu.make_async_copy(wm_v, wm_out, local_sem.at[6])
+    wm_copy.start()
+
+    @tiles(width // 512, 512)
+    def mix(cols, _):
+        residual_ref[:, cols] = (
+            tokens_v[:, cols].astype(F32) + dot(mixed_v[...], wm_v[:, cols]) + vec_v[3:4, cols]
+        )
+
+    def second_norm(span):
+        unit, _ = norm_rows(residual_ref[span, :])
+        second_ref[span, :] = (unit * vec_v[4:5, :] + vec_v[5:6, :]).astype(BF)
+
+    for_rows(rows, second_norm)
+
+    for copy in up_far:
+        copy.wait_recv()
+    for target in range(length):
+        @pl.when(target != z)
+        def share():
+            for k in range(2):
+                up_share(k, z, target).start()
+
+    cot_x.wait_recv()
+    cot_y.wait_recv()
+    begin(cot_share[1])
+    begin(cot_share[2])
+    begin(cot_dx)
+    begin(cot_dy)
+    cot_dx.wait_recv()
+    cot_dy.wait_recv()
+    begin(cot_share[3])
+    for copy in cot_share + up_near:
+        copy.wait_recv()
+    for copy in up_local:
+        copy.wait()
+    for target in range(length):
+        @pl.when(target != z)
+        def shared():
+            for k in range(2):
+                up_share(k, z, target).wait_send()
+                up_share(k, target, z).wait_recv()
+    for copy in sent + stream.sent:
+        copy.wait_send()
+    for copy in (cot_local, wq_copy, wm_copy):
+        copy.wait()
+
+
+def front(lengths, tokens, smalls, kvw, qw, mw, up, cot, slots, length, with_length, aligned, hidden):
+    rows, width = tokens.shape
+    seg = rows // slots
+    both = kvw.shape[1]
+    groups = width // (both // 2) // 4
+    hbm = pl.BlockSpec(memory_space=pltpu.HBM)
+    vmem = pl.BlockSpec(memory_space=pltpu.VMEM)
+    sems = pltpu.SemaphoreType.DMA
+    return pl.pallas_call(
+        functools.partial(
+            front_kernel, length=length, slots=slots, with_length=with_length, aligned=aligned
+        ),
+        in_specs=[pl.BlockSpec(memory_space=pltpu.SMEM), vmem, hbm, hbm, hbm, hbm, hbm, hbm],
+        out_specs=[vmem] * 8 + [hbm, hbm, vmem, hbm, hbm],
+        out_shape=[
+            jax.ShapeDtypeStruct((rows, width), BF),
+            jax.ShapeDtypeStruct((rows, width), F32),
+            jax.ShapeDtypeStruct((rows, width), BF),
+            jax.ShapeDtypeStruct((rows, width), BF),
+            jax.ShapeDtypeStruct((slots, length, 2 * seg, both), BF),
+            jax.ShapeDtypeStruct((rows, width), BF),
+            jax.ShapeDtypeStruct((slots, groups, 1, 4 * seg), F32),
+            jax.ShapeDtypeStruct((16, width), F32),
+            jax.ShapeDtypeStruct((width, width), BF),
+            jax.ShapeDtypeStruct((width, width), BF),
+            jax.ShapeDtypeStruct((width, both), BF),
+            jax.ShapeDtypeStruct((width, hidden), BF),
+            jax.ShapeDtypeStruct((4, 2 * rows, width), BF),
+        ],
+        scratch_shapes=[
+            pltpu.VMEM((width, width), BF),
+            pltpu.VMEM((width, width), BF),
+            pltpu.VMEM((4, 16, width // 4), BF),
+            sems((7,)),
+            sems((34,)),
+            sems((34,)),
+            sems((6,)),
+            sems((6,)),
+            sems((2 * length,)),
+            sems((2 * length,)),
+            sems((4 * length,)),
+            sems((4 * length,)),
+            sems((2, length)),
+            sems((2, length)),
+            sems((8,)),
+            sems((8,)),
+        ],
+        compiler_params=pltpu.CompilerParams(
+            collective_id=2, has_side_effects=True, vmem_limit_bytes=60 << 20
+        ),
+        cost_estimate=pl.CostEstimate(
+            flops=6 * rows * width * width, bytes_accessed=40 << 20, transcendentals=0
+        ),
+    )(lengths, tokens, smalls, kvw, qw, mw, up, cot)
+
+
 def body(
     tokens,
     lengths,
@@ -600,73 +1090,69 @@
     scal = jnp.concatenate([jnp.stack([z, x]).astype(jnp.int32), lengths])
 
     quarter = width // 4
+    v_part = value_bias.shape[0]
+    v_place = lax.dynamic_update_slice(jnp.zeros((quarter,), BF), value_bias, (place * v_part,))
     small = jnp.stack(
-        [
-            norm_gain,
-            norm_shift,
-            query_bias,
-            mixer_bias,
-            ffnorm_gain,
-            ffnorm_shift,
-            down_bias,
-            jnp.pad(value_bias, (0, quarter - value_bias.shape[0])),
-        ]
-    )
-    pair = jnp.stack([small, swap(small, "c")])
-    pair = jnp.where(c == 0, pair, pair[::-1])
-    quad = jnp.stack([pair, swap(pair, "y")])
-    quad = jnp.where(y == 0, quad, quad[::-1]).reshape(4, 8, quarter)
-    smalls = quad.transpose(1, 0, 2).reshape(8, width).astype(F32)
-    gain, shift, q_bias, m_bias, ffgain, ffshift, d_bias = [smalls[i][None, :] for i in range(7)]
-    v_bias = quad[:, 7, : value_bias.shape[0]].reshape(1, head_dim).astype(F32)
-
-    full_keyval = gather_rows(keyval_weight, x, place)
-    full_query = gather_rows(query_weight, x, place)
-    full_mixer = gather_rows(mixer_weight, x, place)
+        [norm_gain, norm_shift, query_bias, mixer_bias, ffnorm_gain, ffnorm_shift, down_bias, v_place]
+    )
+    small = jnp.concatenate([small, jnp.zeros_like(small)], axis=0)
 
     down_mine = pick(down_weight.reshape(length, 2, hidden_block, width), x, 1).reshape(
         hidden_mine, width
     )
     up_bias_mine = pick(up_bias.reshape(length, 2, hidden_block), x, 1).reshape(1, hidden_mine)
-    up_parts = pick(up_weight.reshape(quarter, 4, length, 2, hidden_block), x, 3).reshape(
-        quarter, 4, hidden_mine
-    )
-    up_mine = jnp.zeros((width, hidden_mine), BF)
-    for flip in range(4):
-        piece = pick(up_parts, place ^ flip, 1)
-        if flip:
-            piece = lax.ppermute(piece, ("y", "c"), [(i, i ^ flip) for i in range(4)])
-        up_mine = lax.dynamic_update_slice_in_dim(up_mine, piece, (place ^ flip) * quarter, 0)
-
-    inputs = tokens.reshape(rows, width).astype(F32)
-    unit1, rstd1 = norm_stats(inputs)
-    first = (unit1 * gain + shift).astype(BF)
-    kv_bias = jnp.concatenate([jnp.zeros_like(v_bias), v_bias], axis=1)
-    keyvals = (dot(first, full_keyval) + kv_bias).astype(BF).reshape(slots, seg, 2 * head_dim)
-    blocks = []
-    current = keyvals
-    for step in range(length):
-        if step:
-            current = lax.ppermute(current, "z", [(i, i + 1) for i in range(length - 1)])
-        both = jnp.stack([current, swap(current, "x")], axis=1)
-        both = jnp.where(x == 0, both, both[:, ::-1])
-        blocks.append(both.reshape(slots, 2 * seg, 2 * head_dim))
-    kv_all = jnp.stack(blocks, axis=1)
-    q_t = (dot(full_query, first, ((0,), (1,))) + q_bias.reshape(width, 1)).astype(BF)
-    mixed_t, lse = attn_forward(scal, q_t, kv_all, 4, with_length)
-    residual = inputs + dot(mixed_t, full_mixer, ((0,), (0,))) + m_bias
-    unit2, rstd2 = norm_stats(residual)
-    second = (unit2 * ffgain + ffshift).astype(BF)
+    aligned = hidden_block % 128 == 0
+    up_given = up_weight
+    if not aligned:
+        up_given = pick(up_weight.reshape(quarter, 4, length, 2, hidden_block), x, 3)
+        up_given = up_given.reshape(quarter, 4, hidden_mine).transpose(1, 0, 2)
 
     token_pos = (z * 2 + x) * seg + jnp.arange(seg, dtype=jnp.int32)
     valid = (token_pos[None, :] < lengths[:, None]).astype(F32).reshape(rows, 1)
-    d_out = cotangent.reshape(rows, width).astype(F32) * valid
-    d_down = d_out.astype(BF)
-
-    down_all = gather_plane(d_down)
+    d_down = cotangent.reshape(rows, width)
+    if with_length:
+        d_down = (d_down.astype(F32) * valid).astype(BF)
+    d_out = d_down.astype(F32)
+
+    flat = tokens.reshape(rows, width)
+    (
+        second,
+        residual,
+        first,
+        queries,
+        kv_all,
+        mixed,
+        lse,
+        vectors,
+        full_query,
+        full_mixer,
+        full_keyval,
+        up_mine,
+        down_all,
+    ) = front(
+        lengths,
+        flat,
+        small,
+        keyval_weight,
+        query_weight,
+        mixer_weight,
+        up_given,
+        d_down,
+        slots,
+        length,
+        with_length,
+        aligned,
+        hidden_mine,
+    )
+    inputs = flat.astype(F32)
+    gain, ffgain, d_bias = vectors[0:1], vectors[4:5], vectors[6:7]
+    unit1, rstd1 = norm_stats(inputs)
+    unit2, rstd2 = norm_stats(residual)
+    q_t, mixed_t = queries.T, mixed.T
+
     d_second, out_parts, down_part, up_part, ubias_part = ffn(
         second,
-        jnp.concatenate(down_all, axis=0),
+        down_all.reshape(8 * rows, width),
         up_mine,
         up_bias_mine.astype(F32),
         down_mine,
@@ -694,7 +1180,7 @@
     where = (y, c, z, x)
     sizes = (length, width)
     mixer_all = scatter_all(
-        mixed_t.T,
+        mixed,
         d_mix,
         (
             jnp.sum(d_mix.astype(F32), axis=0),

time: 802 us -> 657 us (0.82)
  Pallas kernels: 108 us -> 243 us
  local copies, waits for them, and re-layouts: 195 us -> 84.9 us
  waiting for transfers between devices: 217 us -> 112 us
  starting transfers between devices: 164 us -> 117 us
  matrix products: 37.2 us -> 22 us
    pallas_call x1, Pallas kernels: 5.08 us -> 141 us  [front(): pl.pallas_call(functools.partial(front_kernel, length=length, slots=slots...]
    ppermute x55 -> x26, waiting for transfers between devices: 121 us -> 45.5 us  [swap(): return lax.ppermute(values, axis, [(0, 1), (1, 0)])]
    dynamic_slice x12 -> x7, local copies, waits for them, and re-layouts: 58.3 us -> 14.9 us  [pick(): return lax.dynamic_index_in_dim(values, index, axis, keepdims=False)]
    dynamic_update_slice x22 -> x1, local copies, waits for them, and re-layouts: 28 us -> 0.12 us  [body(): lax.dynamic_update_slice(jnp.zeros((quarter,), BF), value_bias, (place *...]
    ppermute x55 -> x26, starting transfers between devices: 42 us -> 19.5 us  [swap(): return lax.ppermute(values, axis, [(0, 1), (1, 0)])]
    ppermute x6 -> x0, waiting for transfers between devices: 20 us -> none  [the longest x3 20 us: body(): piece = lax.ppermute(piece, ('y', 'c'), [(i, i ^ flip) for i in range(4)])]
    ppermute x15, waiting for transfers between devices: 50.3 us -> 30.8 us  [scatter_line(): lax.ppermute(up.astype(BF), 'z', [(i, i + 1) for i in range(step)])]
    reshape x2, local copies, waits for them, and re-layouts: 21.7 us -> 4.63 us  [scatter_all(): left_parts = left_side.reshape(tokens, 2, 2, width // 4)]
  transfers between devices with their start and end apart: 95 -> 60, of which waited for: 34 -> 22; matrix products, arithmetic and copies ran while one was open for 34% -> 23% of each run, Pallas kernels for 2% -> 1%
where the time goes in v3:
time: 657 us; the launch traced here: 646 us
  Pallas kernels  243 us (37%)
  starting transfers between devices  117 us (18%)
  waiting for transfers between devices  112 us (17%)
  local copies, waits for them, and re-layouts  84.9 us (13%)
  other arithmetic  64.7 us (10%)
  matrix products  22 us (3%)
    pallas_call x1, Pallas kernels, front(): pl.pallas_call(functools.partial(front_kernel, length=length, slots=slots...  141 us
    pallas_call x1, Pallas kernels, ffn(): pl.pallas_call(functools.partial(ffn_kernel, length=length), in_specs=[hb...  94.2 us
    ppermute x15, starting transfers between devices, scatter_line(): lax.ppermute(up.astype(BF), 'z', [(i, i + 1) for i in range(step)])  73.8 us
    ppermute x26, waiting for transfers between devices, swap(): return lax.ppermute(values, axis, [(0, 1), (1, 0)])  45.5 us
    ppermute x15, waiting for transfers between devices, scatter_line(): lax.ppermute(up.astype(BF), 'z', [(i, i + 1) for i in range(step)])  30.8 us
    ppermute x3, waiting for transfers between devices, body(): lax.ppermute(running.astype(BF), 'z', [(i, i - 1) for i in range(1, lengt...  24.4 us
    dot_general x5, matrix products, dot(): lax.dot_general(left_side, right_side, (dims, ((), ())), preferred_elemen...  22 us
    ppermute x26, starting transfers between devices, swap(): return lax.ppermute(values, axis, [(0, 1), (1, 0)])  19.5 us
  transfers between devices with their start and end apart: 60, of which 22 were waited for; matrix products, arithmetic and copies ran while one was open for 23% of the time, Pallas kernels for 1%

profile of v3, /device:TPU:0, one launch (start us, length us, event | category | flops | bytes accessed | tf_op | source)
XLA Modules:
  0.0 646.0 jit_solution(492204019116468234)
XLA Ops:
  6.1 4.7 constant_dynamic-slice_fusion.17
  12.9 141.2 %shard_map.288 = (bf16[256,2048]{1,0:T(8,128)(2,1)}, f32[256,2048]{1,0:T(8,128)}, bf16[256,2048]{1,0:T(8,128)(2,1)}, bf16[256,2048]{1,0:T(8,128)(2,1)}, bf16[2,4...) custom-call(s32[2]{0:T(128)} %lengths_ref.1, ...), custom_call_target="tpu_custom_call" | custom-call | flops 6442450944 | bytes 41943040 | tf_op jit(solution)/shard_map/pallas_call | solution.py:1013
  154.0 94.2 %shard_map.289 = (f32[256,2048]{1,0:T(8,128)}, bf16[4,512,2048]{2,1,0:T(8,128)(2,1)}, bf16[1024,2048]{1,0:T(8,128)(2,1)}, bf16[4,4,128,1024]{3,2,1,0:T(8,128)(2,1)}, f32[1,1024]{1,0:T(1,128)}) custom-call(bf16[256,2048]{1,0:T(8,128)(2,1)} %get-tuple-element.37.second_ref, bf16[2048,2048]{1,0:T(8,128)(2,1)} %bitcast.370, ...), custom_call_target="tpu_custom_call" | custom-call | flops 51539607552 | bytes 41943040 | tf_op jit(solution)/shard_map/pallas_call | solution.py:531
  248.3 3.1 dynamic-slice_bitcast_fusion.1
  251.4 13.8 %collective-permute-start.53 = (bf16[256,2048]{1,0:T(8,128)(2,1)}, bf16[256,2048]{1,0:T(8,128)(2,1)}, u32[]{:S(2)}, u32[]{:S(2)}) collective-permute-start(bf16[256,2048]{1,0:T(8,128)(2,1)} %get-tuple-element.85), channel_id=1, source_target_pairs={{0,2},{1,3},{8,10},{9,11},{16,18},{17,19},{24,26},{25,27}} | collective-permute-start | bytes 3145736 | tf_op jit(solution)/shard_map/ppermute | solution.py:244
  267.8 4.4 slice_bitcast_fusion.3
  272.7 2.0 reshape.280
  275.5 3.2 dynamic-slice_bitcast_fusion.3
  280.2 2.6 reshape.275
  282.9 7.6 %constant_dynamic-slice_fusion.12 = (bf16[256,2,1,512]{3,2,1,0:T(2,128)(2,1)}, bf16[256,2,1,512]{3,2,1,0:T(2,128)(2,1)S(1)}, bf16[256,2,1,512]{3,2,1,0:T(2,128)(2,1)}, bf16[256,2,1,512]{3,2,1,0:T(2,128)(2,1)}) fusion(bf16[256,2,2,512]{3,2,1,0:T(2,128)(2,1)} %reshape.280, s32[]{:T(128)S(6)} %select_n.105, s32[]{:T(128)S(6)} %select_n.106, ...), kind=kLoop, calls=%fused_computation.258 | loop fusion | bytes 4194312 | tf_op jit(solution)/shard_map/jit(dynamic_index_in_dim)/dynamic_slice | solution.py:28
  291.4 3.5 copy.134
  297.2 2.6 multiply_reduce_fusion
  301.6 2.2 copy.161
  303.8 2.0 copy.126
  310.5 10.1 %collective-permute-start.41 = (bf16[4,128,1024]{2,1,0:T(8,128)(2,1)}, bf16[4,128,1024]{2,1,0:T(8,128)(2,1)S(1)}, u32[]{:S(2)}, u32[]{:S(2)}) collective-permute-start(bf16[4,128,1024]{2,1,0:T(8,128)(2,1)} %get-tuple-element.89), channel_id=1, source_target_pairs={{0,2},{1,3},{8,10},{9,11},{16,18},{17,19},{24,26},{25,27}} | collective-permute-start | bytes 3145736 | tf_op jit(solution)/shard_map/ppermute | solution.py:244
  321.9 4.1 convert_add_fusion.12
  327.6 1.9 fusion.28
  329.5 11.2 %collective-permute-done.41 = bf16[4,128,1024]{2,1,0:T(8,128)(2,1)S(1)} collective-permute-done((bf16[4,128,1024]{2,1,0:T(8,128)(2,1)}, bf16[4,128,1024]{2,1,0:T(8,128)(2,1)S(1)}, u32[]{:S(2)}, u32[]{:S(2)}) %collective-permute-start.41) | collective-permute-done | bytes 1048608 | tf_op jit(solution)/shard_map/ppermute | solution.py:244
  342.1 2.6 fusion.33
  344.9 4.5 collective-permute-start.54
  352.4 4.4 collective-permute-done.52
  358.4 4.9 collective-permute-start.42
  367.0 5.9 collective-permute-done.54
  374.5 2.0 copy.106
  376.5 2.1 copy.99
  378.6 4.5 fusion.29
  384.7 5.9 collective-permute-done.42
  390.6 5.8 collective-permute-start.55
  396.4 4.0 fusion.34
  400.4 4.8 convert_reduce_fusion.2
  409.9 6.2 convolution_convert_fusion.dout_ref
  416.1 7.8 %shard_map.290 = (bf16[2048,256]{1,0:T(8,128)(2,1)S(1)}, f32[2,4,256,256]{3,2,1,0:T(8,128)}) custom-call(s32[4]{0:T(128)S(1)} %pad_add_fusion.scal_ref, bf16[2048,256]{1,0:T(8,128)(2,1)S(1)} %bitcast.314, bf16[2,4,256,256]{3,2,1,0:T(8,128)(2,1)S(1)} %copy-done, bf16[2048,256]{1,0:T(8,128)(2,1)S(1)} %bitcast.313, ...), custom_call_target="tpu_custom_call" | custom-call | flops 5368709120 | bytes 9437184 | tf_op jit(solution)/shard_map/pallas_call | solution.py:155
  429.4 3.8 fusion.133
  437.6 5.8 collective-permute-done.12
  448.6 7.5 %collective-permute-start.43 = (bf16[4,128,1024]{2,1,0:T(8,128)(2,1)}, bf16[4,128,1024]{2,1,0:T(8,128)(2,1)}, u32[]{:S(2)}, u32[]{:S(2)}) collective-permute-start(bf16[4,128,1024]{2,1,0:T(8,128)(2,1)} %get-tuple-element.87), channel_id=1, source_target_pairs={{0,2},{2,4},{4,6},{1,3},{3,5},{5,7},{8,10},{10,12},{12,14},{9,11},... | collective-permute-start | bytes 3145736 | tf_op jit(solution)/shard_map/ppermute | solution.py:244
  457.7 3.0 fusion.27
  462.1 2.6 fusion.32
  466.1 18.6 %collective-permute-done.14 = bf16[2,128,256]{2,1,0:T(8,128)(2,1)S(1)} collective-permute-done((bf16[2,128,256]{2,1,0:T(8,128)(2,1)S(1)}, bf16[2,128,256]{2,1,0:T(8,128)(2,1)S(1)}, u32[]{:S(2)}, u32[]{:S(2)}) %collective-permute-start.14) | collective-permute-done | bytes 131104 | tf_op jit(solution)/shard_map/ppermute | solution.py:1202
  485.2 4.3 multiply_reduce_fusion.1
  492.7 3.4 add_convert_fusion
  498.1 3.6 fusion.21
  509.9 3.5 fusion.36
  513.4 4.6 all-to-all-start
  518.0 4.2 fusion.12
  523.9 2.0 collective-permute-start.17
  525.9 4.3 collective-permute-done.30
  534.6 3.8 collective-permute-done.33
  541.7 3.7 fusion.30
  548.0 2.0 reshape.303
  550.0 3.0 copy.159
  553.0 4.0 reshape.297
  557.0 3.9 collective-permute-done.31
  562.1 16.6 %collective-permute-done.34 = bf16[4,64,1152]{2,1,0:T(8,128)(2,1)} collective-permute-done((bf16[4,64,1152]{2,1,0:T(8,128)(2,1)}, bf16[4,64,1152]{2,1,0:T(8,128)(2,1)}, u32[]{:S(2)}, u32[]{:S(2)}) %collective-permute-start.34) | collective-permute-done | bytes 589856 | tf_op jit(solution)/shard_map/ppermute | solution.py:24
  580.0 2.8 fusion.18
  583.6 5.3 collective-permute-done.20
  590.0 3.7 collective-permute-start.35
  594.4 5.8 collective-permute-done.18
  600.3 3.2 collective-permute-done.21
  603.8 4.1 collective-permute-start.22
  610.7 4.9 collective-permute-done.22
  615.8 4.4 collective-permute-start.23
  621.8 4.4 collective-permute-start.37
  628.4 5.4 collective-permute-start.24
  638.6 4.1 collective-permute-done.27
  (303 shorter events, 107.9 us)
Async XLA Ops:
  251.4 74.7 %collective-permute-start.53 = (bf16[256,2048]{1,0:T(8,128)(2,1)}, bf16[256,2048]{1,0:T(8,128)(2,1)}, u32[]{:S(2)}, u32[]{:S(2)}) collective-permute-start(bf16[256,2048]{1,0:T(8,128)(2,1)} %get-tuple-element.85), channel_id=1, source_target_pairs={{0,2},{1,3},{8,10},{9,11},{16,18},{17,19},{24,26},{25,27}} | collective-permute-start | bytes 3145736 | tf_op jit(solution)/shard_map/ppermute | solution.py:244
  266.5 39.3 %collective-permute-start.47 = (bf16[256]{0:T(256)(128)(2,1)S(1)}, bf16[256]{0:T(256)(128)(2,1)S(1)}, u32[]{:S(2)}, u32[]{:S(2)}) collective-permute-start(bf16[256]{0:T(256)(128)(2,1)S(1)} %get-tuple-element.71), channel_id=1, source_target_pairs={{0,2},{1,3},{8,10},{9,11},{16,18},{17,19},{24,26},{25,27}} | collective-permute-start | bytes 1544 | tf_op jit(solution)/shard_map/ppermute | solution.py:244
  272.2 38.2 %collective-permute-start.1 = (bf16[256,2048]{1,0:T(8,128)(2,1)}, bf16[256,2048]{1,0:T(8,128)(2,1)}, u32[]{:S(2)}, u32[]{:S(2)}) collective-permute-start(bf16[256,2048]{1,0:T(8,128)(2,1)} %get-tuple-element.79), channel_id=1, source_target_pairs={{0,8},{8,0},{1,9},{9,1},{2,10},{10,2},{3,11},{11,3},{4,12},{12,4},... | collective-permute-start | bytes 3145736 | tf_op jit(solution)/shard_map/ppermute | solution.py:24
  272.2 48.3 %collective-permute-start.2 = (bf16[256,2048]{1,0:T(8,128)(2,1)}, bf16[256,2048]{1,0:T(8,128)(2,1)}, u32[]{:S(2)}, u32[]{:S(2)}) collective-permute-start(bf16[256,2048]{1,0:T(8,128)(2,1)} %get-tuple-element.78), channel_id=1, source_target_pairs={{0,8},{8,0},{1,9},{9,1},{2,10},{10,2},{3,11},{11,3},{4,12},{12,4},... | collective-permute-start | bytes 3145736 | tf_op jit(solution)/shard_map/ppermute | solution.py:24
  272.7 47.9 %collective-permute-start.5 = (bf16[256,2048]{1,0:T(8,128)(2,1)}, bf16[256,2048]{1,0:T(8,128)(2,1)}, u32[]{:S(2)}, u32[]{:S(2)}) collective-permute-start(bf16[256,2048]{1,0:T(8,128)(2,1)} %get-tuple-element.77), channel_id=1, source_target_pairs={{0,8},{8,0},{1,9},{9,1},{2,10},{10,2},{3,11},{11,3},{4,12},{12,4},... | collective-permute-start | bytes 3145736 | tf_op jit(solution)/shard_map/ppermute | solution.py:24
  305.8 0.7 collective-permute-start.50
  306.4 2.6 collective-permute-start.48
  309.0 0.7 collective-permute-start.51
  309.7 55.8 %collective-permute-start.56 = (bf16[256,2048]{1,0:T(8,128)(2,1)}, bf16[256,2048]{1,0:T(8,128)(2,1)S(1)}, u32[]{:S(2)}, u32[]{:S(2)}) collective-permute-start(bf16[256,2048]{1,0:T(8,128)(2,1)} %get-tuple-element.86), channel_id=1, source_target_pairs={{6,4},{7,5},{14,12},{15,13},{22,20},{23,21},{30,28},{31,29}} | collective-permute-start | bytes 3145736 | tf_op jit(solution)/shard_map/ppermute | solution.py:245
  310.5 30.2 %collective-permute-start.41 = (bf16[4,128,1024]{2,1,0:T(8,128)(2,1)}, bf16[4,128,1024]{2,1,0:T(8,128)(2,1)S(1)}, u32[]{:S(2)}, u32[]{:S(2)}) collective-permute-start(bf16[4,128,1024]{2,1,0:T(8,128)(2,1)} %get-tuple-element.89), channel_id=1, source_target_pairs={{0,2},{1,3},{8,10},{9,11},{16,18},{17,19},{24,26},{25,27}} | collective-permute-start | bytes 3145736 | tf_op jit(solution)/shard_map/ppermute | solution.py:244
  320.6 37.8 %collective-permute-start.28 = (bf16[256,2,512]{2,0,1:T(8,128)(2,1)}, bf16[256,2,512]{2,0,1:T(8,128)(2,1)S(1)}, u32[]{:S(2)}, u32[]{:S(2)}) collective-permute-start(bf16[256,2,512]{2,0,1:T(8,128)(2,1)} %bitcast.345), channel_id=1, source_target_pairs={{0,8},{8,0},{1,9},{9,1},{2,10},{10,2},{3,11},{11,3},{4,12},{12,4},... | collective-permute-start | bytes 1572872 | tf_op jit(solution)/shard_map/ppermute | solution.py:24
  320.7 28.9 %collective-permute-start.49 = (bf16[256]{0:T(256)(128)(2,1)S(1)}, bf16[256]{0:T(256)(128)(2,1)S(1)}, u32[]{:S(2)}, u32[]{:S(2)}) collective-permute-start(bf16[256]{0:T(256)(128)(2,1)S(1)} %add_convert_fusion.3), channel_id=1, source_target_pairs={{0,2},{2,4},{4,6},{1,3},{3,5},{5,7},{8,10},{10,12},{12,14},{9,11},... | collective-permute-start | bytes 1544 | tf_op jit(solution)/shard_map/ppermute | solution.py:244
  326.1 18.8 %collective-permute-start.3 = (bf16[128,2048]{1,0:T(8,128)(2,1)S(1)}, bf16[128,2048]{1,0:T(8,128)(2,1)S(1)}, u32[]{:S(2)}, u32[]{:S(2)}) collective-permute-start(bf16[128,2048]{1,0:T(8,128)(2,1)S(1)} %get-tuple-element.112), channel_id=1, source_target_pairs={{0,16},{16,0},{1,17},{17,1},{2,18},{18,2},{3,19},{19,3},{4,20},{20... | collective-permute-start | bytes 1572872 | tf_op jit(solution)/shard_map/ppermute | solution.py:24
  340.7 10.2 %collective-permute-start.6 = (bf16[128,2048]{1,0:T(8,128)(2,1)S(1)}, bf16[128,2048]{1,0:T(8,128)(2,1)S(1)}, u32[]{:S(2)}, u32[]{:S(2)}) collective-permute-start(bf16[128,2048]{1,0:T(8,128)(2,1)S(1)} %get-tuple-element.113), channel_id=1, source_target_pairs={{0,1},{1,0},{2,3},{3,2},{4,5},{5,4},{6,7},{7,6},{8,9},{9,8},{10,11... | collective-permute-start | bytes 1572872 | tf_op jit(solution)/shard_map/ppermute | solution.py:24
  344.9 28.0 %collective-permute-start.54 = (bf16[256,2048]{1,0:T(8,128)(2,1)S(1)}, bf16[256,2048]{1,0:T(8,128)(2,1)S(1)}, u32[]{:S(2)}, u32[]{:S(2)}) collective-permute-start(bf16[256,2048]{1,0:T(8,128)(2,1)S(1)} %fusion.28), channel_id=1, source_target_pairs={{0,2},{2,4},{1,3},{3,5},{8,10},{10,12},{9,11},{11,13},{16,18},{18,... | collective-permute-start | bytes 3145736 | tf_op jit(solution)/shard_map/ppermute | solution.py:244
  349.5 15.9 %collective-permute-start.15 = (bf16[256,2,512]{2,0,1:T(8,128)(2,1)S(1)}, bf16[256,2,512]{2,0,1:T(8,128)(2,1)S(1)}, u32[]{:S(2)}, u32[]{:S(2)}) collective-permute-start(bf16[256,2,512]{2,0,1:T(8,128)(2,1)S(1)} %bitcast.346), channel_id=1, source_target_pairs={{0,8},{8,0},{1,9},{9,1},{2,10},{10,2},{3,11},{11,3},{4,12},{12,4},... | collective-permute-start | bytes 1572872 | tf_op jit(solution)/shard_map/ppermute | solution.py:24
  350.9 5.8 collective-permute-start.52
  356.7 26.4 %collective-permute-start.44 = (bf16[4,128,1024]{2,1,0:T(8,128)(2,1)S(1)}, bf16[4,128,1024]{2,1,0:T(8,128)(2,1)}, u32[]{:S(2)}, u32[]{:S(2)}) collective-permute-start(bf16[4,128,1024]{2,1,0:T(8,128)(2,1)S(1)} %copy-done.31), channel_id=1, source_target_pairs={{6,4},{7,5},{14,12},{15,13},{22,20},{23,21},{30,28},{31,29}} | collective-permute-start | bytes 3145736 | tf_op jit(solution)/shard_map/ppermute | solution.py:245
  358.4 32.2 %collective-permute-start.42 = (bf16[4,128,1024]{2,1,0:T(8,128)(2,1)}, bf16[4,128,1024]{2,1,0:T(8,128)(2,1)}, u32[]{:S(2)}, u32[]{:S(2)}) collective-permute-start(bf16[4,128,1024]{2,1,0:T(8,128)(2,1)} %fusion.33), channel_id=1, source_target_pairs={{0,2},{2,4},{1,3},{3,5},{8,10},{10,12},{9,11},{11,13},{16,18},{18,... | collective-permute-start | bytes 3145736 | tf_op jit(solution)/shard_map/ppermute | solution.py:244
  365.4 34.9 %collective-permute-start = (bf16[256,2048]{1,0:T(8,128)(2,1)}, bf16[256,2048]{1,0:T(8,128)(2,1)}, u32[]{:S(2)}, u32[]{:S(2)}) collective-permute-start(bf16[256,2048]{1,0:T(8,128)(2,1)} %get-tuple-element.76), channel_id=1, source_target_pairs={{0,8},{8,0},{1,9},{9,1},{2,10},{10,2},{3,11},{11,3},{4,12},{12,4},... | collective-permute-start | bytes 3145736 | tf_op jit(solution)/shard_map/ppermute | solution.py:24
  365.5 34.8 %collective-permute-start.4 = (bf16[256,2048]{1,0:T(8,128)(2,1)}, bf16[256,2048]{1,0:T(8,128)(2,1)}, u32[]{:S(2)}, u32[]{:S(2)}) collective-permute-start(bf16[256,2048]{1,0:T(8,128)(2,1)} %pad_maximum_fusion.1), channel_id=1, source_target_pairs={{0,1},{1,0},{2,3},{3,2},{4,5},{5,4},{6,7},{7,6},{8,9},{9,8},{10,11... | collective-permute-start | bytes 3145736 | tf_op jit(solution)/shard_map/ppermute | solution.py:24
  372.9 27.5 %collective-permute-start.7 = (bf16[256,2048]{1,0:T(8,128)(2,1)}, bf16[256,2048]{1,0:T(8,128)(2,1)}, u32[]{:S(2)}, u32[]{:S(2)}) collective-permute-start(bf16[256,2048]{1,0:T(8,128)(2,1)} %pad_maximum_fusion.2), channel_id=1, source_target_pairs={{0,16},{16,0},{1,17},{17,1},{2,18},{18,2},{3,19},{19,3},{4,20},{20... | collective-permute-start | bytes 3145736 | tf_op jit(solution)/shard_map/ppermute | solution.py:24
  383.1 73.2 %collective-permute-start.57 = (bf16[256,2048]{1,0:T(8,128)(2,1)}, bf16[256,2048]{1,0:T(8,128)(2,1)}, u32[]{:S(2)}, u32[]{:S(2)}) collective-permute-start(bf16[256,2048]{1,0:T(8,128)(2,1)} %get-tuple-element.84), channel_id=1, source_target_pairs={{4,2},{6,4},{5,3},{7,5},{12,10},{14,12},{13,11},{15,13},{20,18},{2... | collective-permute-start | bytes 3145736 | tf_op jit(solution)/shard_map/ppermute | solution.py:245
  390.6 151.1 %collective-permute-start.55 = (bf16[256,2048]{1,0:T(8,128)(2,1)}, bf16[256,2048]{1,0:T(8,128)(2,1)}, u32[]{:S(2)}, u32[]{:S(2)}) collective-permute-start(bf16[256,2048]{1,0:T(8,128)(2,1)} %get-tuple-element.83), channel_id=1, source_target_pairs={{0,2},{2,4},{4,6},{1,3},{3,5},{5,7},{8,10},{10,12},{12,14},{9,11},... | collective-permute-start | bytes 3145736 | tf_op jit(solution)/shard_map/ppermute | solution.py:244
  409.9 36.0 %collective-permute-start.32 = (bf16[2,512,128]{2,1,0:T(8,128)(2,1)}, bf16[2,512,128]{2,1,0:T(8,128)(2,1)S(1)}, u32[]{:S(2)}, u32[]{:S(2)}) collective-permute-start(bf16[2,512,128]{2,1,0:T(8,128)(2,1)} %bitcast.300), channel_id=1, source_target_pairs={{0,8},{8,0},{1,9},{9,1},{2,10},{10,2},{3,11},{11,3},{4,12},{12,4},... | collective-permute-start | bytes 786440 | tf_op jit(solution)/shard_map/ppermute | solution.py:24
  425.7 7.9 %collective-permute-start.11 = (bf16[2,128,256]{2,1,0:T(8,128)(2,1)S(1)}, bf16[2,128,256]{2,1,0:T(8,128)(2,1)S(1)}, u32[]{:S(2)}, u32[]{:S(2)}) collective-permute-start(bf16[2,128,256]{2,1,0:T(8,128)(2,1)S(1)} %fusion.119), channel_id=1, source_target_pairs={{0,1},{1,0},{2,3},{3,2},{4,5},{5,4},{6,7},{7,6},{8,9},{9,8},{10,11... | collective-permute-start | bytes 393224 | tf_op jit(solution)/shard_map/ppermute | solution.py:24
  427.0 9.7 %collective-permute-start.10 = (bf16[2,128,256]{2,1,0:T(8,128)(2,1)}, bf16[2,128,256]{2,1,0:T(8,128)(2,1)}, u32[]{:S(2)}, u32[]{:S(2)}) collective-permute-start(bf16[2,128,256]{2,1,0:T(8,128)(2,1)} %fusion.122), channel_id=1, source_target_pairs={{0,1},{1,0},{2,3},{3,2},{4,5},{5,4},{6,7},{7,6},{8,9},{9,8},{10,11... | collective-permute-start | bytes 393224 | tf_op jit(solution)/shard_map/ppermute | solution.py:24
  433.7 9.8 %collective-permute-start.12 = (bf16[2,128,256]{2,1,0:T(8,128)(2,1)S(1)}, bf16[2,128,256]{2,1,0:T(8,128)(2,1)}, u32[]{:S(2)}, u32[]{:S(2)}) collective-permute-start(bf16[2,128,256]{2,1,0:T(8,128)(2,1)S(1)} %fusion.118), channel_id=1, source_target_pairs={{2,0},{4,2},{6,4},{3,1},{5,3},{7,5},{10,8},{12,10},{14,12},{11,9},... | collective-permute-start | bytes 393224 | tf_op jit(solution)/shard_map/ppermute | solution.py:1202
  436.7 24.0 %collective-permute-start.45 = (bf16[4,128,1024]{2,1,0:T(8,128)(2,1)}, bf16[4,128,1024]{2,1,0:T(8,128)(2,1)S(1)}, u32[]{:S(2)}, u32[]{:S(2)}) collective-permute-start(bf16[4,128,1024]{2,1,0:T(8,128)(2,1)} %get-tuple-element.88), channel_id=1, source_target_pairs={{4,2},{6,4},{5,3},{7,5},{12,10},{14,12},{13,11},{15,13},{20,18},{2... | collective-permute-start | bytes 3145736 | tf_op jit(solution)/shard_map/ppermute | solution.py:245
  443.4 5.2 collective-permute-start.9
  446.0 10.2 %collective-permute-start.13 = (bf16[2,128,256]{2,1,0:T(8,128)(2,1)S(1)}, bf16[2,128,256]{2,1,0:T(8,128)(2,1)S(1)}, u32[]{:S(2)}, u32[]{:S(2)}) collective-permute-start(bf16[2,128,256]{2,1,0:T(8,128)(2,1)S(1)} %fusion.113), channel_id=1, source_target_pairs={{2,0},{4,2},{6,4},{3,1},{5,3},{7,5},{10,8},{12,10},{14,12},{11,9},... | collective-permute-start | bytes 393224 | tf_op jit(solution)/shard_map/ppermute | solution.py:1202
  448.6 58.4 %collective-permute-start.43 = (bf16[4,128,1024]{2,1,0:T(8,128)(2,1)}, bf16[4,128,1024]{2,1,0:T(8,128)(2,1)}, u32[]{:S(2)}, u32[]{:S(2)}) collective-permute-start(bf16[4,128,1024]{2,1,0:T(8,128)(2,1)} %get-tuple-element.87), channel_id=1, source_target_pairs={{0,2},{2,4},{4,6},{1,3},{3,5},{5,7},{8,10},{10,12},{12,14},{9,11},... | collective-permute-start | bytes 3145736 | tf_op jit(solution)/shard_map/ppermute | solution.py:244
  456.1 41.4 %collective-permute-start.29 = (bf16[256,2048]{1,0:T(8,128)(2,1)}, bf16[256,2048]{1,0:T(8,128)(2,1)}, u32[]{:S(2)}, u32[]{:S(2)}) collective-permute-start(bf16[256,2048]{1,0:T(8,128)(2,1)} %get-tuple-element.74), channel_id=1, source_target_pairs={{0,8},{8,0},{1,9},{9,1},{2,10},{10,2},{3,11},{11,3},{4,12},{12,4},... | collective-permute-start | bytes 3145736 | tf_op jit(solution)/shard_map/ppermute | solution.py:24
  456.3 8.5 %collective-permute-start.8 = (bf16[2,128,256]{2,1,0:T(8,128)(2,1)S(1)}, bf16[2,128,256]{2,1,0:T(8,128)(2,1)S(1)}, u32[]{:S(2)}, u32[]{:S(2)}) collective-permute-start(bf16[2,128,256]{2,1,0:T(8,128)(2,1)S(1)} %copy-done.41), channel_id=1, source_target_pairs={{0,1},{1,0},{2,3},{3,2},{4,5},{5,4},{6,7},{7,6},{8,9},{9,8},{10,11... | collective-permute-start | bytes 393224 | tf_op jit(solution)/shard_map/ppermute | solution.py:24
  460.7 24.0 %copy-start.27 = (f32[2,1,2,128,256]{4,3,2,1,0:T(8,128)S(1)}, f32[2,1,2,128,256]{4,3,2,1,0:T(8,128)}, u32[]{:S(2)}) copy-start(f32[2,1,2,128,256]{4,3,2,1,0:T(8,128)} %copy-done.26) | copy-start | bytes 1572868
  460.7 24.4 %copy-start.12 = (bf16[2,128,2048]{2,1,0:T(8,128)(2,1)S(1)}, bf16[2,128,2048]{2,1,0:T(8,128)(2,1)}, u32[]{:S(2)}) copy-start(bf16[2,128,2048]{2,1,0:T(8,128)(2,1)} %param.17) | copy-start | bytes 3145732
  460.7 24.5 %copy-start.44 = (f32[256]{0:T(256)S(1)}, f32[256]{0:T(256)}, u32[]{:S(2)}) copy-start(f32[256]{0:T(256)} %rsqrt_bitcast_fusion) | copy-start | bytes 3076
  460.7 24.0 %collective-permute-start.14 = (bf16[2,128,256]{2,1,0:T(8,128)(2,1)S(1)}, bf16[2,128,256]{2,1,0:T(8,128)(2,1)S(1)}, u32[]{:S(2)}, u32[]{:S(2)}) collective-permute-start(bf16[2,128,256]{2,1,0:T(8,128)(2,1)S(1)} %fusion.115), channel_id=1, source_target_pairs={{2,0},{4,2},{6,4},{3,1},{5,3},{7,5},{10,8},{12,10},{14,12},{11,9},... | collective-permute-start | bytes 393224 | tf_op jit(solution)/shard_map/ppermute | solution.py:1202
  464.8 44.4 %collective-permute-start.46 = (bf16[4,128,1024]{2,1,0:T(8,128)(2,1)}, bf16[4,128,1024]{2,1,0:T(8,128)(2,1)}, u32[]{:S(2)}, u32[]{:S(2)}) collective-permute-start(bf16[4,128,1024]{2,1,0:T(8,128)(2,1)} %fusion.32), channel_id=1, source_target_pairs={{2,0},{4,2},{6,4},{3,1},{5,3},{7,5},{10,8},{12,10},{14,12},{11,9},... | collective-permute-start | bytes 3145736 | tf_op jit(solution)/shard_map/ppermute | solution.py:245
  492.3 4.9 collective-permute-start.19
  497.2 20.8 %collective-permute-start.16 = (bf16[256,2304]{0,1:T(8,128)(2,1)}, bf16[256,2304]{0,1:T(8,128)(2,1)}, u32[]{:S(2)}, u32[]{:S(2)}) collective-permute-start(bf16[256,2304]{0,1:T(8,128)(2,1)} %pad_maximum_fusion), channel_id=1, source_target_pairs={{0,8},{8,0},{1,9},{9,1},{2,10},{10,2},{3,11},{11,3},{4,12},{12,4},... | collective-permute-start | bytes 3538952 | tf_op jit(solution)/shard_map/ppermute | solution.py:24
  497.5 47.9 %copy-start.19 = (f32[2,512,128]{2,1,0:T(8,128)}, f32[2,512,128]{2,1,0:T(8,128)S(1)}, u32[]{:S(2)}) copy-start(f32[2,512,128]{2,1,0:T(8,128)S(1)} %bitcast_add_fusion.5) | copy-start | bytes 1572868
  503.9 26.3 %collective-permute-start.30 = (bf16[4,2,64,1024]{3,2,0,1:T(8,128)(2,1)}, bf16[4,2,64,1024]{3,2,0,1:T(8,128)(2,1)}, u32[]{:S(2)}, u32[]{:S(2)}) collective-permute-start(bf16[4,2,64,1024]{3,2,0,1:T(8,128)(2,1)} %fusion.46), channel_id=1, source_target_pairs={{0,16},{16,0},{1,17},{17,1},{2,18},{18,2},{3,19},{19,3},{4,20},{20... | collective-permute-start | bytes 3145736 | tf_op jit(solution)/shard_map/ppermute | solution.py:24
  507.0 34.7 %collective-permute-start.58 = (bf16[256,2048]{1,0:T(8,128)(2,1)}, bf16[256,2048]{1,0:T(8,128)(2,1)}, u32[]{:S(2)}, u32[]{:S(2)}) collective-permute-start(bf16[256,2048]{1,0:T(8,128)(2,1)} %fusion.27), channel_id=1, source_target_pairs={{2,0},{4,2},{6,4},{3,1},{5,3},{7,5},{10,8},{12,10},{14,12},{11,9},... | collective-permute-start | bytes 3145736 | tf_op jit(solution)/shard_map/ppermute | solution.py:245
  509.2 29.2 %collective-permute-start.33 = (bf16[2,4,64,1152]{3,2,1,0:T(8,128)(2,1)}, bf16[2,4,64,1152]{3,2,1,0:T(8,128)(2,1)}, u32[]{:S(2)}, u32[]{:S(2)}) collective-permute-start(bf16[2,4,64,1152]{3,2,1,0:T(8,128)(2,1)} %fusion.45), channel_id=1, source_target_pairs={{0,1},{1,0},{2,3},{3,2},{4,5},{5,4},{6,7},{7,6},{8,9},{9,8},{10,11... | collective-permute-start | bytes 3538952 | tf_op jit(solution)/shard_map/ppermute | solution.py:24
  513.4 34.6 %all-to-all-start = ((bf16[8,64,1024]{2,1,0:T(8,128)(2,1)}), bf16[8,64,1024]{2,1,0:T(8,128)(2,1)}, u32[]{:S(2)}, u32[]{:S(2)}) async-start(bf16[8,64,1024]{2,1,0:T(8,128)(2,1)} %bitcast.334), calls=%async_computation | async-start | bytes 2097152 | tf_op jit(solution)/shard_map/all_to_all | solution.py:1167
  523.9 56.1 %collective-permute-start.17 = (bf16[4,2,64,1152]{3,2,0,1:T(8,128)(2,1)}, bf16[4,2,64,1152]{3,2,0,1:T(8,128)(2,1)}, u32[]{:S(2)}, u32[]{:S(2)}) collective-permute-start(bf16[4,2,64,1152]{3,2,0,1:T(8,128)(2,1)} %fusion.44), channel_id=1, source_target_pairs={{0,16},{16,0},{1,17},{17,1},{2,18},{18,2},{3,19},{19,3},{4,20},{20... | collective-permute-start | bytes 3538952 | tf_op jit(solution)/shard_map/ppermute | solution.py:24
  532.8 28.1 %collective-permute-start.31 = (bf16[4,64,1024]{2,1,0:T(8,128)(2,1)}, bf16[4,64,1024]{2,1,0:T(8,128)(2,1)}, u32[]{:S(2)}, u32[]{:S(2)}) collective-permute-start(bf16[4,64,1024]{2,1,0:T(8,128)(2,1)} %fusion.106), channel_id=1, source_target_pairs={{0,1},{1,0},{2,3},{3,2},{4,5},{5,4},{6,7},{7,6},{8,9},{9,8},{10,11... | collective-permute-start | bytes 1572872 | tf_op jit(solution)/shard_map/ppermute | solution.py:24
  541.0 37.6 %collective-permute-start.34 = (bf16[4,64,1152]{2,1,0:T(8,128)(2,1)}, bf16[4,64,1152]{2,1,0:T(8,128)(2,1)}, u32[]{:S(2)}, u32[]{:S(2)}) collective-permute-start(bf16[4,64,1152]{2,1,0:T(8,128)(2,1)} %fusion.81), channel_id=1, source_target_pairs={{0,16},{16,0},{1,17},{17,1},{2,18},{18,2},{3,19},{19,3},{4,20},{20... | collective-permute-start | bytes 1769480 | tf_op jit(solution)/shard_map/ppermute | solution.py:24
  546.7 42.2 %collective-permute-start.20 = (bf16[2,4,64,1280]{3,2,1,0:T(8,128)(2,1)}, bf16[2,4,64,1280]{3,2,1,0:T(8,128)(2,1)S(1)}, u32[]{:S(2)}, u32[]{:S(2)}) collective-permute-start(bf16[2,4,64,1280]{3,2,1,0:T(8,128)(2,1)} %fusion.43), channel_id=1, source_target_pairs={{0,1},{1,0},{2,3},{3,2},{4,5},{5,4},{6,7},{7,6},{8,9},{9,8},{10,11... | collective-permute-start | bytes 3932168 | tf_op jit(solution)/shard_map/ppermute | solution.py:24
  582.9 17.4 %collective-permute-start.18 = (bf16[4,64,1152]{2,1,0:T(8,128)(2,1)S(1)}, bf16[4,64,1152]{2,1,0:T(8,128)(2,1)S(1)}, u32[]{:S(2)}, u32[]{:S(2)}) collective-permute-start(bf16[4,64,1152]{2,1,0:T(8,128)(2,1)S(1)} %fusion.80), channel_id=1, source_target_pairs={{0,1},{1,0},{2,3},{3,2},{4,5},{5,4},{6,7},{7,6},{8,9},{9,8},{10,11... | collective-permute-start | bytes 1769480 | tf_op jit(solution)/shard_map/ppermute | solution.py:24
  589.3 14.3 %collective-permute-start.21 = (bf16[4,64,1280]{2,1,0:T(8,128)(2,1)S(1)}, bf16[4,64,1280]{2,1,0:T(8,128)(2,1)S(1)}, u32[]{:S(2)}, u32[]{:S(2)}) collective-permute-start(bf16[4,64,1280]{2,1,0:T(8,128)(2,1)S(1)} %fusion.55), channel_id=1, source_target_pairs={{0,16},{16,0},{1,17},{17,1},{2,18},{18,2},{3,19},{19,3},{4,20},{20... | collective-permute-start | bytes 1966088 | tf_op jit(solution)/shard_map/ppermute | solution.py:24
  590.0 18.5 %collective-permute-start.35 = (bf16[64,2176]{1,0:T(8,128)(2,1)S(1)}, bf16[64,2176]{1,0:T(8,128)(2,1)S(1)}, u32[]{:S(2)}, u32[]{:S(2)}) collective-permute-start(bf16[64,2176]{1,0:T(8,128)(2,1)S(1)} %get-tuple-element.101), channel_id=1, source_target_pairs={{0,2},{1,3},{8,10},{9,11},{16,18},{17,19},{24,26},{25,27}} | collective-permute-start | bytes 835592 | tf_op jit(solution)/shard_map/ppermute | solution.py:244
  593.8 14.8 %collective-permute-start.38 = (bf16[64,2176]{1,0:T(8,128)(2,1)S(1)}, bf16[64,2176]{1,0:T(8,128)(2,1)S(1)}, u32[]{:S(2)}, u32[]{:S(2)}) collective-permute-start(bf16[64,2176]{1,0:T(8,128)(2,1)S(1)} %get-tuple-element.102), channel_id=1, source_target_pairs={{6,4},{7,5},{14,12},{15,13},{22,20},{23,21},{30,28},{31,29}} | collective-permute-start | bytes 835592 | tf_op jit(solution)/shard_map/ppermute | solution.py:245
  603.8 11.9 %collective-permute-start.22 = (bf16[64,2432]{1,0:T(8,128)(2,1)S(1)}, bf16[64,2432]{1,0:T(8,128)(2,1)S(1)}, u32[]{:S(2)}, u32[]{:S(2)}) collective-permute-start(bf16[64,2432]{1,0:T(8,128)(2,1)S(1)} %get-tuple-element.95), channel_id=1, source_target_pairs={{0,2},{1,3},{8,10},{9,11},{16,18},{17,19},{24,26},{25,27}} | collective-permute-start | bytes 933896 | tf_op jit(solution)/shard_map/ppermute | solution.py:244
  607.9 7.8 %collective-permute-start.25 = (bf16[64,2432]{1,0:T(8,128)(2,1)S(1)}, bf16[64,2432]{1,0:T(8,128)(2,1)S(1)}, u32[]{:S(2)}, u32[]{:S(2)}) collective-permute-start(bf16[64,2432]{1,0:T(8,128)(2,1)S(1)} %get-tuple-element.96), channel_id=1, source_target_pairs={{6,4},{7,5},{14,12},{15,13},{22,20},{23,21},{30,28},{31,29}} | collective-permute-start | bytes 933896 | tf_op jit(solution)/shard_map/ppermute | solution.py:245
  608.7 12.9 %collective-permute-start.36 = (bf16[64,2176]{1,0:T(8,128)(2,1)S(1)}, bf16[64,2176]{1,0:T(8,128)(2,1)S(1)}, u32[]{:S(2)}, u32[]{:S(2)}) collective-permute-start(bf16[64,2176]{1,0:T(8,128)(2,1)S(1)} %get-tuple-element.99), channel_id=1, source_target_pairs={{0,2},{2,4},{1,3},{3,5},{8,10},{10,12},{9,11},{11,13},{16,18},{18,... | collective-permute-start | bytes 835592 | tf_op jit(solution)/shard_map/ppermute | solution.py:244
  610.0 11.6 %collective-permute-start.39 = (bf16[64,2176]{1,0:T(8,128)(2,1)S(1)}, bf16[64,2176]{1,0:T(8,128)(2,1)S(1)}, u32[]{:S(2)}, u32[]{:S(2)}) collective-permute-start(bf16[64,2176]{1,0:T(8,128)(2,1)S(1)} %get-tuple-element.100), channel_id=1, source_target_pairs={{4,2},{6,4},{5,3},{7,5},{12,10},{14,12},{13,11},{15,13},{20,18},{2... | collective-permute-start | bytes 835592 | tf_op jit(solution)/shard_map/ppermute | solution.py:245
  615.8 12.5 %collective-permute-start.23 = (bf16[64,2432]{1,0:T(8,128)(2,1)S(1)}, bf16[64,2432]{1,0:T(8,128)(2,1)S(1)}, u32[]{:S(2)}, u32[]{:S(2)}) collective-permute-start(bf16[64,2432]{1,0:T(8,128)(2,1)S(1)} %get-tuple-element.93), channel_id=1, source_target_pairs={{0,2},{2,4},{1,3},{3,5},{8,10},{10,12},{9,11},{11,13},{16,18},{18,... | collective-permute-start | bytes 933896 | tf_op jit(solution)/shard_map/ppermute | solution.py:244
  620.2 8.1 %collective-permute-start.26 = (bf16[64,2432]{1,0:T(8,128)(2,1)S(1)}, bf16[64,2432]{1,0:T(8,128)(2,1)S(1)}, u32[]{:S(2)}, u32[]{:S(2)}) collective-permute-start(bf16[64,2432]{1,0:T(8,128)(2,1)S(1)} %get-tuple-element.94), channel_id=1, source_target_pairs={{4,2},{6,4},{5,3},{7,5},{12,10},{14,12},{13,11},{15,13},{20,18},{2... | collective-permute-start | bytes 933896 | tf_op jit(solution)/shard_map/ppermute | solution.py:245
  621.8 13.4 %collective-permute-start.37 = (bf16[64,2176]{1,0:T(8,128)(2,1)S(1)}, bf16[64,2176]{1,0:T(8,128)(2,1)S(1)}, u32[]{:S(2)}, u32[]{:S(2)}) collective-permute-start(bf16[64,2176]{1,0:T(8,128)(2,1)S(1)} %get-tuple-element.97), channel_id=1, source_target_pairs={{0,2},{2,4},{4,6},{1,3},{3,5},{5,7},{8,10},{10,12},{12,14},{9,11},... | collective-permute-start | bytes 835592 | tf_op jit(solution)/shard_map/ppermute | solution.py:244
  626.2 10.7 %collective-permute-start.40 = (bf16[64,2176]{1,0:T(8,128)(2,1)S(1)}, bf16[64,2176]{1,0:T(8,128)(2,1)S(1)}, u32[]{:S(2)}, u32[]{:S(2)}) collective-permute-start(bf16[64,2176]{1,0:T(8,128)(2,1)S(1)} %get-tuple-element.98), channel_id=1, source_target_pairs={{2,0},{4,2},{6,4},{3,1},{5,3},{7,5},{10,8},{12,10},{14,12},{11,9},... | collective-permute-start | bytes 835592 | tf_op jit(solution)/shard_map/ppermute | solution.py:245
  628.4 10.2 %collective-permute-start.24 = (bf16[64,2432]{1,0:T(8,128)(2,1)S(1)}, bf16[64,2432]{1,0:T(8,128)(2,1)S(1)}, u32[]{:S(2)}, u32[]{:S(2)}) collective-permute-start(bf16[64,2432]{1,0:T(8,128)(2,1)S(1)} %get-tuple-element.91), channel_id=1, source_target_pairs={{0,2},{2,4},{4,6},{1,3},{3,5},{5,7},{8,10},{10,12},{12,14},{9,11},... | collective-permute-start | bytes 933896 | tf_op jit(solution)/shard_map/ppermute | solution.py:244
  633.8 8.8 %collective-permute-start.27 = (bf16[64,2432]{1,0:T(8,128)(2,1)S(1)}, bf16[64,2432]{1,0:T(8,128)(2,1)S(1)}, u32[]{:S(2)}, u32[]{:S(2)}) collective-permute-start(bf16[64,2432]{1,0:T(8,128)(2,1)S(1)} %get-tuple-element.92), channel_id=1, source_target_pairs={{2,0},{4,2},{6,4},{3,1},{5,3},{7,5},{10,8},{12,10},{14,12},{11,9},... | collective-permute-start | bytes 933896 | tf_op jit(solution)/shard_map/ppermute | solution.py:245
  (47 other events, 403.9 us)
